TPU v7x, 32 devices: a whole 2x2x4 slice. The times are simulated.
32 devices in a mesh: seq: 4 (over z), head: 8 (over y, x, core).
Axes of the slice: x: 2, y: 2, z: 4, core: 2. Of those that a mesh axis runs over, the one named last changes fastest.
Arguments:
- queries: bfloat16 [4096, 1024], P(('seq', 'head')), may hold values from -6 to 6
- keys: bfloat16 [4096, 256], P(('seq', 'head')), may hold values from -6 to 6
- values: bfloat16 [4096, 256], P(('seq', 'head')), may hold values from -6 to 6
- out_grad: bfloat16 [4096, 1024], P(('seq', 'head')), may hold values from -6 to 6
Outputs:
- queries_grad: bfloat16 [4096, 1024], P(('seq', 'head'))
- keys_grad: bfloat16 [4096, 256], P(('seq', 'head'))
- values_grad: bfloat16 [4096, 256], P(('seq', 'head'))
All inputs are finite; a program needn't handle non-finite values.
Results may differ from a plain program's by a relative error of at most 0.0065.
Values may be sent and summed in bfloat16 or wider, within the bound.
No kernel may reach another device: no remote copies, remote signals or barrier semaphores. Data moves between devices by JAX's collectives and lax.ppermute only.
A program may use at most 64 MiB of HBM per device.

v0:
```python
import jax
import jax.numpy as jnp
from jax import lax
from jax.sharding import PartitionSpec as P

HD = 128
BLK = 256


def carried_in(value, axis, join, neutral, backward):
    count, mine = (lax.axis_size(axis), lax.axis_index(axis))
    pieces = lax.all_gather(value, axis)
    if backward:
        pieces = pieces[::-1]
        mine = count - 1 - mine
    running = jnp.full_like(value, 0) + jnp.asarray(neutral, value.dtype)

    def step(position, running):
        longer = join(running, pieces[position])
        return jnp.where(position < mine, longer, running)

    return lax.fori_loop(0, count - 1, step, running)


def add_states(earlier, later):
    return earlier + later


def states_before(states):
    running = jnp.cumsum(states, axis=0)
    return jnp.concatenate([jnp.zeros_like(states[:1]), running[:-1]], axis=0)


def states_after(states):
    running = jnp.cumsum(states[::-1], axis=0)[::-1]
    return jnp.concatenate([running[1:], jnp.zeros_like(states[:1])], axis=0)


def block_grads(pieces):
    (
        query_block,
        key_block,
        value_block,
        cot_block,
        scaled_block,
        scale_block,
        prior_state,
        future_state,
    ) = pieces
    row_count = query_block.shape[0]
    causal = jnp.arange(row_count)[:, None] >= jnp.arange(row_count)[None, :]
    key_scores = jnp.einsum(
        "thd,shd->hts", query_block, key_block, preferred_element_type=jnp.float32
    )
    forward_weights = jnp.where(causal[None], scale_block[None, :, None] * key_scores, 0.0).astype(
        jnp.bfloat16
    )
    value_scores = jnp.einsum(
        "the,she->hts", scaled_block, value_block, preferred_element_type=jnp.float32
    )
    backward_weights = jnp.where(causal[None], value_scores, 0.0).astype(jnp.bfloat16)
    query_grad = jnp.einsum(
        "hts,shd->thd", backward_weights, key_block, preferred_element_type=jnp.float32
    )
    query_grad = query_grad + jnp.einsum(
        "the,hde->thd", scaled_block, prior_state, preferred_element_type=jnp.float32
    )
    key_grad = jnp.einsum(
        "hts,thd->shd", backward_weights, query_block, preferred_element_type=jnp.float32
    )
    key_grad = key_grad + jnp.einsum(
        "she,hed->shd", value_block, future_state, preferred_element_type=jnp.float32
    )
    value_grad = jnp.einsum(
        "hts,the->she", forward_weights, cot_block, preferred_element_type=jnp.float32
    )
    value_grad = value_grad + jnp.einsum(
        "shd,hed->she", key_block, future_state, preferred_element_type=jnp.float32
    )
    return (
        query_grad.astype(jnp.bfloat16),
        key_grad.astype(jnp.bfloat16),
        value_grad.astype(jnp.bfloat16),
    )


def seq_states(pair_total, grad_total):
    prior_group = carried_in(pair_total, "seq", add_states, jnp.zeros_like(pair_total), False)
    future_group = carried_in(grad_total, "seq", add_states, jnp.zeros_like(grad_total), True)
    return (prior_group, future_group)


def local_grads(query_local, key_local, value_local, cot_local, start, combine_states):
    local_tokens = query_local.shape[0]
    local_heads = query_local.shape[1]
    block_count = local_tokens // BLK
    positions = start + jnp.arange(local_tokens, dtype=jnp.int32)
    scale = 1.0 / jnp.sqrt((HD * (positions + 1)).astype(jnp.float32))
    scaled_cot = (scale[:, None, None] * cot_local.astype(jnp.float32)).astype(jnp.bfloat16)
    block_shape = (block_count, BLK, local_heads, HD)
    pair_shape = (block_count, BLK, 1, HD)
    query_blocks = query_local.reshape(block_shape)
    key_single = key_local.reshape(pair_shape)
    value_single = value_local.reshape(pair_shape)
    cot_blocks = cot_local.reshape(block_shape)
    scaled_blocks = scaled_cot.reshape(block_shape)
    pair_states = jnp.einsum(
        "bshd,bshe->bhde", key_single, value_single, preferred_element_type=jnp.float32
    )
    grad_states = jnp.einsum(
        "bthe,bthd->bhed", scaled_blocks, query_blocks, preferred_element_type=jnp.float32
    )
    prior_group, future_group = combine_states(
        jnp.sum(pair_states, axis=0), jnp.sum(grad_states, axis=0)
    )
    prior_states = prior_group[None] + states_before(pair_states)
    prior_states = prior_states.astype(jnp.bfloat16)
    future_states = (future_group[None] + states_after(grad_states)).astype(jnp.bfloat16)
    scale_blocks = scale.reshape(block_count, BLK)
    query_grad, key_grad, value_grad = lax.map(
        block_grads,
        (
            query_blocks,
            key_single,
            value_single,
            cot_blocks,
            scaled_blocks,
            scale_blocks,
            prior_states,
            future_states,
        ),
    )
    local_shape = (local_tokens, local_heads, HD)
    return (
        query_grad.reshape(local_shape),
        key_grad.reshape(local_shape),
        value_grad.reshape(local_shape),
    )


def body(queries, keys, values, out_grad):
    tok_dev = queries.shape[0]
    head_count = queries.shape[1] // HD
    kv_count = keys.shape[1] // HD
    group_size = head_count // kv_count
    seq_index = lax.axis_index("seq")
    query_cube = queries.reshape(tok_dev, head_count, HD)
    key_cube = jnp.repeat(keys.reshape(tok_dev, kv_count, HD), group_size, axis=1)
    value_cube = jnp.repeat(values.reshape(tok_dev, kv_count, HD), group_size, axis=1)
    cot_cube = out_grad.reshape(tok_dev, head_count, HD)
    query_local = lax.all_to_all(query_cube, "head", split_axis=1, concat_axis=0, tiled=True)
    key_local, value_local = (
        lax.all_to_all(key_cube, "head", split_axis=1, concat_axis=0, tiled=True),
        lax.all_to_all(value_cube, "head", split_axis=1, concat_axis=0, tiled=True),
    )
    cot_local = lax.all_to_all(cot_cube, "head", split_axis=1, concat_axis=0, tiled=True)
    local_tokens = query_local.shape[0]
    start = seq_index * local_tokens
    query_grad, key_grad, value_grad = local_grads(
        query_local, key_local, value_local, cot_local, start, seq_states
    )
    query_back, key_back, value_back = (
        lax.all_to_all(query_grad, "head", split_axis=0, concat_axis=1, tiled=True),
        lax.all_to_all(key_grad, "head", split_axis=0, concat_axis=1, tiled=True),
        lax.all_to_all(value_grad, "head", split_axis=0, concat_axis=1, tiled=True),
    )
    queries_grad = query_back.reshape(tok_dev, head_count * HD)
    key_sum = jnp.sum(
        key_back.reshape(tok_dev, kv_count, group_size, HD).astype(jnp.float32), axis=2
    )
    value_sum = jnp.sum(
        value_back.reshape(tok_dev, kv_count, group_size, HD).astype(jnp.float32), axis=2
    )
    keys_grad = key_sum.astype(jnp.bfloat16).reshape(tok_dev, kv_count * HD)
    values_grad = value_sum.astype(jnp.bfloat16).reshape(tok_dev, kv_count * HD)
    return (queries_grad, keys_grad, values_grad)


def solution(mesh):
    return jax.shard_map(
        body,
        mesh=mesh,
        in_specs=(
            P(("seq", "head"), None),
            P(("seq", "head"), None),
            P(("seq", "head"), None),
            P(("seq", "head"), None),
        ),
        out_specs=(P(("seq", "head"), None), P(("seq", "head"), None), P(("seq", "head"), None)),
        check_vma=False,
    )
```

profile of v0, /device:TPU:0, one launch (start us, length us, event | category | flops | bytes accessed | tf_op | source)
XLA Modules:
  0.0 114.6 jit_solution(16904321531153555835)
XLA Ops:
  0.6 1.8 %copy.75 = bf16[128,1024]{0,1:T(8,128)(2,1)} copy(bf16[128,1024]{1,0:T(8,128)(2,1)} %param.13) | data formatting | bytes 524288 | tf_op args[3]
  2.5 5.3 %all-to-all-start.1 = ((bf16[128,8,128]{0,2,1:T(8,128)(2,1)}), bf16[128,8,128]{0,2,1:T(8,128)(2,1)S(1)}, u32[]{:S(2)}, u32[]{:S(2)}) async-start(bf16[128,8,128]{0,2,1:T(8,128)(2,1)} %bitcast.22), calls=%async_computation.1 | async-start | bytes 524288 | tf_op jit(solution)/shard_map/all_to_all | solution.py:156
  7.9 0.8 copy.79
  8.7 6.0 %all-to-all-done.1 = bf16[128,8,128]{0,2,1:T(8,128)(2,1)S(1)} async-done(((bf16[128,8,128]{0,2,1:T(8,128)(2,1)}), bf16[128,8,128]{0,2,1:T(8,128)(2,1)S(1)}, u32[]{:S(2)}, u32[]{:S(2)}) %all-to-all-start.1) | async-done | bytes 262176 | tf_op jit(solution)/shard_map/all_to_all | solution.py:156
  14.7 3.4 %all-to-all-start.3 = ((bf16[128,8,128]{0,2,1:T(8,128)(2,1)}), bf16[128,8,128]{0,2,1:T(8,128)(2,1)S(1)}, u32[]{:S(2)}, u32[]{:S(2)}) async-start(bf16[128,8,128]{0,2,1:T(8,128)(2,1)} %bitcast.40), calls=%async_computation.3 | async-start | bytes 524288 | tf_op jit(solution)/shard_map/all_to_all | solution.py:151
  18.2 0.2 copy.81
  18.4 6.6 %all-to-all-done.3 = bf16[128,8,128]{0,2,1:T(8,128)(2,1)S(1)} async-done(((bf16[128,8,128]{0,2,1:T(8,128)(2,1)}), bf16[128,8,128]{0,2,1:T(8,128)(2,1)S(1)}, u32[]{:S(2)}, u32[]{:S(2)}) %all-to-all-start.3) | async-done | bytes 262176 | tf_op jit(solution)/shard_map/all_to_all | solution.py:151
  25.0 0.7 broadcast_in_dim.29
  25.7 3.4 %all-to-all-start = ((bf16[128,8,128]{2,0,1:T(8,128)(2,1)}), bf16[128,8,128]{2,0,1:T(8,128)(2,1)S(1)}, u32[]{:S(2)}, u32[]{:S(2)}) async-start(bf16[128,8,128]{2,0,1:T(8,128)(2,1)} %bitcast.17), calls=%async_computation | async-start | bytes 524288 | tf_op jit(solution)/shard_map/all_to_all | solution.py:153
  29.2 0.2 copy.80
  29.3 0.4 fusion.65
  29.8 14.2 %all-gather.1 = f32[512,128]{1,0:T(8,128)S(1)} all-gather(f32[128,128]{1,0:T(8,128)S(1)} %get-tuple-element.373), channel_id=3, replica_groups=mesh['seq'=4,'head'=8] {'seq'}, dimensions={0}, use_global_device_ids=true | all-gather | bytes 327680 | tf_op jit(solution)/shard_map/all_gather | solution.py:12
  44.2 0.7 broadcast_in_dim.30
  44.9 4.0 %all-to-all-start.2 = ((bf16[128,8,128]{2,0,1:T(8,128)(2,1)}), bf16[128,8,128]{2,0,1:T(8,128)(2,1)S(1)}, u32[]{:S(2)}, u32[]{:S(2)}) async-start(bf16[128,8,128]{2,0,1:T(8,128)(2,1)} %bitcast.27), calls=%async_computation.2 | async-start | bytes 524288 | tf_op jit(solution)/shard_map/all_to_all | solution.py:154
  49.1 6.7 %all-to-all-done.2 = bf16[128,8,128]{2,0,1:T(8,128)(2,1)S(1)} async-done(((bf16[128,8,128]{2,0,1:T(8,128)(2,1)}), bf16[128,8,128]{2,0,1:T(8,128)(2,1)S(1)}, u32[]{:S(2)}, u32[]{:S(2)}) %all-to-all-start.2) | async-done | bytes 262176 | tf_op jit(solution)/shard_map/all_to_all | solution.py:154
  55.8 0.3 fusion.64
  56.1 13.9 %all-gather = f32[512,128]{1,0:T(8,128)S(1)} all-gather(f32[128,128]{1,0:T(8,128)S(1)} %get-tuple-element.371), channel_id=2, replica_groups=mesh['seq'=4,'head'=8] {'seq'}, dimensions={0}, use_global_device_ids=true | all-gather | bytes 327680 | tf_op jit(solution)/shard_map/all_gather | solution.py:12
  70.1 0.2 fusion.59
  70.3 0.7 copy-done.1
  71.0 0.2 copy.76
  71.2 0.2 fusion.55
  71.5 0.9 slice-done
  72.4 8.0 %while.42 = (s32[]{:T(128)}, bf16[4,256,1,128]{3,1,0,2:T(8,128)(2,1)S(1)}, bf16[4,256,1,128]{3,1,0,2:T(8,128)(2,1)S(1)}, bf16[4,256,1,128]{3,1,0,2:T(8,128)(2,1)...) while((s32[]{:T(128)}, ...), condition=%wide.region_9.10_spmd, body=%wide.region_8.9_spmd.sunk | while | flops 109707264 | bytes 2925201 | solution.py:120
  72.4 0.2 fusion.111
  72.6 0.2 fusion.115
  72.8 0.2 fusion.116
  73.3 0.4 fusion.114
  73.8 0.2 fusion.110
  74.0 0.2 fusion.112
  74.4 0.2 fusion.111
  74.6 0.2 fusion.115
  74.8 0.2 fusion.116
  75.3 0.4 fusion.114
  76.0 0.2 fusion.112
  76.4 0.2 fusion.111
  76.6 0.2 fusion.115
  76.8 0.2 fusion.116
  77.3 0.4 fusion.114
  78.0 0.2 fusion.112
  78.4 0.2 fusion.111
  78.6 0.2 fusion.115
  78.8 0.2 fusion.116
  79.3 0.4 fusion.114
  80.0 0.2 fusion.112
  80.4 0.5 broadcast.62
  80.9 0.8 reduce.6
  81.7 0.8 reshape.234
  82.5 3.4 %all-to-all-start.4 = ((bf16[8,2,8192]{2,1,0:T(2,128)(2,1)}), bf16[8,2,8192]{2,1,0:T(2,128)(2,1)S(1)}, u32[]{:S(2)}, u32[]{:S(2)}) async-start(bf16[8,2,8192]{2,1,0:T(2,128)(2,1)} %reshape.234), calls=%async_computation.4 | async-start | bytes 524288 | tf_op jit(solution)/shard_map/all_to_all | solution.py:163
  85.9 0.8 reduce.7
  86.7 0.8 reshape.236
  87.5 5.3 %all-to-all-done.4 = bf16[8,2,8192]{2,1,0:T(2,128)(2,1)S(1)} async-done(((bf16[8,2,8192]{2,1,0:T(2,128)(2,1)}), bf16[8,2,8192]{2,1,0:T(2,128)(2,1)S(1)}, u32[]{:S(2)}, u32[]{:S(2)}) %all-to-all-start.4) | async-done | bytes 262176 | tf_op jit(solution)/shard_map/all_to_all | solution.py:163
  92.7 3.4 %all-to-all-start.5 = ((bf16[8,2,8192]{2,1,0:T(2,128)(2,1)}), bf16[8,2,8192]{2,1,0:T(2,128)(2,1)S(1)}, u32[]{:S(2)}, u32[]{:S(2)}) async-start(bf16[8,2,8192]{2,1,0:T(2,128)(2,1)} %reshape.236), calls=%async_computation.5 | async-start | bytes 524288 | tf_op jit(solution)/shard_map/all_to_all | solution.py:164
  96.2 0.8 reduce.8
  97.0 0.8 reshape.238
  97.7 5.3 %all-to-all-done.5 = bf16[8,2,8192]{2,1,0:T(2,128)(2,1)S(1)} async-done(((bf16[8,2,8192]{2,1,0:T(2,128)(2,1)}), bf16[8,2,8192]{2,1,0:T(2,128)(2,1)S(1)}, u32[]{:S(2)}, u32[]{:S(2)}) %all-to-all-start.5) | async-done | bytes 262176 | tf_op jit(solution)/shard_map/all_to_all | solution.py:164
  103.0 3.4 %all-to-all-start.6 = ((bf16[8,2,8192]{2,1,0:T(2,128)(2,1)}), bf16[8,2,8192]{2,1,0:T(2,128)(2,1)S(1)}, u32[]{:S(2)}, u32[]{:S(2)}) async-start(bf16[8,2,8192]{2,1,0:T(2,128)(2,1)} %reshape.238), calls=%async_computation.6 | async-start | bytes 524288 | tf_op jit(solution)/shard_map/all_to_all | solution.py:165
  106.4 0.3 reshape.235
  106.8 0.2 copy.93
  107.0 0.9 copy.100
  107.8 0.3 reshape.237
  108.3 0.7 copy.101
  109.1 4.3 %all-to-all-done.6 = bf16[8,2,8192]{2,1,0:T(2,128)(2,1)S(1)} async-done(((bf16[8,2,8192]{2,1,0:T(2,128)(2,1)}), bf16[8,2,8192]{2,1,0:T(2,128)(2,1)S(1)}, u32[]{:S(2)}, u32[]{:S(2)}) %all-to-all-start.6) | async-done | bytes 262176 | tf_op jit(solution)/shard_map/all_to_all | solution.py:165
  113.3 0.3 reshape.239
  113.8 0.7 copy.102
  (71 shorter events, 3.8 us)
Async XLA Ops:
  0.6 7.1 %copy-start = (bf16[128,256]{1,0:T(8,128)(2,1)S(1)}, bf16[128,256]{1,0:T(8,128)(2,1)}, u32[]{:S(2)}) copy-start(bf16[128,256]{1,0:T(8,128)(2,1)} %param.11) | copy-start | bytes 196612
  2.5 5.4 %copy-start.2 = (bf16[128,1024]{1,0:T(8,128)(2,1)S(1)}, bf16[128,1024]{1,0:T(8,128)(2,1)}, u32[]{:S(2)}) copy-start(bf16[128,1024]{1,0:T(8,128)(2,1)} %param.10) | copy-start | bytes 786436
  2.5 12.2 %all-to-all-start.1 = ((bf16[128,8,128]{0,2,1:T(8,128)(2,1)}), bf16[128,8,128]{0,2,1:T(8,128)(2,1)S(1)}, u32[]{:S(2)}, u32[]{:S(2)}) async-start(bf16[128,8,128]{0,2,1:T(8,128)(2,1)} %bitcast.22), calls=%async_computation.1 | async-start | bytes 524288 | tf_op jit(solution)/shard_map/all_to_all | solution.py:156
  7.9 0.8 copy-start.3
  14.7 10.3 %all-to-all-start.3 = ((bf16[128,8,128]{0,2,1:T(8,128)(2,1)}), bf16[128,8,128]{0,2,1:T(8,128)(2,1)S(1)}, u32[]{:S(2)}, u32[]{:S(2)}) async-start(bf16[128,8,128]{0,2,1:T(8,128)(2,1)} %bitcast.40), calls=%async_computation.3 | async-start | bytes 524288 | tf_op jit(solution)/shard_map/all_to_all | solution.py:151
  25.7 18.4 %all-to-all-start = ((bf16[128,8,128]{2,0,1:T(8,128)(2,1)}), bf16[128,8,128]{2,0,1:T(8,128)(2,1)S(1)}, u32[]{:S(2)}, u32[]{:S(2)}) async-start(bf16[128,8,128]{2,0,1:T(8,128)(2,1)} %bitcast.17), calls=%async_computation | async-start | bytes 524288 | tf_op jit(solution)/shard_map/all_to_all | solution.py:153
  44.9 10.9 %all-to-all-start.2 = ((bf16[128,8,128]{2,0,1:T(8,128)(2,1)}), bf16[128,8,128]{2,0,1:T(8,128)(2,1)S(1)}, u32[]{:S(2)}, u32[]{:S(2)}) async-start(bf16[128,8,128]{2,0,1:T(8,128)(2,1)} %bitcast.27), calls=%async_computation.2 | async-start | bytes 524288 | tf_op jit(solution)/shard_map/all_to_all | solution.py:154
  70.3 0.7 copy-start.1
  71.4 0.9 slice-start
  82.5 10.3 %all-to-all-start.4 = ((bf16[8,2,8192]{2,1,0:T(2,128)(2,1)}), bf16[8,2,8192]{2,1,0:T(2,128)(2,1)S(1)}, u32[]{:S(2)}, u32[]{:S(2)}) async-start(bf16[8,2,8192]{2,1,0:T(2,128)(2,1)} %reshape.234), calls=%async_computation.4 | async-start | bytes 524288 | tf_op jit(solution)/shard_map/all_to_all | solution.py:163
  92.7 10.3 %all-to-all-start.5 = ((bf16[8,2,8192]{2,1,0:T(2,128)(2,1)}), bf16[8,2,8192]{2,1,0:T(2,128)(2,1)S(1)}, u32[]{:S(2)}, u32[]{:S(2)}) async-start(bf16[8,2,8192]{2,1,0:T(2,128)(2,1)} %reshape.236), calls=%async_computation.5 | async-start | bytes 524288 | tf_op jit(solution)/shard_map/all_to_all | solution.py:164
  103.0 10.3 %all-to-all-start.6 = ((bf16[8,2,8192]{2,1,0:T(2,128)(2,1)}), bf16[8,2,8192]{2,1,0:T(2,128)(2,1)S(1)}, u32[]{:S(2)}, u32[]{:S(2)}) async-start(bf16[8,2,8192]{2,1,0:T(2,128)(2,1)} %reshape.238), calls=%async_computation.6 | async-start | bytes 524288 | tf_op jit(solution)/shard_map/all_to_all | solution.py:165
where the time goes:
time: 116 us; the launch traced here: 115 us
  waiting for transfers between devices  34.2 us (29%)
  blocking collectives  28.1 us (24%)
  starting transfers between devices  26.3 us (23%)
  local copies, waits for them, and re-layouts  14.5 us (12%)
  matrix products  6.76 us (6%)
  other arithmetic  3.21 us (3%)
    all_gather x2, blocking collectives, carried_in(): pieces = lax.all_gather(value, axis)  28.1 us
    unnamed x22, local copies, waits for them, and re-layouts  8.93 us
    all_to_all x1, waiting for transfers between devices, body(): lax.all_to_all(value_cube, 'head', split_axis=1, concat_axis=0, tiled=True)  6.74 us
    all_to_all x1, waiting for transfers between devices, body(): lax.all_to_all(query_cube, 'head', split_axis=1, concat_axis=0, tiled=True)  6.62 us
    all_to_all x1, waiting for transfers between devices, body(): lax.all_to_all(cot_cube, 'head', split_axis=1, concat_axis=0, tiled=True)  5.98 us
    all_to_all x1, starting transfers between devices, body(): lax.all_to_all(cot_cube, 'head', split_axis=1, concat_axis=0, tiled=True)  5.3 us
    all_to_all x1, waiting for transfers between devices, body(): lax.all_to_all(query_grad, 'head', split_axis=0, concat_axis=1, tiled=True)  5.29 us
    all_to_all x1, waiting for transfers between devices, body(): lax.all_to_all(key_grad, 'head', split_axis=0, concat_axis=1, tiled=True)  5.28 us
  transfers between devices with their start and end apart: 7, of which 6 were waited for; matrix products, arithmetic and copies ran while one was open for 7% of the time, Pallas kernels for 0%

commit v1 on v0

v1 whole, which is shorter than its diff:
```python
import functools

import jax
import jax.numpy as jnp
from jax import lax
from jax.experimental import pallas as pl
from jax.experimental.pallas import tpu as pltpu
from jax.sharding import PartitionSpec as P

HD = 128
SEQ = "seq"
HEAD = "head"
BF16 = jnp.bfloat16
F32 = jnp.float32

NN = (((1,), (0,)), ((), ()))
NT = (((1,), (1,)), ((), ()))
TN = (((0,), (0,)), ((), ()))


def dot(left, right, dims):
    return lax.dot_general(left, right, dims, preferred_element_type=F32)


def columns(ref, index):
    return ref[:, index * HD : (index + 1) * HD]


def row_scale(start, tokens, shape, axis):
    positions = start + lax.broadcasted_iota(jnp.int32, shape, axis)
    return 1.0 / jnp.sqrt((HD * (positions + 1)).astype(F32))


def first_token(tokens):
    device = lax.axis_index(SEQ) * lax.axis_size(HEAD) + lax.axis_index(HEAD)
    return device * tokens


def states_kernel(q_ref, k_ref, v_ref, o_ref, keep_ref, send_ref):
    tokens = q_ref.shape[0]
    kv = k_ref.shape[1] // HD
    group = q_ref.shape[1] // HD // kv
    half = kv // 2
    core = lax.rem(lax.axis_index(HEAD), 2)
    scale = row_scale(first_token(tokens), tokens, (tokens, HD), 0)
    made = []
    for g in range(kv):
        pair = dot(columns(v_ref, g), columns(k_ref, g), TN)
        grad = jnp.zeros((HD, HD), F32)
        for h in range(g * group, (g + 1) * group):
            scaled = (scale * columns(o_ref, h).astype(F32)).astype(BF16)
            grad = grad + dot(scaled, columns(q_ref, h), TN)
        made.append((pair.astype(BF16), grad.astype(BF16)))

    def put(ref, first):
        for g in range(half):
            ref[0, g] = made[first + g][0]
            ref[1, g] = made[first + g][1]

    @pl.when(core == 0)
    def _():
        put(keep_ref, 0)
        put(send_ref, half)

    @pl.when(core == 1)
    def _():
        put(keep_ref, half)
        put(send_ref, 0)


def grads_kernel(q_ref, k_ref, v_ref, o_ref, mine_ref, other_ref, qg_ref, kg_ref, vg_ref, carried):
    tokens = q_ref.shape[0]
    kv = k_ref.shape[1] // HD
    group = q_ref.shape[1] // HD // kv
    half = kv // 2
    core = lax.rem(lax.axis_index(HEAD), 2)
    carried[core] = mine_ref[...]
    carried[1 - core] = other_ref[...]
    start = first_token(tokens)
    scale = row_scale(start, tokens, (tokens, HD), 0)
    scale_row = row_scale(start, tokens, (HD, tokens), 1)
    causal = lax.broadcasted_iota(jnp.int32, (tokens, tokens), 0) >= lax.broadcasted_iota(
        jnp.int32, (tokens, tokens), 1
    )
    causal_t = lax.broadcasted_iota(jnp.int32, (tokens, tokens), 0) <= lax.broadcasted_iota(
        jnp.int32, (tokens, tokens), 1
    )
    for g in range(kv):
        key = columns(k_ref, g)
        value = columns(v_ref, g)
        prior = carried[g // half, 0, g % half]
        future = carried[g // half, 1, g % half]
        key_grad = dot(value, future, NN)
        value_grad = dot(key, future, NT)
        for h in range(g * group, (g + 1) * group):
            query = columns(q_ref, h)
            cot = columns(o_ref, h)
            scaled = (scale * cot.astype(F32)).astype(BF16)
            backward = jnp.where(causal, dot(scaled, value, NT), 0.0).astype(BF16)
            backward_t = jnp.where(causal_t, dot(value, scaled, NT), 0.0).astype(BF16)
            forward_t = jnp.where(causal_t, scale_row * dot(key, query, NT), 0.0).astype(BF16)
            query_grad = dot(backward, key, NN) + dot(scaled, prior, NN)
            qg_ref[:, h * HD : (h + 1) * HD] = query_grad.astype(BF16)
            key_grad = key_grad + dot(backward_t, query, NN)
            value_grad = value_grad + dot(forward_t, cot, NN)
        kg_ref[:, g * HD : (g + 1) * HD] = key_grad.astype(BF16)
        vg_ref[:, g * HD : (g + 1) * HD] = value_grad.astype(BF16)


def digits(size):
    bits = size.bit_length() - 1
    assert 1 << bits == size
    shifts = []
    while bits > 0:
        width = 2 if bits >= 2 else 1
        bits -= width
        shifts.append((bits, width))
    return shifts


def carry_states(keep, send):
    head_count = lax.axis_size(HEAD)
    head_index = lax.axis_index(HEAD)
    core = lax.rem(head_index, 2)
    swap = [(i, i ^ 1) for i in range(head_count)]
    got = lax.ppermute(send, HEAD, swap).astype(F32)
    keep = keep.astype(F32)
    chip = keep + got
    steps = [(SEQ, lax.axis_size(SEQ), lax.axis_index(SEQ), digit) for digit in digits(lax.axis_size(SEQ))]
    steps += [
        (HEAD, head_count, head_index, (shift + 1, width)) for shift, width in digits(head_count // 2)
    ]
    carried = None
    for axis, size, index, (shift, width) in steps:
        received = []
        for flip in range(1, 1 << width):
            mask = flip << shift
            lower = index < (index ^ mask)
            perm = [(i, i ^ mask) for i in range(size)]
            if carried is None:
                message = jnp.where(lower, chip[0], chip[1]).astype(BF16)
                arrived = lax.ppermute(message, axis, perm).astype(F32)
                received.append(
                    jnp.stack([jnp.where(lower, 0.0, arrived), jnp.where(lower, arrived, 0.0)])
                )
            else:
                message = jnp.stack(
                    [
                        carried[0] + jnp.where(lower, chip[0], 0.0),
                        carried[1] + jnp.where(lower, 0.0, chip[1]),
                    ]
                ).astype(BF16)
                received.append(lax.ppermute(message, axis, perm).astype(F32))
        total = functools.reduce(jnp.add, received)
        carried = total if carried is None else carried + total
    first = core == 0
    mine = jnp.stack(
        [carried[0] + jnp.where(first, 0.0, got[0]), carried[1] + jnp.where(first, got[1], 0.0)]
    ).astype(BF16)
    to_other = jnp.stack(
        [carried[0] + jnp.where(first, keep[0], 0.0), carried[1] + jnp.where(first, 0.0, keep[1])]
    ).astype(BF16)
    other = lax.ppermute(to_other, HEAD, swap)
    return mine, other


def body(queries, keys, values, out_grad):
    tokens = queries.shape[0]
    kv = keys.shape[1] // HD
    half = kv // 2
    shape = (2, half, HD, HD)
    vmem = pl.BlockSpec(memory_space=pltpu.VMEM)
    inputs = (queries, keys, values, out_grad)
    keep, send = pl.pallas_call(
        states_kernel,
        out_shape=(jax.ShapeDtypeStruct(shape, BF16),) * 2,
        in_specs=[vmem] * 4,
        out_specs=[vmem] * 2,
        compiler_params=pltpu.CompilerParams(vmem_limit_bytes=32 * 1024 * 1024),
    )(*inputs)
    mine, other = carry_states(keep, send)
    return pl.pallas_call(
        grads_kernel,
        out_shape=tuple(jax.ShapeDtypeStruct(x.shape, BF16) for x in (queries, keys, values)),
        in_specs=[vmem] * 6,
        out_specs=[vmem] * 3,
        scratch_shapes=[pltpu.VMEM((2,) + shape, BF16)],
        compiler_params=pltpu.CompilerParams(vmem_limit_bytes=32 * 1024 * 1024),
    )(*inputs, mine, other)


def solution(mesh):
    spec = P((SEQ, HEAD), None)
    return jax.shard_map(
        body, mesh=mesh, in_specs=(spec,) * 4, out_specs=(spec,) * 3, check_vma=False
    )
```

time: 116 us -> 28.5 us (0.25); the launches traced: 115 us -> 28.2 us
  blocking collectives: 28.1 us -> 0 us
  waiting for transfers between devices: 34.2 us -> 10.9 us
  starting transfers between devices: 26.3 us -> 9.94 us
  local copies, waits for them, and re-layouts: 14.5 us -> 3.6 us
  matrix products: 6.76 us -> 0 us
  other arithmetic: 3.21 us -> 0.3 us
  Pallas kernels: 0 us -> 2.68 us
    all_to_all x7 -> x0, waiting for transfers between devices: 34.2 us -> none  [the longest x1 6.74 us: body(): lax.all_to_all(value_cube, 'head', split_axis=1, concat_axis=0, tiled=True)]
    all_gather x2 -> x0, blocking collectives: 28.1 us -> none  [carried_in(): pieces = lax.all_gather(value, axis)]
    all_to_all x7 -> x0, starting transfers between devices: 26.3 us -> none  [the longest x1 5.3 us: body(): lax.all_to_all(cot_cube, 'head', split_axis=1, concat_axis=0, tiled=True)]
    ppermute x0 -> x8, waiting for transfers between devices: none -> 10.9 us  [the longest x3 4.65 us: carry_states(): received.append(lax.ppermute(message, axis, perm).astype(F32))]
    ppermute x0 -> x8, starting transfers between devices: none -> 9.94 us  [the longest x3 5.67 us: carry_states(): arrived = lax.ppermute(message, axis, perm).astype(F32)]
    dot_general x30 -> x0, matrix products: 6.76 us -> none  [the longest x4 1.49 us: block_grads(): jnp.einsum('hts,the->she', forward_weights, cot_block, preferred_element_...]
    unnamed x22 -> x16, local copies, waits for them, and re-layouts: 8.93 us -> 3.6 us
    pallas_call x0 -> x2, Pallas kernels: none -> 2.68 us  [the longest x1 2.36 us: body(): pl.pallas_call(grads_kernel, out_shape=tuple((jax.ShapeDtypeStruct(x.shap...]
  transfers between devices with their start and end apart: 7 -> 8, of which waited for: 6 -> 7; matrix products, arithmetic and copies ran while one was open for 7% -> 0% of each run, Pallas kernels for 0% -> 0%
where the time goes in v1:
time: 28.5 us; the launch traced here: 28.2 us
  waiting for transfers between devices  10.9 us (38%)
  starting transfers between devices  9.94 us (35%)
  local copies, waits for them, and re-layouts  3.6 us (13%)
  Pallas kernels  2.68 us (9%)
  between operations  0.8 us (3%)
  other arithmetic  0.3 us (1%)
    ppermute x3, starting transfers between devices, carry_states(): arrived = lax.ppermute(message, axis, perm).astype(F32)  5.67 us
    ppermute x3, waiting for transfers between devices, carry_states(): received.append(lax.ppermute(message, axis, perm).astype(F32))  4.65 us
    ppermute x3, waiting for transfers between devices, carry_states(): arrived = lax.ppermute(message, axis, perm).astype(F32)  4.14 us
    ppermute x3, starting transfers between devices, carry_states(): received.append(lax.ppermute(message, axis, perm).astype(F32))  3.67 us
    unnamed x16, local copies, waits for them, and re-layouts  3.6 us
    pallas_call x1, Pallas kernels, body(): pl.pallas_call(grads_kernel, out_shape=tuple((jax.ShapeDtypeStruct(x.shap...  2.36 us
    ppermute x1, waiting for transfers between devices, carry_states(): other = lax.ppermute(to_other, HEAD, swap)  1.22 us
    ppermute x1, waiting for transfers between devices, carry_states(): got = lax.ppermute(send, HEAD, swap).astype(F32)  0.9 us
  transfers between devices with their start and end apart: 8, of which 7 were waited for; matrix products, arithmetic and copies ran while one was open for 0% of the time, Pallas kernels for 0%

profile of v1, /device:TPU:0, one launch (start us, length us, event | category | flops | bytes accessed | tf_op | source)
XLA Modules:
  0.0 28.2 jit_solution(10997673630625537910)
XLA Ops:
  0.6 0.0 copy-start
  0.6 0.9 %copy-done = bf16[128,1024]{1,0:T(8,128)(2,1)S(1)} copy-done((bf16[128,1024]{1,0:T(8,128)(2,1)S(1)}, bf16[128,1024]{1,0:T(8,128)(2,1)}, u32[]{:S(2)}) %copy-start) | copy-done | bytes 262168
  1.6 0.0 copy-start.2
  1.6 0.9 %copy-done.2 = bf16[128,1024]{1,0:T(8,128)(2,1)S(1)} copy-done((bf16[128,1024]{1,0:T(8,128)(2,1)S(1)}, bf16[128,1024]{1,0:T(8,128)(2,1)}, u32[]{:S(2)}) %copy-start.2) | copy-done | bytes 262168
  2.5 0.0 copy-start.4
  2.5 0.8 %copy-done.4 = bf16[128,256]{1,0:T(8,128)(2,1)S(1)} copy-done((bf16[128,256]{1,0:T(8,128)(2,1)S(1)}, bf16[128,256]{1,0:T(8,128)(2,1)}, u32[]{:S(2)}) %copy-start.4) | copy-done | bytes 65560
  3.4 0.0 copy-start.6
  3.4 0.8 %copy-done.6 = bf16[128,256]{1,0:T(8,128)(2,1)S(1)} copy-done((bf16[128,256]{1,0:T(8,128)(2,1)S(1)}, bf16[128,256]{1,0:T(8,128)(2,1)}, u32[]{:S(2)}) %copy-start.6) | copy-done | bytes 65560
  4.2 0.3 %shard_map.67 = (bf16[2,1,128,128]{3,2,1,0:T(8,128)(2,1)S(1)}, bf16[2,1,128,128]{3,2,1,0:T(8,128)(2,1)S(1)}) custom-call(bf16[128,1024]{1,0:T(8,128)(2,1)S(1)} %copy-done, bf16[128,256]{1,0:T(8,128)(2,1)S(1)} %copy-done.4, bf16[128,256]{1,0:T(8,128)(2,1)S(1)} %copy-done.6, bf16[128,1024]{1,0:T(8,128)(2,1)S(1)} %copy-done.2), custom_call_target="tpu_custom_call" | custom-call | tf_op jit(solution)/shard_map/pallas_call | solution.py:174
  4.5 0.5 %collective-permute-start = (bf16[2,1,128,128]{3,2,1,0:T(8,128)(2,1)S(1)}, bf16[2,1,128,128]{3,2,1,0:T(8,128)(2,1)S(1)}, u32[]{:S(2)}, u32[]{:S(2)}) collective-permute-start(bf16[2,1,128,128]{3,2,1,0:T(8,128)(2,1)S(1)} %get-tuple-element.6), channel_id=1, source_target_pairs={{0,1},{1,0},{2,3},{3,2},{4,5},{5,4},{6,7},{7,6},{8,9},{9,8},{10,11... | collective-permute-start | bytes 196616 | tf_op jit(solution)/shard_map/ppermute | solution.py:126
  5.1 0.9 %collective-permute-done = bf16[2,1,128,128]{3,2,1,0:T(8,128)(2,1)S(1)} collective-permute-done((bf16[2,1,128,128]{3,2,1,0:T(8,128)(2,1)S(1)}, bf16[2,1,128,128]{3,2,1,0:T(8,128)(2,1)S(1)}, u32[]{:S(2)}, u32[]{:S(2)}) %collective-permute-start) | collective-permute-done | bytes 65568 | tf_op jit(solution)/shard_map/ppermute | solution.py:126
  6.0 5.0 %collective-permute-start.3 = (bf16[1,128,128]{2,1,0:T(8,128)(2,1)S(1)}, bf16[1,128,128]{2,1,0:T(8,128)(2,1)S(1)}, u32[]{:S(2)}, u32[]{:S(2)}) collective-permute-start(bf16[1,128,128]{2,1,0:T(8,128)(2,1)S(1)} %get-tuple-element.19), channel_id=1, source_target_pairs={{0,24},{8,16},{16,8},{24,0},{1,25},{9,17},{17,9},{25,1},{2,26},{10... | collective-permute-start | bytes 98312 | tf_op jit(solution)/shard_map/ppermute | solution.py:142
  11.0 0.0 collective-permute-start.2
  11.0 0.7 %collective-permute-start.1 = (bf16[1,128,128]{2,1,0:T(8,128)(2,1)S(1)}, bf16[1,128,128]{2,1,0:T(8,128)(2,1)S(1)}, u32[]{:S(2)}, u32[]{:S(2)}) collective-permute-start(bf16[1,128,128]{2,1,0:T(8,128)(2,1)S(1)} %get-tuple-element.21), channel_id=1, source_target_pairs={{0,8},{8,0},{16,24},{24,16},{1,9},{9,1},{17,25},{25,17},{2,10},{10... | collective-permute-start | bytes 98312 | tf_op jit(solution)/shard_map/ppermute | solution.py:142
  11.7 1.3 %collective-permute-done.3 = bf16[1,128,128]{2,1,0:T(8,128)(2,1)S(1)} collective-permute-done((bf16[1,128,128]{2,1,0:T(8,128)(2,1)S(1)}, bf16[1,128,128]{2,1,0:T(8,128)(2,1)S(1)}, u32[]{:S(2)}, u32[]{:S(2)}) %collective-permute-start.3) | collective-permute-done | bytes 32800 | tf_op jit(solution)/shard_map/ppermute | solution.py:142
  13.0 2.9 %collective-permute-done.2 = bf16[1,128,128]{2,1,0:T(8,128)(2,1)S(1)} collective-permute-done((bf16[1,128,128]{2,1,0:T(8,128)(2,1)S(1)}, bf16[1,128,128]{2,1,0:T(8,128)(2,1)S(1)}, u32[]{:S(2)}, u32[]{:S(2)}) %collective-permute-start.2) | collective-permute-done | bytes 32800 | tf_op jit(solution)/shard_map/ppermute | solution.py:142
  15.9 0.0 collective-permute-done.1
  15.9 0.1 add_convert_fusion.5
  16.0 1.6 %collective-permute-start.4 = (bf16[2,1,128,128]{3,2,1,0:T(8,128)(2,1)S(1)}, bf16[2,1,128,128]{3,2,1,0:T(8,128)(2,1)S(1)}, u32[]{:S(2)}, u32[]{:S(2)}) collective-permute-start(bf16[2,1,128,128]{3,2,1,0:T(8,128)(2,1)S(1)} %pad_maximum_fusion), channel_id=1, source_target_pairs={{0,2},{1,3},{2,0},{3,1},{4,6},{5,7},{6,4},{7,5},{8,10},{9,11},{10,... | collective-permute-start | bytes 196616 | tf_op jit(solution)/shard_map/ppermute | solution.py:153
  17.6 1.6 %collective-permute-start.5 = (bf16[2,1,128,128]{3,2,1,0:T(8,128)(2,1)S(1)}, bf16[2,1,128,128]{3,2,1,0:T(8,128)(2,1)S(1)}, u32[]{:S(2)}, u32[]{:S(2)}) collective-permute-start(bf16[2,1,128,128]{3,2,1,0:T(8,128)(2,1)S(1)} %pad_maximum_fusion.1), channel_id=1, source_target_pairs={{0,4},{1,5},{2,6},{3,7},{4,0},{5,1},{6,2},{7,3},{8,12},{9,13},{10,... | collective-permute-start | bytes 196616 | tf_op jit(solution)/shard_map/ppermute | solution.py:153
  19.1 0.5 %collective-permute-start.6 = (bf16[2,1,128,128]{3,2,1,0:T(8,128)(2,1)S(1)}, bf16[2,1,128,128]{3,2,1,0:T(8,128)(2,1)S(1)}, u32[]{:S(2)}, u32[]{:S(2)}) collective-permute-start(bf16[2,1,128,128]{3,2,1,0:T(8,128)(2,1)S(1)} %pad_maximum_fusion.2), channel_id=1, source_target_pairs={{0,6},{1,7},{2,4},{3,5},{4,2},{5,3},{6,0},{7,1},{8,14},{9,15},{10,... | collective-permute-start | bytes 196616 | tf_op jit(solution)/shard_map/ppermute | solution.py:153
  19.7 0.7 %collective-permute-done.4 = bf16[2,1,128,128]{3,2,1,0:T(8,128)(2,1)S(1)} collective-permute-done((bf16[2,1,128,128]{3,2,1,0:T(8,128)(2,1)S(1)}, bf16[2,1,128,128]{3,2,1,0:T(8,128)(2,1)S(1)}, u32[]{:S(2)}, u32[]{:S(2)}) %collective-permute-start.4) | collective-permute-done | bytes 65568 | tf_op jit(solution)/shard_map/ppermute | solution.py:153
  20.4 2.2 %collective-permute-done.5 = bf16[2,1,128,128]{3,2,1,0:T(8,128)(2,1)S(1)} collective-permute-done((bf16[2,1,128,128]{3,2,1,0:T(8,128)(2,1)S(1)}, bf16[2,1,128,128]{3,2,1,0:T(8,128)(2,1)S(1)}, u32[]{:S(2)}, u32[]{:S(2)}) %collective-permute-start.5) | collective-permute-done | bytes 65568 | tf_op jit(solution)/shard_map/ppermute | solution.py:153
  22.6 1.8 %collective-permute-done.6 = bf16[2,1,128,128]{3,2,1,0:T(8,128)(2,1)S(1)} collective-permute-done((bf16[2,1,128,128]{3,2,1,0:T(8,128)(2,1)S(1)}, bf16[2,1,128,128]{3,2,1,0:T(8,128)(2,1)S(1)}, u32[]{:S(2)}, u32[]{:S(2)}) %collective-permute-start.6) | collective-permute-done | bytes 65568 | tf_op jit(solution)/shard_map/ppermute | solution.py:153
  24.4 0.0 copy-start.3
  24.4 0.0 copy-start.5
  24.4 0.0 copy-start.7
  24.5 0.0 copy-start.1
  24.5 0.1 collective-permute-start.7
  24.6 1.2 %collective-permute-done.7.other_ref = bf16[2,1,128,128]{3,2,1,0:T(8,128)(2,1)S(1)} collective-permute-done((bf16[2,1,128,128]{3,2,1,0:T(8,128)(2,1)S(1)}, bf16[2,1,128,128]{3,2,1,0:T(8,128)(2,1)S(1)}, u32[]{:S(2)}, u32[]{:S(2)}) %collective-permute-start.7) | collective-permute-done | bytes 65568 | tf_op jit(solution)/shard_map/ppermute | solution.py:163
  25.9 0.0 copy-done.3
  25.9 0.0 copy-done.5
  25.9 0.0 copy-done.7
  25.9 0.0 copy-done.1
  25.9 2.4 %shard_map.68 = (bf16[128,1024]{1,0:T(8,128)(2,1)}, bf16[128,256]{1,0:T(8,128)(2,1)}, bf16[128,256]{1,0:T(8,128)(2,1)}) custom-call(bf16[128,1024]{1,0:T(8,128)(2,1)S(1)} %copy-done.1, bf16[128,256]{1,0:T(8,128)(2,1)S(1)} %copy-done.5, bf16[128,256]{1,0:T(8,128)(2,1)S(1)} %copy-done.7, bf16[128,1024]{1,0:T(8,128)(2,1)S(1)} %copy-done.3, ...), custom_call_target="tpu_custom_call" | custom-call | tf_op jit(solution)/shard_map/pallas_call | solution.py:182
  (15 shorter events, 0.2 us)
Async XLA Ops:
  0.6 1.0 %copy-start = (bf16[128,1024]{1,0:T(8,128)(2,1)S(1)}, bf16[128,1024]{1,0:T(8,128)(2,1)}, u32[]{:S(2)}) copy-start(bf16[128,1024]{1,0:T(8,128)(2,1)} %q_ref.3) | copy-start | bytes 786436
  1.6 0.9 %copy-start.2 = (bf16[128,1024]{1,0:T(8,128)(2,1)S(1)}, bf16[128,1024]{1,0:T(8,128)(2,1)}, u32[]{:S(2)}) copy-start(bf16[128,1024]{1,0:T(8,128)(2,1)} %o_ref.3) | copy-start | bytes 786436
  2.5 0.8 %copy-start.4 = (bf16[128,256]{1,0:T(8,128)(2,1)S(1)}, bf16[128,256]{1,0:T(8,128)(2,1)}, u32[]{:S(2)}) copy-start(bf16[128,256]{1,0:T(8,128)(2,1)} %k_ref.3) | copy-start | bytes 196612
  3.4 0.8 %copy-start.6 = (bf16[128,256]{1,0:T(8,128)(2,1)S(1)}, bf16[128,256]{1,0:T(8,128)(2,1)}, u32[]{:S(2)}) copy-start(bf16[128,256]{1,0:T(8,128)(2,1)} %v_ref.3) | copy-start | bytes 196612
  4.5 1.4 %collective-permute-start = (bf16[2,1,128,128]{3,2,1,0:T(8,128)(2,1)S(1)}, bf16[2,1,128,128]{3,2,1,0:T(8,128)(2,1)S(1)}, u32[]{:S(2)}, u32[]{:S(2)}) collective-permute-start(bf16[2,1,128,128]{3,2,1,0:T(8,128)(2,1)S(1)} %get-tuple-element.6), channel_id=1, source_target_pairs={{0,1},{1,0},{2,3},{3,2},{4,5},{5,4},{6,7},{7,6},{8,9},{9,8},{10,11... | collective-permute-start | bytes 196616 | tf_op jit(solution)/shard_map/ppermute | solution.py:126
  6.0 7.0 %collective-permute-start.3 = (bf16[1,128,128]{2,1,0:T(8,128)(2,1)S(1)}, bf16[1,128,128]{2,1,0:T(8,128)(2,1)S(1)}, u32[]{:S(2)}, u32[]{:S(2)}) collective-permute-start(bf16[1,128,128]{2,1,0:T(8,128)(2,1)S(1)} %get-tuple-element.19), channel_id=1, source_target_pairs={{0,24},{8,16},{16,8},{24,0},{1,25},{9,17},{17,9},{25,1},{2,26},{10... | collective-permute-start | bytes 98312 | tf_op jit(solution)/shard_map/ppermute | solution.py:142
  11.0 4.8 %collective-permute-start.2 = (bf16[1,128,128]{2,1,0:T(8,128)(2,1)S(1)}, bf16[1,128,128]{2,1,0:T(8,128)(2,1)S(1)}, u32[]{:S(2)}, u32[]{:S(2)}) collective-permute-start(bf16[1,128,128]{2,1,0:T(8,128)(2,1)S(1)} %get-tuple-element.20), channel_id=1, source_target_pairs={{0,16},{8,24},{16,0},{24,8},{1,17},{9,25},{17,1},{25,9},{2,18},{10... | collective-permute-start | bytes 98312 | tf_op jit(solution)/shard_map/ppermute | solution.py:142
  11.0 4.8 %collective-permute-start.1 = (bf16[1,128,128]{2,1,0:T(8,128)(2,1)S(1)}, bf16[1,128,128]{2,1,0:T(8,128)(2,1)S(1)}, u32[]{:S(2)}, u32[]{:S(2)}) collective-permute-start(bf16[1,128,128]{2,1,0:T(8,128)(2,1)S(1)} %get-tuple-element.21), channel_id=1, source_target_pairs={{0,8},{8,0},{16,24},{24,16},{1,9},{9,1},{17,25},{25,17},{2,10},{10... | collective-permute-start | bytes 98312 | tf_op jit(solution)/shard_map/ppermute | solution.py:142
  16.0 4.4 %collective-permute-start.4 = (bf16[2,1,128,128]{3,2,1,0:T(8,128)(2,1)S(1)}, bf16[2,1,128,128]{3,2,1,0:T(8,128)(2,1)S(1)}, u32[]{:S(2)}, u32[]{:S(2)}) collective-permute-start(bf16[2,1,128,128]{3,2,1,0:T(8,128)(2,1)S(1)} %pad_maximum_fusion), channel_id=1, source_target_pairs={{0,2},{1,3},{2,0},{3,1},{4,6},{5,7},{6,4},{7,5},{8,10},{9,11},{10,... | collective-permute-start | bytes 196616 | tf_op jit(solution)/shard_map/ppermute | solution.py:153
  17.6 5.0 %collective-permute-start.5 = (bf16[2,1,128,128]{3,2,1,0:T(8,128)(2,1)S(1)}, bf16[2,1,128,128]{3,2,1,0:T(8,128)(2,1)S(1)}, u32[]{:S(2)}, u32[]{:S(2)}) collective-permute-start(bf16[2,1,128,128]{3,2,1,0:T(8,128)(2,1)S(1)} %pad_maximum_fusion.1), channel_id=1, source_target_pairs={{0,4},{1,5},{2,6},{3,7},{4,0},{5,1},{6,2},{7,3},{8,12},{9,13},{10,... | collective-permute-start | bytes 196616 | tf_op jit(solution)/shard_map/ppermute | solution.py:153
  19.1 5.2 %collective-permute-start.6 = (bf16[2,1,128,128]{3,2,1,0:T(8,128)(2,1)S(1)}, bf16[2,1,128,128]{3,2,1,0:T(8,128)(2,1)S(1)}, u32[]{:S(2)}, u32[]{:S(2)}) collective-permute-start(bf16[2,1,128,128]{3,2,1,0:T(8,128)(2,1)S(1)} %pad_maximum_fusion.2), channel_id=1, source_target_pairs={{0,6},{1,7},{2,4},{3,5},{4,2},{5,3},{6,0},{7,1},{8,14},{9,15},{10,... | collective-permute-start | bytes 196616 | tf_op jit(solution)/shard_map/ppermute | solution.py:153
  24.4 1.4 %copy-start.3 = (bf16[128,1024]{1,0:T(8,128)(2,1)S(1)}, bf16[128,1024]{1,0:T(8,128)(2,1)}, u32[]{:S(2)}) copy-start(bf16[128,1024]{1,0:T(8,128)(2,1)} %o_ref.3) | copy-start | bytes 786436
  24.4 1.4 %copy-start.5 = (bf16[128,256]{1,0:T(8,128)(2,1)S(1)}, bf16[128,256]{1,0:T(8,128)(2,1)}, u32[]{:S(2)}) copy-start(bf16[128,256]{1,0:T(8,128)(2,1)} %k_ref.3) | copy-start | bytes 196612
  24.4 1.4 %copy-start.7 = (bf16[128,256]{1,0:T(8,128)(2,1)S(1)}, bf16[128,256]{1,0:T(8,128)(2,1)}, u32[]{:S(2)}) copy-start(bf16[128,256]{1,0:T(8,128)(2,1)} %v_ref.3) | copy-start | bytes 196612
  24.5 1.4 %copy-start.1 = (bf16[128,1024]{1,0:T(8,128)(2,1)S(1)}, bf16[128,1024]{1,0:T(8,128)(2,1)}, u32[]{:S(2)}) copy-start(bf16[128,1024]{1,0:T(8,128)(2,1)} %q_ref.3) | copy-start | bytes 786436
  24.5 1.3 %collective-permute-start.7 = (bf16[2,1,128,128]{3,2,1,0:T(8,128)(2,1)S(1)}, bf16[2,1,128,128]{3,2,1,0:T(8,128)(2,1)S(1)}, u32[]{:S(2)}, u32[]{:S(2)}) collective-permute-start(bf16[2,1,128,128]{3,2,1,0:T(8,128)(2,1)S(1)} %pad_maximum_fusion.4), channel_id=1, source_target_pairs={{0,1},{1,0},{2,3},{3,2},{4,5},{5,4},{6,7},{7,6},{8,9},{9,8},{10,11... | collective-permute-start | bytes 196616 | tf_op jit(solution)/shard_map/ppermute | solution.py:163

commit v2 on v1

v2 whole, which is shorter than its diff:
```python
import functools

import jax
import jax.numpy as jnp
from jax import lax
from jax.experimental import pallas as pl
from jax.experimental.pallas import tpu as pltpu
from jax.sharding import PartitionSpec as P

HD = 128
SEQ = "seq"
HEAD = "head"
DEVICES = (SEQ, HEAD)
TOP_BITS = 2
LOW_BITS = 2
MIB = 1024 * 1024
BF16 = jnp.bfloat16
F32 = jnp.float32

NN = (((1,), (0,)), ((), ()))
NT = (((1,), (1,)), ((), ()))
TN = (((0,), (0,)), ((), ()))


def dot(left, right, dims):
    return lax.dot_general(left, right, dims, preferred_element_type=F32)


def columns(index):
    return (slice(None), slice(index * HD, (index + 1) * HD))


def device_index():
    return lax.axis_index(SEQ) * lax.axis_size(HEAD) + lax.axis_index(HEAD)


def row_scale(tokens, shape, axis):
    positions = device_index() * tokens + lax.broadcasted_iota(jnp.int32, shape, axis)
    return 1.0 / jnp.sqrt((HD * (positions + 1)).astype(F32))


def states_kernel(q_hbm, k_hbm, v_hbm, o_hbm, keep_ref, send_ref, q_ref, k_ref, v_ref, o_ref, sems):
    tokens = q_hbm.shape[0]
    kv = k_hbm.shape[1] // HD
    width = q_hbm.shape[1] // kv
    group = width // HD
    half = kv // 2
    small = [
        pltpu.make_async_copy(k_hbm, k_ref, sems.at[0, 0]),
        pltpu.make_async_copy(v_hbm, v_ref, sems.at[1, 0]),
    ]
    large = []
    for g in range(kv):
        at = (slice(None), slice(g * width, (g + 1) * width))
        large.append(
            [
                pltpu.make_async_copy(o_hbm.at[at], o_ref.at[at], sems.at[0, 1 + g]),
                pltpu.make_async_copy(q_hbm.at[at], q_ref.at[at], sems.at[1, 1 + g]),
            ]
        )
    for copy in small:
        copy.start()
    for copies in large:
        for copy in copies:
            copy.start()
    core = lax.rem(lax.axis_index(HEAD), 2)
    scale = row_scale(tokens, (tokens, HD), 0)

    def put(g, kind, state):
        mine = core == g // half

        @pl.when(mine)
        def _():
            keep_ref[kind, g % half] = state

        @pl.when(jnp.logical_not(mine))
        def _():
            send_ref[kind, g % half] = state

    for copy in small:
        copy.wait()
    for g in range(kv):
        put(g, 0, dot(v_ref[columns(g)], k_ref[columns(g)], TN).astype(BF16))
    for g in range(kv):
        for copy in large[g]:
            copy.wait()
        grad = jnp.zeros((HD, HD), F32)
        for h in range(g * group, (g + 1) * group):
            scaled = (scale * o_ref[columns(h)].astype(F32)).astype(BF16)
            grad = grad + dot(scaled, q_ref[columns(h)], TN)
        put(g, 1, grad.astype(BF16))


def local_kernel(q_ref, k_ref, v_ref, o_ref, qg_ref, kg_ref, vg_ref):
    tokens = q_ref.shape[0]
    kv = k_ref.shape[1] // HD
    group = q_ref.shape[1] // HD // kv
    scale = row_scale(tokens, (tokens, HD), 0)
    scale_row = row_scale(tokens, (HD, tokens), 1)
    rows = lax.broadcasted_iota(jnp.int32, (tokens, tokens), 0)
    cols = lax.broadcasted_iota(jnp.int32, (tokens, tokens), 1)
    causal = rows >= cols
    causal_t = rows <= cols
    for g in range(kv):
        key = k_ref[columns(g)]
        value = v_ref[columns(g)]
        key_grad = jnp.zeros((tokens, HD), F32)
        value_grad = jnp.zeros((tokens, HD), F32)
        for h in range(g * group, (g + 1) * group):
            query = q_ref[columns(h)]
            cot = o_ref[columns(h)]
            scaled = (scale * cot.astype(F32)).astype(BF16)
            backward = jnp.where(causal, dot(scaled, value, NT), 0.0).astype(BF16)
            backward_t = jnp.where(causal_t, dot(value, scaled, NT), 0.0).astype(BF16)
            forward_t = jnp.where(causal_t, scale_row * dot(key, query, NT), 0.0).astype(BF16)
            qg_ref[columns(h)] = dot(backward, key, NN)
            key_grad = key_grad + dot(backward_t, query, NN)
            value_grad = value_grad + dot(forward_t, cot, NN)
        kg_ref[columns(g)] = key_grad
        vg_ref[columns(g)] = value_grad


def finish_kernel(
    k_ref, v_ref, o_ref, ql_ref, kl_ref, vl_ref, mine_ref, other_ref,
    qg_hbm, kg_hbm, vg_hbm, carried, qg_ref, kg_ref, vg_ref, sems,
):
    tokens = o_ref.shape[0]
    kv = k_ref.shape[1] // HD
    width = o_ref.shape[1] // kv
    group = width // HD
    half = kv // 2
    core = lax.rem(lax.axis_index(HEAD), 2)
    carried[core] = mine_ref[...]
    carried[1 - core] = other_ref[...]
    scale = row_scale(tokens, (tokens, HD), 0)
    copies = []
    for g in range(kv):
        prior = carried[g // half, 0, g % half]
        for h in range(g * group, (g + 1) * group):
            scaled = (scale * o_ref[columns(h)].astype(F32)).astype(BF16)
            qg_ref[columns(h)] = (ql_ref[columns(h)] + dot(scaled, prior, NN)).astype(BF16)
        at = (slice(None), slice(g * width, (g + 1) * width))
        copies.append(pltpu.make_async_copy(qg_ref.at[at], qg_hbm.at[at], sems.at[g]))
        copies[-1].start()
    for g in range(kv):
        future = carried[g // half, 1, g % half]
        key_grad = kl_ref[columns(g)] + dot(v_ref[columns(g)], future, NN)
        value_grad = vl_ref[columns(g)] + dot(k_ref[columns(g)], future, NT)
        kg_ref[columns(g)] = key_grad.astype(BF16)
        vg_ref[columns(g)] = value_grad.astype(BF16)
    copies.append(pltpu.make_async_copy(kg_ref, kg_hbm, sems.at[kv]))
    copies.append(pltpu.make_async_copy(vg_ref, vg_hbm, sems.at[kv + 1]))
    for copy in copies[-2:]:
        copy.start()
    for copy in copies:
        copy.wait()


def bit_groups(size):
    bits = size.bit_length() - 1
    assert 1 << bits == size
    low = list(range(1, max(1, bits - TOP_BITS)))
    groups = [low[i : i + LOW_BITS] for i in range(0, len(low), LOW_BITS)]
    return groups + [list(range(max(1, bits - TOP_BITS), bits))]


def flips_of(group):
    masks = [0]
    for bit in group:
        masks += [mask | 1 << bit for mask in masks]
    return masks[1:]


def carry_states(keep, send):
    size = lax.axis_size(SEQ) * lax.axis_size(HEAD)
    index = device_index()
    swap = [(i, i ^ 1) for i in range(size)]
    got = lax.ppermute(send, DEVICES, swap).astype(F32)
    keep = keep.astype(F32)
    total = keep + got
    earlier = jnp.zeros_like(total[0])
    later = jnp.zeros_like(total[1])
    groups = bit_groups(size)
    for group in groups[:-1]:
        message = total.astype(BF16)
        for flip in flips_of(group):
            arrived = lax.ppermute(message, DEVICES, [(i, i ^ flip) for i in range(size)]).astype(F32)
            lower = index < (index ^ flip)
            earlier = earlier + jnp.where(lower, 0.0, arrived[0])
            later = later + jnp.where(lower, arrived[1], 0.0)
            total = total + arrived
    message = total.astype(BF16)
    for flip in flips_of(groups[-1]):
        lower = index < (index ^ flip)
        arrived = lax.ppermute(
            jnp.where(lower, message[0], message[1]), DEVICES, [(i, i ^ flip) for i in range(size)]
        ).astype(F32)
        earlier = earlier + jnp.where(lower, 0.0, arrived)
        later = later + jnp.where(lower, arrived, 0.0)
    first = index % 2 == 0
    mine = jnp.stack([earlier + jnp.where(first, 0.0, got[0]), later + jnp.where(first, got[1], 0.0)])
    theirs = jnp.stack([earlier + jnp.where(first, keep[0], 0.0), later + jnp.where(first, 0.0, keep[1])])
    return mine.astype(BF16), lax.ppermute(theirs.astype(BF16), DEVICES, swap)


def body(queries, keys, values, out_grad):
    kv = keys.shape[1] // HD
    shape = (2, kv // 2, HD, HD)
    vmem = pl.BlockSpec(memory_space=pltpu.VMEM)
    anywhere = pl.BlockSpec(memory_space=pltpu.HBM)
    inputs = (queries, keys, values, out_grad)
    tokens, wide, narrow = queries.shape[0], queries.shape[1], keys.shape[1]
    keep, send = pl.pallas_call(
        states_kernel,
        out_shape=(jax.ShapeDtypeStruct(shape, BF16),) * 2,
        in_specs=[anywhere] * 4,
        out_specs=[vmem] * 2,
        scratch_shapes=[pltpu.VMEM(x.shape, BF16) for x in inputs] + [pltpu.SemaphoreType.DMA((2, kv + 1))],
        compiler_params=pltpu.CompilerParams(vmem_limit_bytes=55104 * 1024),
    )(*inputs)
    local = pl.pallas_call(
        local_kernel,
        out_shape=tuple(jax.ShapeDtypeStruct(x.shape, F32) for x in (queries, keys, values)),
        in_specs=[vmem] * 4,
        out_specs=[vmem] * 3,
        cost_estimate=pl.CostEstimate(
            flops=12 * tokens * tokens * wide, bytes_accessed=12 * tokens * wide, transcendentals=0
        ),
        compiler_params=pltpu.CompilerParams(vmem_limit_bytes=24 * MIB),
    )(*inputs)
    mine, other = carry_states(keep, send)
    return pl.pallas_call(
        finish_kernel,
        out_shape=tuple(jax.ShapeDtypeStruct(x.shape, BF16) for x in (queries, keys, values)),
        in_specs=[vmem] * 8,
        out_specs=[anywhere] * 3,
        scratch_shapes=[pltpu.VMEM((2,) + shape, BF16)]
        + [pltpu.VMEM(x.shape, BF16) for x in (queries, keys, values)]
        + [pltpu.SemaphoreType.DMA((kv + 2,))],
        compiler_params=pltpu.CompilerParams(vmem_limit_bytes=24 * MIB),
    )(keys, values, out_grad, *local, mine, other)


def solution(mesh):
    spec = P(DEVICES, None)
    return jax.shard_map(
        body, mesh=mesh, in_specs=(spec,) * 4, out_specs=(spec,) * 3, check_vma=False
    )
```

time: 28.5 us -> 24.5 us (0.86)
  local copies, waits for them, and re-layouts: 3.6 us -> 0.83 us
  waiting for transfers between devices: 10.9 us -> 8.75 us
  Pallas kernels: 2.68 us -> 4.39 us
  starting transfers between devices: 9.94 us -> 9.32 us
    unnamed x16 -> x8, local copies, waits for them, and re-layouts: 3.6 us -> 0.83 us
    ppermute x8, waiting for transfers between devices: 10.9 us -> 8.75 us  [the longest x3 4.13 us: carry_states(): lax.ppermute(message, DEVICES, [(i, i ^ flip) for i in range(size)])]
    pallas_call x1, Pallas kernels: 0.32 us -> 1.79 us  [body(): pl.pallas_call(states_kernel, out_shape=(jax.ShapeDtypeStruct(shape, BF16...]
    ppermute x8, starting transfers between devices: 9.94 us -> 9.32 us  [the longest x3 4.5 us: carry_states(): lax.ppermute(message, DEVICES, [(i, i ^ flip) for i in range(size)])]
    pallas_call x1 -> x2, Pallas kernels: 2.36 us -> 2.6 us  [the longest x1 1.56 us: body(): pl.pallas_call(local_kernel, out_shape=tuple((jax.ShapeDtypeStruct(x.shap...]
  transfers between devices with their start and end apart: 8 -> 8, of which waited for: 7 -> 7; matrix products, arithmetic and copies ran while one was open for 0% -> 0% of each run, Pallas kernels for 0% -> 6%
where the time goes in v2:
time: 24.5 us; the launch traced here: 24.3 us
  starting transfers between devices  9.32 us (38%)
  waiting for transfers between devices  8.75 us (36%)
  Pallas kernels  4.39 us (18%)
  local copies, waits for them, and re-layouts  0.83 us (3%)
  between operations  0.78 us (3%)
  other arithmetic  0.26 us (1%)
    ppermute x3, starting transfers between devices, carry_states(): lax.ppermute(message, DEVICES, [(i, i ^ flip) for i in range(size)])  4.5 us
    ppermute x3, starting transfers between devices, carry_states(): lax.ppermute(jnp.where(lower, message[0], message[1]), DEVICES, [(i, i ^...  4.23 us
    ppermute x3, waiting for transfers between devices, carry_states(): lax.ppermute(message, DEVICES, [(i, i ^ flip) for i in range(size)])  4.13 us
    ppermute x3, waiting for transfers between devices, carry_states(): lax.ppermute(jnp.where(lower, message[0], message[1]), DEVICES, [(i, i ^...  2.53 us
    pallas_call x1, Pallas kernels, body(): pl.pallas_call(states_kernel, out_shape=(jax.ShapeDtypeStruct(shape, BF16...  1.79 us
    pallas_call x1, Pallas kernels, body(): pl.pallas_call(local_kernel, out_shape=tuple((jax.ShapeDtypeStruct(x.shap...  1.56 us
    ppermute x1, waiting for transfers between devices, carry_states(): return (mine.astype(BF16), lax.ppermute(theirs.astype(BF16), DEVICES, swap))  1.2 us
    pallas_call x1, Pallas kernels, body(): pl.pallas_call(finish_kernel, out_shape=tuple((jax.ShapeDtypeStruct(x.sha...  1.04 us
  transfers between devices with their start and end apart: 8, of which 7 were waited for; matrix products, arithmetic and copies ran while one was open for 0% of the time, Pallas kernels for 6%

profile of v2, /device:TPU:0, one launch (start us, length us, event | category | flops | bytes accessed | tf_op | source)
XLA Modules:
  0.0 24.3 jit_solution(11356703914508980902)
XLA Ops:
  0.6 1.8 %shard_map.68 = (bf16[2,1,128,128]{3,2,1,0:T(8,128)(2,1)S(1)}, bf16[2,1,128,128]{3,2,1,0:T(8,128)(2,1)S(1)}) custom-call(bf16[128,1024]{1,0:T(8,128)(2,1)} %q_hbm.1, bf16[128,256]{1,0:T(8,128)(2,1)} %k_ref.3, bf16[128,256]{1,0:T(8,128)(2,1)} %v_ref.3, bf16[128,1024]{1,0:T(8,128)(2,1)} %o_ref.3), custom_call_target="tpu_custom_call" | custom-call | tf_op jit(solution)/shard_map/pallas_call | solution.py:213
  2.4 0.5 %collective-permute-start = (bf16[2,1,128,128]{3,2,1,0:T(8,128)(2,1)S(1)}, bf16[2,1,128,128]{3,2,1,0:T(8,128)(2,1)S(1)}, u32[]{:S(2)}, u32[]{:S(2)}) collective-permute-start(bf16[2,1,128,128]{3,2,1,0:T(8,128)(2,1)S(1)} %get-tuple-element.12), channel_id=1, source_target_pairs={{0,1},{1,0},{2,3},{3,2},{4,5},{5,4},{6,7},{7,6},{8,9},{9,8},{10,11... | collective-permute-start | bytes 196616 | tf_op jit(solution)/shard_map/ppermute | solution.py:178
  2.9 0.9 %collective-permute-done = bf16[2,1,128,128]{3,2,1,0:T(8,128)(2,1)S(1)} collective-permute-done((bf16[2,1,128,128]{3,2,1,0:T(8,128)(2,1)S(1)}, bf16[2,1,128,128]{3,2,1,0:T(8,128)(2,1)S(1)}, u32[]{:S(2)}, u32[]{:S(2)}) %collective-permute-start) | collective-permute-done | bytes 65568 | tf_op jit(solution)/shard_map/ppermute | solution.py:178
  3.9 3.9 %collective-permute-start.3 = (bf16[2,1,128,128]{3,2,1,0:T(8,128)(2,1)S(1)}, bf16[2,1,128,128]{3,2,1,0:T(8,128)(2,1)S(1)}, u32[]{:S(2)}, u32[]{:S(2)}) collective-permute-start(bf16[2,1,128,128]{3,2,1,0:T(8,128)(2,1)S(1)} %fusion.28), channel_id=1, source_target_pairs={{0,6},{1,7},{2,4},{3,5},{4,2},{5,3},{6,0},{7,1},{8,14},{9,15},{10,... | collective-permute-start | bytes 196616 | tf_op jit(solution)/shard_map/ppermute | solution.py:187
  7.7 0.5 %collective-permute-start.2 = (bf16[2,1,128,128]{3,2,1,0:T(8,128)(2,1)S(1)}, bf16[2,1,128,128]{3,2,1,0:T(8,128)(2,1)S(1)}, u32[]{:S(2)}, u32[]{:S(2)}) collective-permute-start(bf16[2,1,128,128]{3,2,1,0:T(8,128)(2,1)S(1)} %fusion.28), channel_id=1, source_target_pairs={{0,4},{1,5},{2,6},{3,7},{4,0},{5,1},{6,2},{7,3},{8,12},{9,13},{10,... | collective-permute-start | bytes 196616 | tf_op jit(solution)/shard_map/ppermute | solution.py:187
  8.2 0.1 collective-permute-start.1
  8.4 1.8 %collective-permute-done.3 = bf16[2,1,128,128]{3,2,1,0:T(8,128)(2,1)S(1)} collective-permute-done((bf16[2,1,128,128]{3,2,1,0:T(8,128)(2,1)S(1)}, bf16[2,1,128,128]{3,2,1,0:T(8,128)(2,1)S(1)}, u32[]{:S(2)}, u32[]{:S(2)}) %collective-permute-start.3) | collective-permute-done | bytes 65568 | tf_op jit(solution)/shard_map/ppermute | solution.py:187
  10.2 1.9 %collective-permute-done.2 = bf16[2,1,128,128]{3,2,1,0:T(8,128)(2,1)S(1)} collective-permute-done((bf16[2,1,128,128]{3,2,1,0:T(8,128)(2,1)S(1)}, bf16[2,1,128,128]{3,2,1,0:T(8,128)(2,1)S(1)}, u32[]{:S(2)}, u32[]{:S(2)}) %collective-permute-start.2) | collective-permute-done | bytes 65568 | tf_op jit(solution)/shard_map/ppermute | solution.py:187
  12.0 0.5 %collective-permute-done.1 = bf16[2,1,128,128]{3,2,1,0:T(8,128)(2,1)S(1)} collective-permute-done((bf16[2,1,128,128]{3,2,1,0:T(8,128)(2,1)S(1)}, bf16[2,1,128,128]{3,2,1,0:T(8,128)(2,1)S(1)}, u32[]{:S(2)}, u32[]{:S(2)}) %collective-permute-start.1) | collective-permute-done | bytes 65568 | tf_op jit(solution)/shard_map/ppermute | solution.py:187
  12.5 0.0 copy-start.3
  12.6 0.0 copy-start
  12.6 1.6 %collective-permute-start.4 = (bf16[1,128,128]{2,1,0:T(8,128)(2,1)S(1)}, bf16[1,128,128]{2,1,0:T(8,128)(2,1)S(1)}, u32[]{:S(2)}, u32[]{:S(2)}) collective-permute-start(bf16[1,128,128]{2,1,0:T(8,128)(2,1)S(1)} %get-tuple-element.21), channel_id=1, source_target_pairs={{0,8},{1,9},{2,10},{3,11},{4,12},{5,13},{6,14},{7,15},{8,0},{9,1},... | collective-permute-start | bytes 98312 | tf_op jit(solution)/shard_map/ppermute | solution.py:195
  14.2 2.5 %collective-permute-start.6 = (bf16[1,128,128]{2,1,0:T(8,128)(2,1)S(1)}, bf16[1,128,128]{2,1,0:T(8,128)(2,1)S(1)}, u32[]{:S(2)}, u32[]{:S(2)}) collective-permute-start(bf16[1,128,128]{2,1,0:T(8,128)(2,1)S(1)} %get-tuple-element.22), channel_id=1, source_target_pairs={{0,24},{1,25},{2,26},{3,27},{4,28},{5,29},{6,30},{7,31},{8,16},{9,... | collective-permute-start | bytes 98312 | tf_op jit(solution)/shard_map/ppermute | solution.py:195
  16.7 0.1 collective-permute-start.5
  16.8 0.0 copy-start.1
  16.8 0.0 copy-start.2
  16.9 0.0 copy-done.3
  16.9 0.0 copy-done
  16.9 0.8 %copy-done.1 = bf16[128,256]{1,0:T(8,128)(2,1)S(1)} copy-done((bf16[128,256]{1,0:T(8,128)(2,1)S(1)}, bf16[128,256]{1,0:T(8,128)(2,1)}, u32[]{:S(2)}) %copy-start.1) | copy-done | bytes 65560
  17.7 0.0 copy-done.2
  17.7 1.6 %shard_map.67 = (f32[128,1024]{1,0:T(8,128)S(1)}, f32[128,256]{1,0:T(8,128)S(1)}, f32[128,256]{1,0:T(8,128)S(1)}) custom-call(bf16[128,1024]{1,0:T(8,128)(2,1)S(1)} %copy-done.3, bf16[128,256]{1,0:T(8,128)(2,1)S(1)} %copy-done.1, bf16[128,256]{1,0:T(8,128)(2,1)S(1)} %copy-done.2, bf16[128,1024]{1,0:T(8,128)(2,1)S(1)} %copy-done), custom_call_target="tpu_custom_call" | custom-call | flops 201326592 | bytes 1572864 | tf_op jit(solution)/shard_map/pallas_call | solution.py:221
  19.3 0.0 collective-permute-done.4
  19.4 0.6 %collective-permute-done.6 = bf16[1,128,128]{2,1,0:T(8,128)(2,1)S(1)} collective-permute-done((bf16[1,128,128]{2,1,0:T(8,128)(2,1)S(1)}, bf16[1,128,128]{2,1,0:T(8,128)(2,1)S(1)}, u32[]{:S(2)}, u32[]{:S(2)}) %collective-permute-start.6) | collective-permute-done | bytes 32800 | tf_op jit(solution)/shard_map/ppermute | solution.py:195
  20.0 1.9 %collective-permute-done.5 = bf16[1,128,128]{2,1,0:T(8,128)(2,1)S(1)} collective-permute-done((bf16[1,128,128]{2,1,0:T(8,128)(2,1)S(1)}, bf16[1,128,128]{2,1,0:T(8,128)(2,1)S(1)}, u32[]{:S(2)}, u32[]{:S(2)}) %collective-permute-start.5) | collective-permute-done | bytes 32800 | tf_op jit(solution)/shard_map/ppermute | solution.py:195
  21.9 0.1 fusion.26
  22.0 0.1 collective-permute-start.7
  22.1 1.2 %collective-permute-done.7.other_ref = bf16[2,1,128,128]{3,2,1,0:T(8,128)(2,1)S(1)} collective-permute-done((bf16[2,1,128,128]{3,2,1,0:T(8,128)(2,1)S(1)}, bf16[2,1,128,128]{3,2,1,0:T(8,128)(2,1)S(1)}, u32[]{:S(2)}, u32[]{:S(2)}) %collective-permute-start.7) | collective-permute-done | bytes 65568 | tf_op jit(solution)/shard_map/ppermute | solution.py:203
  23.3 1.0 %shard_map.69 = (bf16[128,1024]{1,0:T(8,128)(2,1)}, bf16[128,256]{1,0:T(8,128)(2,1)}, bf16[128,256]{1,0:T(8,128)(2,1)}) custom-call(bf16[128,256]{1,0:T(8,128)(2,1)S(1)} %copy-done.1, bf16[128,256]{1,0:T(8,128)(2,1)S(1)} %copy-done.2, bf16[128,1024]{1,0:T(8,128)(2,1)S(1)} %copy-done, f32[128,1024]{1,0:T(8,128)S(1)} %get-tuple-element.8.ql_ref, ...), custom_call_target="tpu_custom_call" | custom-call | tf_op jit(solution)/shard_map/pallas_call | solution.py:232
  (11 shorter events, 0.2 us)
Async XLA Ops:
  2.4 1.4 %collective-permute-start = (bf16[2,1,128,128]{3,2,1,0:T(8,128)(2,1)S(1)}, bf16[2,1,128,128]{3,2,1,0:T(8,128)(2,1)S(1)}, u32[]{:S(2)}, u32[]{:S(2)}) collective-permute-start(bf16[2,1,128,128]{3,2,1,0:T(8,128)(2,1)S(1)} %get-tuple-element.12), channel_id=1, source_target_pairs={{0,1},{1,0},{2,3},{3,2},{4,5},{5,4},{6,7},{7,6},{8,9},{9,8},{10,11... | collective-permute-start | bytes 196616 | tf_op jit(solution)/shard_map/ppermute | solution.py:178
  3.9 6.3 %collective-permute-start.3 = (bf16[2,1,128,128]{3,2,1,0:T(8,128)(2,1)S(1)}, bf16[2,1,128,128]{3,2,1,0:T(8,128)(2,1)S(1)}, u32[]{:S(2)}, u32[]{:S(2)}) collective-permute-start(bf16[2,1,128,128]{3,2,1,0:T(8,128)(2,1)S(1)} %fusion.28), channel_id=1, source_target_pairs={{0,6},{1,7},{2,4},{3,5},{4,2},{5,3},{6,0},{7,1},{8,14},{9,15},{10,... | collective-permute-start | bytes 196616 | tf_op jit(solution)/shard_map/ppermute | solution.py:187
  7.7 4.3 %collective-permute-start.2 = (bf16[2,1,128,128]{3,2,1,0:T(8,128)(2,1)S(1)}, bf16[2,1,128,128]{3,2,1,0:T(8,128)(2,1)S(1)}, u32[]{:S(2)}, u32[]{:S(2)}) collective-permute-start(bf16[2,1,128,128]{3,2,1,0:T(8,128)(2,1)S(1)} %fusion.28), channel_id=1, source_target_pairs={{0,4},{1,5},{2,6},{3,7},{4,0},{5,1},{6,2},{7,3},{8,12},{9,13},{10,... | collective-permute-start | bytes 196616 | tf_op jit(solution)/shard_map/ppermute | solution.py:187
  8.2 4.3 %collective-permute-start.1 = (bf16[2,1,128,128]{3,2,1,0:T(8,128)(2,1)S(1)}, bf16[2,1,128,128]{3,2,1,0:T(8,128)(2,1)S(1)}, u32[]{:S(2)}, u32[]{:S(2)}) collective-permute-start(bf16[2,1,128,128]{3,2,1,0:T(8,128)(2,1)S(1)} %fusion.28), channel_id=1, source_target_pairs={{0,2},{1,3},{2,0},{3,1},{4,6},{5,7},{6,4},{7,5},{8,10},{9,11},{10,... | collective-permute-start | bytes 196616 | tf_op jit(solution)/shard_map/ppermute | solution.py:187
  12.5 4.4 %copy-start.3 = (bf16[128,1024]{1,0:T(8,128)(2,1)S(1)}, bf16[128,1024]{1,0:T(8,128)(2,1)}, u32[]{:S(2)}) copy-start(bf16[128,1024]{1,0:T(8,128)(2,1)} %q_hbm.1) | copy-start | bytes 786436
  12.6 4.3 %copy-start = (bf16[128,1024]{1,0:T(8,128)(2,1)S(1)}, bf16[128,1024]{1,0:T(8,128)(2,1)}, u32[]{:S(2)}) copy-start(bf16[128,1024]{1,0:T(8,128)(2,1)} %o_ref.3) | copy-start | bytes 786436
  12.6 6.7 %collective-permute-start.4 = (bf16[1,128,128]{2,1,0:T(8,128)(2,1)S(1)}, bf16[1,128,128]{2,1,0:T(8,128)(2,1)S(1)}, u32[]{:S(2)}, u32[]{:S(2)}) collective-permute-start(bf16[1,128,128]{2,1,0:T(8,128)(2,1)S(1)} %get-tuple-element.21), channel_id=1, source_target_pairs={{0,8},{1,9},{2,10},{3,11},{4,12},{5,13},{6,14},{7,15},{8,0},{9,1},... | collective-permute-start | bytes 98312 | tf_op jit(solution)/shard_map/ppermute | solution.py:195
  14.2 5.7 %collective-permute-start.6 = (bf16[1,128,128]{2,1,0:T(8,128)(2,1)S(1)}, bf16[1,128,128]{2,1,0:T(8,128)(2,1)S(1)}, u32[]{:S(2)}, u32[]{:S(2)}) collective-permute-start(bf16[1,128,128]{2,1,0:T(8,128)(2,1)S(1)} %get-tuple-element.22), channel_id=1, source_target_pairs={{0,24},{1,25},{2,26},{3,27},{4,28},{5,29},{6,30},{7,31},{8,16},{9,... | collective-permute-start | bytes 98312 | tf_op jit(solution)/shard_map/ppermute | solution.py:195
  16.7 5.2 %collective-permute-start.5 = (bf16[1,128,128]{2,1,0:T(8,128)(2,1)S(1)}, bf16[1,128,128]{2,1,0:T(8,128)(2,1)S(1)}, u32[]{:S(2)}, u32[]{:S(2)}) collective-permute-start(bf16[1,128,128]{2,1,0:T(8,128)(2,1)S(1)} %get-tuple-element.23), channel_id=1, source_target_pairs={{0,16},{1,17},{2,18},{3,19},{4,20},{5,21},{6,22},{7,23},{8,24},{9,... | collective-permute-start | bytes 98312 | tf_op jit(solution)/shard_map/ppermute | solution.py:195
  16.8 0.8 %copy-start.1 = (bf16[128,256]{1,0:T(8,128)(2,1)S(1)}, bf16[128,256]{1,0:T(8,128)(2,1)}, u32[]{:S(2)}) copy-start(bf16[128,256]{1,0:T(8,128)(2,1)} %k_ref.3) | copy-start | bytes 196612
  16.8 0.9 %copy-start.2 = (bf16[128,256]{1,0:T(8,128)(2,1)S(1)}, bf16[128,256]{1,0:T(8,128)(2,1)}, u32[]{:S(2)}) copy-start(bf16[128,256]{1,0:T(8,128)(2,1)} %v_ref.3) | copy-start | bytes 196612
  22.0 1.3 %collective-permute-start.7 = (bf16[2,1,128,128]{3,2,1,0:T(8,128)(2,1)S(1)}, bf16[2,1,128,128]{3,2,1,0:T(8,128)(2,1)S(1)}, u32[]{:S(2)}, u32[]{:S(2)}) collective-permute-start(bf16[2,1,128,128]{3,2,1,0:T(8,128)(2,1)S(1)} %pad_maximum_fusion.1), channel_id=1, source_target_pairs={{0,1},{1,0},{2,3},{3,2},{4,5},{5,4},{6,7},{7,6},{8,9},{9,8},{10,11... | collective-permute-start | bytes 196616 | tf_op jit(solution)/shard_map/ppermute | solution.py:203

commit v3 on v2

--- a/solution.py
+++ b/solution.py
@@ -11,8 +11,8 @@
 SEQ = "seq"
 HEAD = "head"
 DEVICES = (SEQ, HEAD)
-TOP_BITS = 2
-LOW_BITS = 2
+LOW_ORDER = (1, 2, 3)
+TOP_ORDER = (3, 2, 1)
 MIB = 1024 * 1024
 BF16 = jnp.bfloat16
 F32 = jnp.float32
@@ -63,11 +63,11 @@
     for copies in large:
         for copy in copies:
             copy.start()
-    core = lax.rem(lax.axis_index(HEAD), 2)
+    side = side_of(device_index(), lax.axis_size(SEQ) * lax.axis_size(HEAD))
     scale = row_scale(tokens, (tokens, HD), 0)
 
     def put(g, kind, state):
-        mine = core == g // half
+        mine = side == g // half
 
         @pl.when(mine)
         def _():
@@ -91,7 +91,8 @@
         put(g, 1, grad.astype(BF16))
 
 
-def local_kernel(q_ref, k_ref, v_ref, o_ref, qg_ref, kg_ref, vg_ref):
+def local_kernel(q_ref, k_ref, v_ref, o_ref, keep_ref, got_ref, qg_ref, kg_ref, vg_ref, total_ref):
+    total_ref[...] = keep_ref[...].astype(F32) + got_ref[...].astype(F32)
     tokens = q_ref.shape[0]
     kv = k_ref.shape[1] // HD
     group = q_ref.shape[1] // HD // kv
@@ -129,9 +130,9 @@
     width = o_ref.shape[1] // kv
     group = width // HD
     half = kv // 2
-    core = lax.rem(lax.axis_index(HEAD), 2)
-    carried[core] = mine_ref[...]
-    carried[1 - core] = other_ref[...]
+    side = side_of(device_index(), lax.axis_size(SEQ) * lax.axis_size(HEAD))
+    carried[side] = mine_ref[...]
+    carried[1 - side] = other_ref[...]
     scale = row_scale(tokens, (tokens, HD), 0)
     copies = []
     for g in range(kv):
@@ -156,51 +157,77 @@
         copy.wait()
 
 
-def bit_groups(size):
+def digits(size):
     bits = size.bit_length() - 1
     assert 1 << bits == size
-    low = list(range(1, max(1, bits - TOP_BITS)))
-    groups = [low[i : i + LOW_BITS] for i in range(0, len(low), LOW_BITS)]
-    return groups + [list(range(max(1, bits - TOP_BITS), bits))]
-
-
-def flips_of(group):
-    masks = [0]
-    for bit in group:
-        masks += [mask | 1 << bit for mask in masks]
-    return masks[1:]
-
-
-def carry_states(keep, send):
+    return [(low, min(2, bits - low)) for low in range(1, bits, 2)]
+
+
+def side_mask(size):
+    places = digits(size)
+    mask = 1 | 1 << places[-1][0]
+    for low, width in places[:-1]:
+        mask |= ((1 << width) - 1) << low
+    return mask
+
+
+def side_of(index, size):
+    mask = side_mask(size)
+    side = index & 1
+    for bit in range(1, size.bit_length()):
+        if mask >> bit & 1:
+            side = side ^ (index >> bit & 1)
+    return side
+
+
+def moved(index, size, place, step, last):
+    low, width = place
+    base = (1 << width) - 1
+    digit = index >> low & base
+    new = (digit + step & base) if last else digit ^ step
+    other = index ^ (digit ^ new) << low
+    return other ^ side_of(other, size) ^ side_of(index, size)
+
+
+def carry_states(keep, send, local_terms):
     size = lax.axis_size(SEQ) * lax.axis_size(HEAD)
     index = device_index()
     swap = [(i, i ^ 1) for i in range(size)]
-    got = lax.ppermute(send, DEVICES, swap).astype(F32)
+    got = lax.ppermute(send, DEVICES, swap)
+    *local, total = local_terms(keep, got)
     keep = keep.astype(F32)
-    total = keep + got
+    got = got.astype(F32)
+    message = (keep + got).astype(BF16)
     earlier = jnp.zeros_like(total[0])
     later = jnp.zeros_like(total[1])
-    groups = bit_groups(size)
-    for group in groups[:-1]:
-        message = total.astype(BF16)
-        for flip in flips_of(group):
-            arrived = lax.ppermute(message, DEVICES, [(i, i ^ flip) for i in range(size)]).astype(F32)
-            lower = index < (index ^ flip)
+    places = digits(size)
+    for place in places[:-1]:
+        for step in [step for step in LOW_ORDER if step < 1 << place[1]]:
+            arrived = lax.ppermute(
+                message, DEVICES, [(i, moved(i, size, place, step, False)) for i in range(size)]
+            ).astype(F32)
+            lower = index < (index ^ step << place[0])
             earlier = earlier + jnp.where(lower, 0.0, arrived[0])
             later = later + jnp.where(lower, arrived[1], 0.0)
             total = total + arrived
-    message = total.astype(BF16)
-    for flip in flips_of(groups[-1]):
-        lower = index < (index ^ flip)
+        message = total.astype(BF16)
+    place = places[-1]
+    count = 1 << place[1]
+    digit = index >> place[0] & count - 1
+    steps = [step for step in TOP_ORDER if step < count]
+    messages = [jnp.where(digit + step < count, message[0], message[1]) for step in steps]
+    messages = lax.optimization_barrier(tuple(messages))
+    for step, message in zip(steps, messages):
         arrived = lax.ppermute(
-            jnp.where(lower, message[0], message[1]), DEVICES, [(i, i ^ flip) for i in range(size)]
+            message, DEVICES, [(i, moved(i, size, place, step, True)) for i in range(size)]
         ).astype(F32)
-        earlier = earlier + jnp.where(lower, 0.0, arrived)
-        later = later + jnp.where(lower, arrived, 0.0)
-    first = index % 2 == 0
+        before = digit >= step
+        earlier = earlier + jnp.where(before, arrived, 0.0)
+        later = later + jnp.where(before, 0.0, arrived)
+    first = index & 1 == 0
     mine = jnp.stack([earlier + jnp.where(first, 0.0, got[0]), later + jnp.where(first, got[1], 0.0)])
     theirs = jnp.stack([earlier + jnp.where(first, keep[0], 0.0), later + jnp.where(first, 0.0, keep[1])])
-    return mine.astype(BF16), lax.ppermute(theirs.astype(BF16), DEVICES, swap)
+    return local, mine.astype(BF16), lax.ppermute(theirs.astype(BF16), DEVICES, swap)
 
 
 def body(queries, keys, values, out_grad):
@@ -218,17 +245,17 @@
         scratch_shapes=[pltpu.VMEM(x.shape, BF16) for x in inputs] + [pltpu.SemaphoreType.DMA((2, kv + 1))],
         compiler_params=pltpu.CompilerParams(vmem_limit_bytes=55104 * 1024),
     )(*inputs)
-    local = pl.pallas_call(
+    local_terms = pl.pallas_call(
         local_kernel,
-        out_shape=tuple(jax.ShapeDtypeStruct(x.shape, F32) for x in (queries, keys, values)),
-        in_specs=[vmem] * 4,
-        out_specs=[vmem] * 3,
+        out_shape=tuple(jax.ShapeDtypeStruct(x.shape, F32) for x in (queries, keys, values, keep)),
+        in_specs=[vmem] * 6,
+        out_specs=[vmem] * 4,
         cost_estimate=pl.CostEstimate(
             flops=12 * tokens * tokens * wide, bytes_accessed=12 * tokens * wide, transcendentals=0
         ),
         compiler_params=pltpu.CompilerParams(vmem_limit_bytes=24 * MIB),
-    )(*inputs)
-    mine, other = carry_states(keep, send)
+    )
+    local, mine, other = carry_states(keep, send, functools.partial(local_terms, *inputs))
     return pl.pallas_call(
         finish_kernel,
         out_shape=tuple(jax.ShapeDtypeStruct(x.shape, BF16) for x in (queries, keys, values)),

time: 24.5 us -> 22.1 us (0.902)
  waiting for transfers between devices: 8.75 us -> 6.5 us
  local copies, waits for them, and re-layouts: 0.83 us -> 0.02 us
  starting transfers between devices: 9.32 us -> 9.99 us
    ppermute x8, waiting for transfers between devices: 8.75 us -> 6.5 us  [the longest x3 2.39 us: carry_states(): lax.ppermute(message, DEVICES, [(i, moved(i, size, place, step, False)) f...]
    unnamed x8, local copies, waits for them, and re-layouts: 0.83 us -> 0.02 us
    ppermute x8, starting transfers between devices: 9.32 us -> 9.99 us  [the longest x3 5.04 us: carry_states(): lax.ppermute(message, DEVICES, [(i, moved(i, size, place, step, True)) fo...]
  transfers between devices with their start and end apart: 8 -> 8, of which waited for: 7 -> 6; matrix products, arithmetic and copies ran while one was open for 0% -> 0% of each run, Pallas kernels for 6% -> 7%
where the time goes in v3:
time: 22.1 us; the launch traced here: 22 us
  starting transfers between devices  9.99 us (45%)
  waiting for transfers between devices  6.5 us (29%)
  Pallas kernels  4.44 us (20%)
  between operations  0.76 us (3%)
  other arithmetic  0.25 us (1%)
    ppermute x3, starting transfers between devices, carry_states(): lax.ppermute(message, DEVICES, [(i, moved(i, size, place, step, True)) fo...  5.04 us
    ppermute x3, starting transfers between devices, carry_states(): lax.ppermute(message, DEVICES, [(i, moved(i, size, place, step, False)) f...  4.22 us
    ppermute x3, waiting for transfers between devices, carry_states(): lax.ppermute(message, DEVICES, [(i, moved(i, size, place, step, False)) f...  2.39 us
    ppermute x3, waiting for transfers between devices, carry_states(): lax.ppermute(message, DEVICES, [(i, moved(i, size, place, step, True)) fo...  2.14 us
    pallas_call x1, Pallas kernels, body(): pl.pallas_call(states_kernel, out_shape=(jax.ShapeDtypeStruct(shape, BF16...  1.85 us
    pallas_call x1, Pallas kernels, carry_states(): *local, total = local_terms(keep, got)  1.57 us
    ppermute x1, waiting for transfers between devices, carry_states(): lax.ppermute(theirs.astype(BF16), DEVICES, swap)  1.06 us
    pallas_call x1, Pallas kernels, body(): pl.pallas_call(finish_kernel, out_shape=tuple((jax.ShapeDtypeStruct(x.sha...  1.02 us
  transfers between devices with their start and end apart: 8, of which 6 were waited for; matrix products, arithmetic and copies ran while one was open for 0% of the time, Pallas kernels for 7%

profile of v3, /device:TPU:0, one launch (start us, length us, event | category | flops | bytes accessed | tf_op | source)
XLA Modules:
  0.0 22.0 jit_solution(15625382263614712655)
XLA Ops:
  0.6 0.0 copy-start
  0.6 0.0 copy-start.1
  0.6 1.8 %shard_map.67 = (bf16[2,1,128,128]{3,2,1,0:T(8,128)(2,1)S(1)}, bf16[2,1,128,128]{3,2,1,0:T(8,128)(2,1)S(1)}) custom-call(bf16[128,1024]{1,0:T(8,128)(2,1)} %q_ref.1, bf16[128,256]{1,0:T(8,128)(2,1)} %k_ref.3, bf16[128,256]{1,0:T(8,128)(2,1)} %v_ref.3, bf16[128,1024]{1,0:T(8,128)(2,1)} %o_ref.3), custom_call_target="tpu_custom_call" | custom-call | tf_op jit(solution)/shard_map/pallas_call | solution.py:240
  2.5 0.5 %collective-permute-start = (bf16[2,1,128,128]{3,2,1,0:T(8,128)(2,1)S(1)}, bf16[2,1,128,128]{3,2,1,0:T(8,128)(2,1)S(1)}, u32[]{:S(2)}, u32[]{:S(2)}) collective-permute-start(bf16[2,1,128,128]{3,2,1,0:T(8,128)(2,1)S(1)} %get-tuple-element.13), channel_id=1, source_target_pairs={{0,1},{1,0},{2,3},{3,2},{4,5},{5,4},{6,7},{7,6},{8,9},{9,8},{10,11... | collective-permute-start | bytes 196616 | tf_op jit(solution)/shard_map/ppermute | solution.py:196
  3.0 0.9 %collective-permute-done.got_ref = bf16[2,1,128,128]{3,2,1,0:T(8,128)(2,1)S(1)} collective-permute-done((bf16[2,1,128,128]{3,2,1,0:T(8,128)(2,1)S(1)}, bf16[2,1,128,128]{3,2,1,0:T(8,128)(2,1)S(1)}, u32[]{:S(2)}, u32[]{:S(2)}) %collective-permute-start) | collective-permute-done | bytes 65568 | tf_op jit(solution)/shard_map/ppermute | solution.py:196
  3.9 0.0 copy-start.2
  3.9 0.0 copy-start.3
  4.0 3.9 %collective-permute-start.3 = (bf16[2,1,128,128]{3,2,1,0:T(8,128)(2,1)S(1)}, bf16[2,1,128,128]{3,2,1,0:T(8,128)(2,1)S(1)}, u32[]{:S(2)}, u32[]{:S(2)}) collective-permute-start(bf16[2,1,128,128]{3,2,1,0:T(8,128)(2,1)S(1)} %add_convert_fusion.1), channel_id=1, source_target_pairs={{0,6},{1,7},{2,4},{3,5},{4,2},{5,3},{6,0},{7,1},{8,14},{9,15},{10,... | collective-permute-start | bytes 196616 | tf_op jit(solution)/shard_map/ppermute | solution.py:206
  7.8 0.0 collective-permute-start.2
  7.8 0.4 %collective-permute-start.1 = (bf16[2,1,128,128]{3,2,1,0:T(8,128)(2,1)S(1)}, bf16[2,1,128,128]{3,2,1,0:T(8,128)(2,1)S(1)}, u32[]{:S(2)}, u32[]{:S(2)}) collective-permute-start(bf16[2,1,128,128]{3,2,1,0:T(8,128)(2,1)S(1)} %add_convert_fusion.1), channel_id=1, source_target_pairs={{0,3},{1,2},{2,1},{3,0},{4,7},{5,6},{6,5},{7,4},{8,11},{9,10},{10,... | collective-permute-start | bytes 196616 | tf_op jit(solution)/shard_map/ppermute | solution.py:206
  8.2 0.0 copy-done
  8.2 0.0 copy-done.1
  8.2 0.0 copy-done.2
  8.2 0.0 copy-done.3
  8.2 1.6 %shard_map.68 = (f32[128,1024]{1,0:T(8,128)S(1)}, f32[128,256]{1,0:T(8,128)S(1)}, f32[128,256]{1,0:T(8,128)S(1)}, f32[2,1,128,128]{3,2,1,0:T(8,128)S(1)}) custom-call(bf16[128,1024]{1,0:T(8,128)(2,1)S(1)} %copy-done.1, bf16[128,256]{1,0:T(8,128)(2,1)S(1)} %copy-done.2, bf16[128,256]{1,0:T(8,128)(2,1)S(1)} %copy-done.3, bf16[128,1024]{1,0:T(8,128)(2,1)S(1)} %copy-done, ...), custom_call_target="tpu_custom_call" | custom-call | flops 201326592 | bytes 1572864 | tf_op jit(solution)/shard_map/pallas_call | solution.py:197
  9.8 0.5 %collective-permute-done.3 = bf16[2,1,128,128]{3,2,1,0:T(8,128)(2,1)S(1)} collective-permute-done((bf16[2,1,128,128]{3,2,1,0:T(8,128)(2,1)S(1)}, bf16[2,1,128,128]{3,2,1,0:T(8,128)(2,1)S(1)}, u32[]{:S(2)}, u32[]{:S(2)}) %collective-permute-start.3) | collective-permute-done | bytes 65568 | tf_op jit(solution)/shard_map/ppermute | solution.py:206
  10.3 1.8 %collective-permute-done.2 = bf16[2,1,128,128]{3,2,1,0:T(8,128)(2,1)S(1)} collective-permute-done((bf16[2,1,128,128]{3,2,1,0:T(8,128)(2,1)S(1)}, bf16[2,1,128,128]{3,2,1,0:T(8,128)(2,1)S(1)}, u32[]{:S(2)}, u32[]{:S(2)}) %collective-permute-start.2) | collective-permute-done | bytes 65568 | tf_op jit(solution)/shard_map/ppermute | solution.py:206
  12.1 0.0 collective-permute-done.1
  12.2 1.3 %collective-permute-start.6 = (bf16[1,128,128]{2,1,0:T(8,128)(2,1)S(1)}, bf16[1,128,128]{2,1,0:T(8,128)(2,1)S(1)}, u32[]{:S(2)}, u32[]{:S(2)}) collective-permute-start(bf16[1,128,128]{2,1,0:T(8,128)(2,1)S(1)} %get-tuple-element.20), channel_id=1, source_target_pairs={{0,9},{1,8},{2,11},{3,10},{4,13},{5,12},{6,15},{7,14},{8,17},{9,16... | collective-permute-start | bytes 98312 | tf_op jit(solution)/shard_map/ppermute | solution.py:221
  13.6 2.6 %collective-permute-start.5 = (bf16[1,128,128]{2,1,0:T(8,128)(2,1)S(1)}, bf16[1,128,128]{2,1,0:T(8,128)(2,1)S(1)}, u32[]{:S(2)}, u32[]{:S(2)}) collective-permute-start(bf16[1,128,128]{2,1,0:T(8,128)(2,1)S(1)} %get-tuple-element.19), channel_id=1, source_target_pairs={{0,16},{1,17},{2,18},{3,19},{4,20},{5,21},{6,22},{7,23},{8,24},{9,... | collective-permute-start | bytes 98312 | tf_op jit(solution)/shard_map/ppermute | solution.py:221
  16.2 1.1 %collective-permute-start.4 = (bf16[1,128,128]{2,1,0:T(8,128)(2,1)S(1)}, bf16[1,128,128]{2,1,0:T(8,128)(2,1)S(1)}, u32[]{:S(2)}, u32[]{:S(2)}) collective-permute-start(bf16[1,128,128]{2,1,0:T(8,128)(2,1)S(1)} %get-tuple-element.18), channel_id=1, source_target_pairs={{0,25},{1,24},{2,27},{3,26},{4,29},{5,28},{6,31},{7,30},{8,1},{9,0... | collective-permute-start | bytes 98312 | tf_op jit(solution)/shard_map/ppermute | solution.py:221
  17.4 0.0 collective-permute-done.6
  17.4 1.1 %collective-permute-done.5 = bf16[1,128,128]{2,1,0:T(8,128)(2,1)S(1)} collective-permute-done((bf16[1,128,128]{2,1,0:T(8,128)(2,1)S(1)}, bf16[1,128,128]{2,1,0:T(8,128)(2,1)S(1)}, u32[]{:S(2)}, u32[]{:S(2)}) %collective-permute-start.5) | collective-permute-done | bytes 32800 | tf_op jit(solution)/shard_map/ppermute | solution.py:221
  18.5 1.0 %collective-permute-done.4 = bf16[1,128,128]{2,1,0:T(8,128)(2,1)S(1)} collective-permute-done((bf16[1,128,128]{2,1,0:T(8,128)(2,1)S(1)}, bf16[1,128,128]{2,1,0:T(8,128)(2,1)S(1)}, u32[]{:S(2)}, u32[]{:S(2)}) %collective-permute-start.4) | collective-permute-done | bytes 32800 | tf_op jit(solution)/shard_map/ppermute | solution.py:221
  19.5 0.1 fusion.26
  19.6 0.2 collective-permute-start.7
  19.9 1.1 %collective-permute-done.7.other_ref = bf16[2,1,128,128]{3,2,1,0:T(8,128)(2,1)S(1)} collective-permute-done((bf16[2,1,128,128]{3,2,1,0:T(8,128)(2,1)S(1)}, bf16[2,1,128,128]{3,2,1,0:T(8,128)(2,1)S(1)}, u32[]{:S(2)}, u32[]{:S(2)}) %collective-permute-start.7) | collective-permute-done | bytes 65568 | tf_op jit(solution)/shard_map/ppermute | solution.py:230
  20.9 1.0 %shard_map.69 = (bf16[128,1024]{1,0:T(8,128)(2,1)}, bf16[128,256]{1,0:T(8,128)(2,1)}, bf16[128,256]{1,0:T(8,128)(2,1)}) custom-call(bf16[128,256]{1,0:T(8,128)(2,1)S(1)} %copy-done.2, bf16[128,256]{1,0:T(8,128)(2,1)S(1)} %copy-done.3, bf16[128,1024]{1,0:T(8,128)(2,1)S(1)} %copy-done, f32[128,1024]{1,0:T(8,128)S(1)} %get-tuple-element.14.ql_ref, ...), custom_call_target="tpu_custom_call" | custom-call | tf_op jit(solution)/shard_map/pallas_call | solution.py:259
  (11 shorter events, 0.2 us)
Async XLA Ops:
  0.6 7.5 %copy-start = (bf16[128,1024]{1,0:T(8,128)(2,1)S(1)}, bf16[128,1024]{1,0:T(8,128)(2,1)}, u32[]{:S(2)}) copy-start(bf16[128,1024]{1,0:T(8,128)(2,1)} %o_ref.3) | copy-start | bytes 786436
  0.6 7.5 %copy-start.1 = (bf16[128,1024]{1,0:T(8,128)(2,1)S(1)}, bf16[128,1024]{1,0:T(8,128)(2,1)}, u32[]{:S(2)}) copy-start(bf16[128,1024]{1,0:T(8,128)(2,1)} %q_ref.1) | copy-start | bytes 786436
  2.5 1.4 %collective-permute-start = (bf16[2,1,128,128]{3,2,1,0:T(8,128)(2,1)S(1)}, bf16[2,1,128,128]{3,2,1,0:T(8,128)(2,1)S(1)}, u32[]{:S(2)}, u32[]{:S(2)}) collective-permute-start(bf16[2,1,128,128]{3,2,1,0:T(8,128)(2,1)S(1)} %get-tuple-element.13), channel_id=1, source_target_pairs={{0,1},{1,0},{2,3},{3,2},{4,5},{5,4},{6,7},{7,6},{8,9},{9,8},{10,11... | collective-permute-start | bytes 196616 | tf_op jit(solution)/shard_map/ppermute | solution.py:196
  3.9 4.3 %copy-start.2 = (bf16[128,256]{1,0:T(8,128)(2,1)S(1)}, bf16[128,256]{1,0:T(8,128)(2,1)}, u32[]{:S(2)}) copy-start(bf16[128,256]{1,0:T(8,128)(2,1)} %k_ref.3) | copy-start | bytes 196612
  3.9 4.3 %copy-start.3 = (bf16[128,256]{1,0:T(8,128)(2,1)S(1)}, bf16[128,256]{1,0:T(8,128)(2,1)}, u32[]{:S(2)}) copy-start(bf16[128,256]{1,0:T(8,128)(2,1)} %v_ref.3) | copy-start | bytes 196612
  4.0 6.3 %collective-permute-start.3 = (bf16[2,1,128,128]{3,2,1,0:T(8,128)(2,1)S(1)}, bf16[2,1,128,128]{3,2,1,0:T(8,128)(2,1)S(1)}, u32[]{:S(2)}, u32[]{:S(2)}) collective-permute-start(bf16[2,1,128,128]{3,2,1,0:T(8,128)(2,1)S(1)} %add_convert_fusion.1), channel_id=1, source_target_pairs={{0,6},{1,7},{2,4},{3,5},{4,2},{5,3},{6,0},{7,1},{8,14},{9,15},{10,... | collective-permute-start | bytes 196616 | tf_op jit(solution)/shard_map/ppermute | solution.py:206
  7.8 4.3 %collective-permute-start.2 = (bf16[2,1,128,128]{3,2,1,0:T(8,128)(2,1)S(1)}, bf16[2,1,128,128]{3,2,1,0:T(8,128)(2,1)S(1)}, u32[]{:S(2)}, u32[]{:S(2)}) collective-permute-start(bf16[2,1,128,128]{3,2,1,0:T(8,128)(2,1)S(1)} %add_convert_fusion.1), channel_id=1, source_target_pairs={{0,5},{1,4},{2,7},{3,6},{4,1},{5,0},{6,3},{7,2},{8,13},{9,12},{10,... | collective-permute-start | bytes 196616 | tf_op jit(solution)/shard_map/ppermute | solution.py:206
  7.8 4.3 %collective-permute-start.1 = (bf16[2,1,128,128]{3,2,1,0:T(8,128)(2,1)S(1)}, bf16[2,1,128,128]{3,2,1,0:T(8,128)(2,1)S(1)}, u32[]{:S(2)}, u32[]{:S(2)}) collective-permute-start(bf16[2,1,128,128]{3,2,1,0:T(8,128)(2,1)S(1)} %add_convert_fusion.1), channel_id=1, source_target_pairs={{0,3},{1,2},{2,1},{3,0},{4,7},{5,6},{6,5},{7,4},{8,11},{9,10},{10,... | collective-permute-start | bytes 196616 | tf_op jit(solution)/shard_map/ppermute | solution.py:206
  12.2 5.2 %collective-permute-start.6 = (bf16[1,128,128]{2,1,0:T(8,128)(2,1)S(1)}, bf16[1,128,128]{2,1,0:T(8,128)(2,1)S(1)}, u32[]{:S(2)}, u32[]{:S(2)}) collective-permute-start(bf16[1,128,128]{2,1,0:T(8,128)(2,1)S(1)} %get-tuple-element.20), channel_id=1, source_target_pairs={{0,9},{1,8},{2,11},{3,10},{4,13},{5,12},{6,15},{7,14},{8,17},{9,16... | collective-permute-start | bytes 98312 | tf_op jit(solution)/shard_map/ppermute | solution.py:221
  13.6 4.9 %collective-permute-start.5 = (bf16[1,128,128]{2,1,0:T(8,128)(2,1)S(1)}, bf16[1,128,128]{2,1,0:T(8,128)(2,1)S(1)}, u32[]{:S(2)}, u32[]{:S(2)}) collective-permute-start(bf16[1,128,128]{2,1,0:T(8,128)(2,1)S(1)} %get-tuple-element.19), channel_id=1, source_target_pairs={{0,16},{1,17},{2,18},{3,19},{4,20},{5,21},{6,22},{7,23},{8,24},{9,... | collective-permute-start | bytes 98312 | tf_op jit(solution)/shard_map/ppermute | solution.py:221
  16.2 3.4 %collective-permute-start.4 = (bf16[1,128,128]{2,1,0:T(8,128)(2,1)S(1)}, bf16[1,128,128]{2,1,0:T(8,128)(2,1)S(1)}, u32[]{:S(2)}, u32[]{:S(2)}) collective-permute-start(bf16[1,128,128]{2,1,0:T(8,128)(2,1)S(1)} %get-tuple-element.18), channel_id=1, source_target_pairs={{0,25},{1,24},{2,27},{3,26},{4,29},{5,28},{6,31},{7,30},{8,1},{9,0... | collective-permute-start | bytes 98312 | tf_op jit(solution)/shard_map/ppermute | solution.py:221
  19.6 1.3 %collective-permute-start.7 = (bf16[2,1,128,128]{3,2,1,0:T(8,128)(2,1)S(1)}, bf16[2,1,128,128]{3,2,1,0:T(8,128)(2,1)S(1)}, u32[]{:S(2)}, u32[]{:S(2)}) collective-permute-start(bf16[2,1,128,128]{3,2,1,0:T(8,128)(2,1)S(1)} %pad_maximum_fusion.1), channel_id=1, source_target_pairs={{0,1},{1,0},{2,3},{3,2},{4,5},{5,4},{6,7},{7,6},{8,9},{9,8},{10,11... | collective-permute-start | bytes 196616 | tf_op jit(solution)/shard_map/ppermute | solution.py:230

commit v4 on v3

v4 whole, which is shorter than its diff:
```python
import functools

import jax
import jax.numpy as jnp
from jax import lax
from jax.experimental import pallas as pl
from jax.experimental.pallas import tpu as pltpu
from jax.sharding import PartitionSpec as P

HD = 128
SEQ = "seq"
HEAD = "head"
DEVICES = (SEQ, HEAD)
LOW_MOVES = ((1, 0, 3, 2), (2, 3, 0, 1), (3, 2, 1, 0))
TOP_MOVES = ((3, 0, 1, 2), (2, 3, 0, 1), (1, 2, 3, 0))
LOW_ODD = (0, 1, 1, 0)
TOP_ODD = (0, 1, 0, 1)
MIB = 1024 * 1024
BF16 = jnp.bfloat16
F32 = jnp.float32

NN = (((1,), (0,)), ((), ()))
NT = (((1,), (1,)), ((), ()))
TN = (((0,), (0,)), ((), ()))


def dot(left, right, dims):
    return lax.dot_general(left, right, dims, preferred_element_type=F32)


def columns(index):
    return (slice(None), slice(index * HD, (index + 1) * HD))


def device_index():
    return lax.axis_index(SEQ) * lax.axis_size(HEAD) + lax.axis_index(HEAD)


def row_scale(tokens, shape, axis):
    positions = device_index() * tokens + lax.broadcasted_iota(jnp.int32, shape, axis)
    return 1.0 / jnp.sqrt((HD * (positions + 1)).astype(F32))


def states_kernel(q_hbm, k_hbm, v_hbm, o_hbm, keep_ref, send_ref, q_ref, k_ref, v_ref, o_ref, sems):
    tokens = q_hbm.shape[0]
    kv = k_hbm.shape[1] // HD
    group = q_hbm.shape[1] // HD // kv
    half = kv // 2
    arrivals = [
        pltpu.make_async_copy(source, place, sems.at[i])
        for i, (source, place) in enumerate([(k_hbm, k_ref), (v_hbm, v_ref), (o_hbm, o_ref), (q_hbm, q_ref)])
    ]
    for copy in arrivals:
        copy.start(priority=1)
    side = side_of(device_index(), lax.axis_size(SEQ) * lax.axis_size(HEAD))
    scale = row_scale(tokens, (tokens, HD), 0)

    def put(g, kind, state):
        mine = side == g // half

        @pl.when(mine)
        def _():
            keep_ref[kind, g % half] = state

        @pl.when(jnp.logical_not(mine))
        def _():
            send_ref[kind, g % half] = state

    arrivals[0].wait()
    arrivals[1].wait()
    for g in range(kv):
        put(g, 0, dot(v_ref[columns(g)], k_ref[columns(g)], TN).astype(BF16))
    arrivals[2].wait()
    scaled = [(scale * o_ref[columns(h)].astype(F32)).astype(BF16) for h in range(kv * group)]
    arrivals[3].wait()
    for g in range(kv):
        grad = jnp.zeros((HD, HD), F32)
        for h in range(g * group, (g + 1) * group):
            grad = grad + dot(scaled[h], q_ref[columns(h)], TN)
        put(g, 1, grad.astype(BF16))


def local_kernel(q_ref, k_ref, v_ref, o_ref, keep_ref, got_ref, qg_ref, kg_ref, vg_ref, total_ref):
    total_ref[...] = keep_ref[...].astype(F32) + got_ref[...].astype(F32)
    tokens = q_ref.shape[0]
    kv = k_ref.shape[1] // HD
    group = q_ref.shape[1] // HD // kv
    scale = row_scale(tokens, (tokens, HD), 0)
    scale_row = row_scale(tokens, (HD, tokens), 1)
    rows = lax.broadcasted_iota(jnp.int32, (tokens, tokens), 0)
    cols = lax.broadcasted_iota(jnp.int32, (tokens, tokens), 1)
    causal = rows >= cols
    causal_t = rows <= cols
    for g in range(kv):
        key = k_ref[columns(g)]
        value = v_ref[columns(g)]
        key_grad = jnp.zeros((tokens, HD), F32)
        value_grad = jnp.zeros((tokens, HD), F32)
        for h in range(g * group, (g + 1) * group):
            query = q_ref[columns(h)]
            cot = o_ref[columns(h)]
            scaled = (scale * cot.astype(F32)).astype(BF16)
            backward = jnp.where(causal, dot(scaled, value, NT), 0.0).astype(BF16)
            backward_t = jnp.where(causal_t, dot(value, scaled, NT), 0.0).astype(BF16)
            forward_t = jnp.where(causal_t, scale_row * dot(key, query, NT), 0.0).astype(BF16)
            qg_ref[columns(h)] = dot(backward, key, NN)
            key_grad = key_grad + dot(backward_t, query, NN)
            value_grad = value_grad + dot(forward_t, cot, NN)
        kg_ref[columns(g)] = key_grad
        vg_ref[columns(g)] = value_grad


def finish_kernel(mine, k_ref, v_ref, o_ref, ql_ref, kl_ref, vl_ref, state_ref, *refs):
    qg_hbm, kg_hbm, vg_hbm, qg_ref, kg_ref, vg_ref, sems = refs[-7:]
    tokens = o_ref.shape[0]
    kv = k_ref.shape[1] // HD
    width = o_ref.shape[1] // kv
    group = width // HD
    half = kv // 2
    side = side_of(device_index(), lax.axis_size(SEQ) * lax.axis_size(HEAD))
    scale = row_scale(tokens, (tokens, HD), 0)

    def finish(part):
        copies = []

        def send(ref, hbm, size):
            at = (slice(None), slice(part * half * size, (part + 1) * half * size))
            copies.append(pltpu.make_async_copy(ref.at[at], hbm.at[at], sems.at[len(copies)]))
            copies[-1].start()

        for g in range(part * half, (part + 1) * half):
            prior = state_ref[0, g % half]
            for h in range(g * group, (g + 1) * group):
                scaled = (scale * o_ref[columns(h)].astype(F32)).astype(BF16)
                qg_ref[columns(h)] = (ql_ref[columns(h)] + dot(scaled, prior, NN)).astype(BF16)
        send(qg_ref, qg_hbm, width)
        for g in range(part * half, (part + 1) * half):
            future = state_ref[1, g % half]
            key_grad = kl_ref[columns(g)] + dot(v_ref[columns(g)], future, NN)
            value_grad = vl_ref[columns(g)] + dot(k_ref[columns(g)], future, NT)
            kg_ref[columns(g)] = key_grad.astype(BF16)
            vg_ref[columns(g)] = value_grad.astype(BF16)
        send(kg_ref, kg_hbm, HD)
        send(vg_ref, vg_hbm, HD)
        for copy in copies:
            copy.wait()

    for part in range(2):
        pl.when(side == (part if mine else 1 - part))(functools.partial(finish, part))


def digits(size):
    bits = size.bit_length() - 1
    assert 1 << bits == size
    return [(low, min(2, bits - low)) for low in range(1, bits, 2)]


def tables(size):
    found = []
    for low, width in digits(size):
        moves, odd = (LOW_MOVES, LOW_ODD) if low + width < size.bit_length() - 1 else (TOP_MOVES, TOP_ODD)
        found.append((low, moves, odd) if width == 2 else (low, ((1, 0),), (0, 1)))
    return found


def side_of(index, size):
    side = index & 1
    for low, moves, odd in tables(size):
        digit = index >> low & len(odd) - 1
        for place in range(len(odd)):
            if odd[place]:
                side = side ^ (digit == place)
    return side


def target(index, size, low, move):
    digit = index >> low & len(move) - 1
    other = index ^ (digit ^ move[digit]) << low
    return other ^ side_of(other, size) ^ side_of(index, size)


def place_among(digit, places):
    return sum(jnp.where(digit == place, other, 0) for place, other in enumerate(places))


def carry_states(keep, send, local_terms):
    size = lax.axis_size(SEQ) * lax.axis_size(HEAD)
    index = device_index()
    swap = [(i, i ^ 1) for i in range(size)]
    got = lax.ppermute(send, DEVICES, swap)
    *local, total = local_terms(keep, got)
    keep = keep.astype(F32)
    got = got.astype(F32)
    message = (keep + got).astype(BF16)
    earlier = jnp.zeros_like(total[0])
    later = jnp.zeros_like(total[1])
    *low_rounds, top_round = tables(size)
    for low, moves, _ in low_rounds:
        digit = index >> low & len(moves)
        for move in moves:
            arrived = lax.ppermute(
                message, DEVICES, [(i, target(i, size, low, move)) for i in range(size)]
            ).astype(F32)
            before = place_among(digit, [move.index(place) for place in range(len(move))]) < digit
            earlier = earlier + jnp.where(before, arrived[0], 0.0)
            later = later + jnp.where(before, 0.0, arrived[1])
            total = total + arrived
        message = total.astype(BF16)
    low, moves, _ = top_round
    digit = index >> low & len(moves)
    messages = [jnp.where(place_among(digit, move) > digit, message[0], message[1]) for move in moves]
    messages = lax.optimization_barrier(tuple(messages))
    for move, message in zip(moves, messages):
        arrived = lax.ppermute(
            message, DEVICES, [(i, target(i, size, low, move)) for i in range(size)]
        ).astype(F32)
        before = place_among(digit, [move.index(place) for place in range(len(move))]) < digit
        earlier = earlier + jnp.where(before, arrived, 0.0)
        later = later + jnp.where(before, 0.0, arrived)
    first = index & 1 == 0
    mine = jnp.stack([earlier + jnp.where(first, 0.0, got[0]), later + jnp.where(first, got[1], 0.0)])
    theirs = jnp.stack([earlier + jnp.where(first, keep[0], 0.0), later + jnp.where(first, 0.0, keep[1])])
    return local, mine.astype(BF16), lax.ppermute(theirs.astype(BF16), DEVICES, swap)


def body(queries, keys, values, out_grad):
    kv = keys.shape[1] // HD
    shape = (2, kv // 2, HD, HD)
    vmem = pl.BlockSpec(memory_space=pltpu.VMEM)
    anywhere = pl.BlockSpec(memory_space=pltpu.HBM)
    inputs = (queries, keys, values, out_grad)
    tokens, wide, narrow = queries.shape[0], queries.shape[1], keys.shape[1]
    keep, send = pl.pallas_call(
        states_kernel,
        out_shape=(jax.ShapeDtypeStruct(shape, BF16),) * 2,
        in_specs=[anywhere] * 4,
        out_specs=[vmem] * 2,
        scratch_shapes=[pltpu.VMEM(x.shape, BF16) for x in inputs] + [pltpu.SemaphoreType.DMA((4,))],
        compiler_params=pltpu.CompilerParams(vmem_limit_bytes=55104 * 1024),
    )(*inputs)
    local_terms = pl.pallas_call(
        local_kernel,
        out_shape=tuple(jax.ShapeDtypeStruct(x.shape, F32) for x in (queries, keys, values, keep)),
        in_specs=[vmem] * 6,
        out_specs=[vmem] * 4,
        cost_estimate=pl.CostEstimate(
            flops=12 * tokens * tokens * wide, bytes_accessed=12 * tokens * wide, transcendentals=0
        ),
        compiler_params=pltpu.CompilerParams(vmem_limit_bytes=24 * MIB),
    )
    local, mine, other = carry_states(keep, send, functools.partial(local_terms, *inputs))

    def finish(mine, state, *written):
        return pl.pallas_call(
            functools.partial(finish_kernel, mine),
            out_shape=tuple(jax.ShapeDtypeStruct(x.shape, BF16) for x in (queries, keys, values)),
            in_specs=[vmem] * 7 + [anywhere] * len(written),
            out_specs=[anywhere] * 3,
            scratch_shapes=[pltpu.VMEM(x.shape, BF16) for x in (queries, keys, values)]
            + [pltpu.SemaphoreType.DMA((3,))],
            input_output_aliases={7 + i: i for i in range(len(written))},
            cost_estimate=pl.CostEstimate(
                flops=4 * tokens * HD * wide, bytes_accessed=4 * tokens * wide, transcendentals=0
            ),
            compiler_params=pltpu.CompilerParams(vmem_limit_bytes=24 * MIB),
        )(keys, values, out_grad, *local, state, *written)

    return finish(False, other, *finish(True, mine))


def solution(mesh):
    spec = P(DEVICES, None)
    return jax.shard_map(
        body, mesh=mesh, in_specs=(spec,) * 4, out_specs=(spec,) * 3, check_vma=False
    )
```

time: 22.1 us -> 22 us (level)
  waiting for transfers between devices: 6.5 us -> 5.58 us
  Pallas kernels: 4.44 us -> 5.25 us
    ppermute x1, waiting for transfers between devices: 1.06 us -> 0.17 us  [carry_states(): lax.ppermute(theirs.astype(BF16), DEVICES, swap)]
    pallas_call x1 -> x2, Pallas kernels: 1.02 us -> 1.83 us  [finish(): pl.pallas_call(functools.partial(finish_kernel, mine), out_shape=tuple((j...]
  transfers between devices with their start and end apart: 8 -> 8, of which waited for: 6 -> 6; matrix products, arithmetic and copies ran while one was open for 0% -> 0% of each run, Pallas kernels for 7% -> 11%
where the time goes in v4:
time: 22 us; the launch traced here: 21.9 us
  starting transfers between devices  9.99 us (45%)
  waiting for transfers between devices  5.58 us (25%)
  Pallas kernels  5.25 us (24%)
  between operations  0.8 us (4%)
  other arithmetic  0.25 us (1%)
    ppermute x6, starting transfers between devices, carry_states(): lax.ppermute(message, DEVICES, [(i, target(i, size, low, move)) for i in...  9.26 us
    ppermute x6, waiting for transfers between devices, carry_states(): lax.ppermute(message, DEVICES, [(i, target(i, size, low, move)) for i in...  4.51 us
    pallas_call x1, Pallas kernels, body(): pl.pallas_call(states_kernel, out_shape=(jax.ShapeDtypeStruct(shape, BF16...  1.85 us
    pallas_call x2, Pallas kernels, finish(): pl.pallas_call(functools.partial(finish_kernel, mine), out_shape=tuple((j...  1.83 us
    pallas_call x1, Pallas kernels, carry_states(): *local, total = local_terms(keep, got)  1.57 us
    ppermute x1, waiting for transfers between devices, carry_states(): got = lax.ppermute(send, DEVICES, swap)  0.9 us
    ppermute x1, starting transfers between devices, carry_states(): got = lax.ppermute(send, DEVICES, swap)  0.52 us
  transfers between devices with their start and end apart: 8, of which 6 were waited for; matrix products, arithmetic and copies ran while one was open for 0% of the time, Pallas kernels for 11%

profile of v4, /device:TPU:0, one launch (start us, length us, event | category | flops | bytes accessed | tf_op | source)
XLA Modules:
  0.0 21.9 jit_solution(117125563295238603)
XLA Ops:
  0.6 0.0 copy-start.1
  0.6 0.0 copy-start.2
  0.7 0.0 copy-start.3
  0.7 1.9 %shard_map.67 = (bf16[2,1,128,128]{3,2,1,0:T(8,128)(2,1)S(1)}, bf16[2,1,128,128]{3,2,1,0:T(8,128)(2,1)S(1)}) custom-call(bf16[128,1024]{1,0:T(8,128)(2,1)} %q_ref.1, bf16[128,256]{1,0:T(8,128)(2,1)} %k_ref.5, bf16[128,256]{1,0:T(8,128)(2,1)} %v_ref.5, bf16[128,1024]{1,0:T(8,128)(2,1)} %o_ref.5), custom_call_target="tpu_custom_call" | custom-call | tf_op jit(solution)/shard_map/pallas_call | solution.py:233
  2.5 0.0 copy-start
  2.5 0.5 %collective-permute-start = (bf16[2,1,128,128]{3,2,1,0:T(8,128)(2,1)S(1)}, bf16[2,1,128,128]{3,2,1,0:T(8,128)(2,1)S(1)}, u32[]{:S(2)}, u32[]{:S(2)}) collective-permute-start(bf16[2,1,128,128]{3,2,1,0:T(8,128)(2,1)S(1)} %get-tuple-element.16), channel_id=1, source_target_pairs={{0,1},{1,0},{2,3},{3,2},{4,5},{5,4},{6,7},{7,6},{8,9},{9,8},{10,11... | collective-permute-start | bytes 196616 | tf_op jit(solution)/shard_map/ppermute | solution.py:190
  3.1 0.9 %collective-permute-done.got_ref = bf16[2,1,128,128]{3,2,1,0:T(8,128)(2,1)S(1)} collective-permute-done((bf16[2,1,128,128]{3,2,1,0:T(8,128)(2,1)S(1)}, bf16[2,1,128,128]{3,2,1,0:T(8,128)(2,1)S(1)}, u32[]{:S(2)}, u32[]{:S(2)}) %collective-permute-start) | collective-permute-done | bytes 65568 | tf_op jit(solution)/shard_map/ppermute | solution.py:190
  4.0 3.9 %collective-permute-start.3 = (bf16[2,1,128,128]{3,2,1,0:T(8,128)(2,1)S(1)}, bf16[2,1,128,128]{3,2,1,0:T(8,128)(2,1)S(1)}, u32[]{:S(2)}, u32[]{:S(2)}) collective-permute-start(bf16[2,1,128,128]{3,2,1,0:T(8,128)(2,1)S(1)} %add_convert_fusion.1), channel_id=1, source_target_pairs={{0,6},{1,7},{2,4},{3,5},{4,2},{5,3},{6,0},{7,1},{8,14},{9,15},{10,... | collective-permute-start | bytes 196616 | tf_op jit(solution)/shard_map/ppermute | solution.py:201
  7.8 0.0 collective-permute-start.2
  7.8 0.4 %collective-permute-start.1 = (bf16[2,1,128,128]{3,2,1,0:T(8,128)(2,1)S(1)}, bf16[2,1,128,128]{3,2,1,0:T(8,128)(2,1)S(1)}, u32[]{:S(2)}, u32[]{:S(2)}) collective-permute-start(bf16[2,1,128,128]{3,2,1,0:T(8,128)(2,1)S(1)} %add_convert_fusion.1), channel_id=1, source_target_pairs={{0,3},{1,2},{2,1},{3,0},{4,7},{5,6},{6,5},{7,4},{8,11},{9,10},{10,... | collective-permute-start | bytes 196616 | tf_op jit(solution)/shard_map/ppermute | solution.py:201
  8.2 0.0 copy-done.1
  8.2 0.0 copy-done.2
  8.2 0.0 copy-done.3
  8.2 0.0 copy-done
  8.2 1.6 %shard_map.68 = (f32[128,1024]{1,0:T(8,128)S(1)}, f32[128,256]{1,0:T(8,128)S(1)}, f32[128,256]{1,0:T(8,128)S(1)}, f32[2,1,128,128]{3,2,1,0:T(8,128)S(1)}) custom-call(bf16[128,1024]{1,0:T(8,128)(2,1)S(1)} %copy-done.3, bf16[128,256]{1,0:T(8,128)(2,1)S(1)} %copy-done.1, bf16[128,256]{1,0:T(8,128)(2,1)S(1)} %copy-done.2, bf16[128,1024]{1,0:T(8,128)(2,1)S(1)} %copy-done, ...), custom_call_target="tpu_custom_call" | custom-call | flops 201326592 | bytes 1572864 | tf_op jit(solution)/shard_map/pallas_call | solution.py:191
  9.8 0.5 %collective-permute-done.3 = bf16[2,1,128,128]{3,2,1,0:T(8,128)(2,1)S(1)} collective-permute-done((bf16[2,1,128,128]{3,2,1,0:T(8,128)(2,1)S(1)}, bf16[2,1,128,128]{3,2,1,0:T(8,128)(2,1)S(1)}, u32[]{:S(2)}, u32[]{:S(2)}) %collective-permute-start.3) | collective-permute-done | bytes 65568 | tf_op jit(solution)/shard_map/ppermute | solution.py:201
  10.3 1.8 %collective-permute-done.2 = bf16[2,1,128,128]{3,2,1,0:T(8,128)(2,1)S(1)} collective-permute-done((bf16[2,1,128,128]{3,2,1,0:T(8,128)(2,1)S(1)}, bf16[2,1,128,128]{3,2,1,0:T(8,128)(2,1)S(1)}, u32[]{:S(2)}, u32[]{:S(2)}) %collective-permute-start.2) | collective-permute-done | bytes 65568 | tf_op jit(solution)/shard_map/ppermute | solution.py:201
  12.2 0.0 collective-permute-done.1
  12.2 1.3 %collective-permute-start.6 = (bf16[1,128,128]{2,1,0:T(8,128)(2,1)S(1)}, bf16[1,128,128]{2,1,0:T(8,128)(2,1)S(1)}, u32[]{:S(2)}, u32[]{:S(2)}) collective-permute-start(bf16[1,128,128]{2,1,0:T(8,128)(2,1)S(1)} %get-tuple-element.23), channel_id=1, source_target_pairs={{0,9},{1,8},{2,11},{3,10},{4,13},{5,12},{6,15},{7,14},{8,17},{9,16... | collective-permute-start | bytes 98312 | tf_op jit(solution)/shard_map/ppermute | solution.py:214
  13.6 2.6 %collective-permute-start.5 = (bf16[1,128,128]{2,1,0:T(8,128)(2,1)S(1)}, bf16[1,128,128]{2,1,0:T(8,128)(2,1)S(1)}, u32[]{:S(2)}, u32[]{:S(2)}) collective-permute-start(bf16[1,128,128]{2,1,0:T(8,128)(2,1)S(1)} %get-tuple-element.22), channel_id=1, source_target_pairs={{0,16},{1,17},{2,18},{3,19},{4,20},{5,21},{6,22},{7,23},{8,24},{9,... | collective-permute-start | bytes 98312 | tf_op jit(solution)/shard_map/ppermute | solution.py:214
  16.2 1.1 %collective-permute-start.4 = (bf16[1,128,128]{2,1,0:T(8,128)(2,1)S(1)}, bf16[1,128,128]{2,1,0:T(8,128)(2,1)S(1)}, u32[]{:S(2)}, u32[]{:S(2)}) collective-permute-start(bf16[1,128,128]{2,1,0:T(8,128)(2,1)S(1)} %get-tuple-element.21), channel_id=1, source_target_pairs={{0,25},{1,24},{2,27},{3,26},{4,29},{5,28},{6,31},{7,30},{8,1},{9,0... | collective-permute-start | bytes 98312 | tf_op jit(solution)/shard_map/ppermute | solution.py:214
  17.4 0.0 collective-permute-done.6
  17.4 1.1 %collective-permute-done.5 = bf16[1,128,128]{2,1,0:T(8,128)(2,1)S(1)} collective-permute-done((bf16[1,128,128]{2,1,0:T(8,128)(2,1)S(1)}, bf16[1,128,128]{2,1,0:T(8,128)(2,1)S(1)}, u32[]{:S(2)}, u32[]{:S(2)}) %collective-permute-start.5) | collective-permute-done | bytes 32800 | tf_op jit(solution)/shard_map/ppermute | solution.py:214
  18.5 1.0 %collective-permute-done.4 = bf16[1,128,128]{2,1,0:T(8,128)(2,1)S(1)} collective-permute-done((bf16[1,128,128]{2,1,0:T(8,128)(2,1)S(1)}, bf16[1,128,128]{2,1,0:T(8,128)(2,1)S(1)}, u32[]{:S(2)}, u32[]{:S(2)}) %collective-permute-start.4) | collective-permute-done | bytes 32800 | tf_op jit(solution)/shard_map/ppermute | solution.py:214
  19.5 0.1 fusion.26
  19.7 0.2 collective-permute-start.7
  19.9 0.9 %shard_map.69 = (bf16[128,1024]{1,0:T(8,128)(2,1)}, bf16[128,256]{1,0:T(8,128)(2,1)}, bf16[128,256]{1,0:T(8,128)(2,1)}) custom-call(bf16[128,256]{1,0:T(8,128)(2,1)S(1)} %copy-done.1, bf16[128,256]{1,0:T(8,128)(2,1)S(1)} %copy-done.2, bf16[128,1024]{1,0:T(8,128)(2,1)S(1)} %copy-done, f32[128,1024]{1,0:T(8,128)S(1)} %get-tuple-element.17.ql_ref, ...), custom_call_target="tpu_custom_call" | custom-call | flops 67108864 | bytes 524288 | tf_op jit(solution)/shard_map/pallas_call | solution.py:254
  20.8 0.2 collective-permute-done.7.state_ref
  21.0 0.9 %shard_map.70 = (bf16[128,1024]{1,0:T(8,128)(2,1)}, bf16[128,256]{1,0:T(8,128)(2,1)}, bf16[128,256]{1,0:T(8,128)(2,1)}) custom-call(bf16[128,256]{1,0:T(8,128)(2,1)S(1)} %copy-done.1, bf16[128,256]{1,0:T(8,128)(2,1)S(1)} %copy-done.2, bf16[128,1024]{1,0:T(8,128)(2,1)S(1)} %copy-done, ...), custom_call_target="tpu_custom_call", output_to_operand_aliasing={{0}: (7, {}), {1}: (8, {}), {2}: (9, {})} | custom-call | flops 67108864 | bytes 524288 | tf_op jit(solution)/shard_map/pallas_call | solution.py:254
  (11 shorter events, 0.2 us)
Async XLA Ops:
  0.6 7.6 %copy-start.1 = (bf16[128,256]{1,0:T(8,128)(2,1)S(1)}, bf16[128,256]{1,0:T(8,128)(2,1)}, u32[]{:S(2)}) copy-start(bf16[128,256]{1,0:T(8,128)(2,1)} %k_ref.5) | copy-start | bytes 196612
  0.6 7.6 %copy-start.2 = (bf16[128,256]{1,0:T(8,128)(2,1)S(1)}, bf16[128,256]{1,0:T(8,128)(2,1)}, u32[]{:S(2)}) copy-start(bf16[128,256]{1,0:T(8,128)(2,1)} %v_ref.5) | copy-start | bytes 196612
  0.7 7.6 %copy-start.3 = (bf16[128,1024]{1,0:T(8,128)(2,1)S(1)}, bf16[128,1024]{1,0:T(8,128)(2,1)}, u32[]{:S(2)}) copy-start(bf16[128,1024]{1,0:T(8,128)(2,1)} %q_ref.1) | copy-start | bytes 786436
  2.5 5.7 %copy-start = (bf16[128,1024]{1,0:T(8,128)(2,1)S(1)}, bf16[128,1024]{1,0:T(8,128)(2,1)}, u32[]{:S(2)}) copy-start(bf16[128,1024]{1,0:T(8,128)(2,1)} %o_ref.5) | copy-start | bytes 786436
  2.5 1.4 %collective-permute-start = (bf16[2,1,128,128]{3,2,1,0:T(8,128)(2,1)S(1)}, bf16[2,1,128,128]{3,2,1,0:T(8,128)(2,1)S(1)}, u32[]{:S(2)}, u32[]{:S(2)}) collective-permute-start(bf16[2,1,128,128]{3,2,1,0:T(8,128)(2,1)S(1)} %get-tuple-element.16), channel_id=1, source_target_pairs={{0,1},{1,0},{2,3},{3,2},{4,5},{5,4},{6,7},{7,6},{8,9},{9,8},{10,11... | collective-permute-start | bytes 196616 | tf_op jit(solution)/shard_map/ppermute | solution.py:190
  4.0 6.3 %collective-permute-start.3 = (bf16[2,1,128,128]{3,2,1,0:T(8,128)(2,1)S(1)}, bf16[2,1,128,128]{3,2,1,0:T(8,128)(2,1)S(1)}, u32[]{:S(2)}, u32[]{:S(2)}) collective-permute-start(bf16[2,1,128,128]{3,2,1,0:T(8,128)(2,1)S(1)} %add_convert_fusion.1), channel_id=1, source_target_pairs={{0,6},{1,7},{2,4},{3,5},{4,2},{5,3},{6,0},{7,1},{8,14},{9,15},{10,... | collective-permute-start | bytes 196616 | tf_op jit(solution)/shard_map/ppermute | solution.py:201
  7.8 4.3 %collective-permute-start.2 = (bf16[2,1,128,128]{3,2,1,0:T(8,128)(2,1)S(1)}, bf16[2,1,128,128]{3,2,1,0:T(8,128)(2,1)S(1)}, u32[]{:S(2)}, u32[]{:S(2)}) collective-permute-start(bf16[2,1,128,128]{3,2,1,0:T(8,128)(2,1)S(1)} %add_convert_fusion.1), channel_id=1, source_target_pairs={{0,5},{1,4},{2,7},{3,6},{4,1},{5,0},{6,3},{7,2},{8,13},{9,12},{10,... | collective-permute-start | bytes 196616 | tf_op jit(solution)/shard_map/ppermute | solution.py:201
  7.8 4.3 %collective-permute-start.1 = (bf16[2,1,128,128]{3,2,1,0:T(8,128)(2,1)S(1)}, bf16[2,1,128,128]{3,2,1,0:T(8,128)(2,1)S(1)}, u32[]{:S(2)}, u32[]{:S(2)}) collective-permute-start(bf16[2,1,128,128]{3,2,1,0:T(8,128)(2,1)S(1)} %add_convert_fusion.1), channel_id=1, source_target_pairs={{0,3},{1,2},{2,1},{3,0},{4,7},{5,6},{6,5},{7,4},{8,11},{9,10},{10,... | collective-permute-start | bytes 196616 | tf_op jit(solution)/shard_map/ppermute | solution.py:201
  12.2 5.2 %collective-permute-start.6 = (bf16[1,128,128]{2,1,0:T(8,128)(2,1)S(1)}, bf16[1,128,128]{2,1,0:T(8,128)(2,1)S(1)}, u32[]{:S(2)}, u32[]{:S(2)}) collective-permute-start(bf16[1,128,128]{2,1,0:T(8,128)(2,1)S(1)} %get-tuple-element.23), channel_id=1, source_target_pairs={{0,9},{1,8},{2,11},{3,10},{4,13},{5,12},{6,15},{7,14},{8,17},{9,16... | collective-permute-start | bytes 98312 | tf_op jit(solution)/shard_map/ppermute | solution.py:214
  13.6 4.9 %collective-permute-start.5 = (bf16[1,128,128]{2,1,0:T(8,128)(2,1)S(1)}, bf16[1,128,128]{2,1,0:T(8,128)(2,1)S(1)}, u32[]{:S(2)}, u32[]{:S(2)}) collective-permute-start(bf16[1,128,128]{2,1,0:T(8,128)(2,1)S(1)} %get-tuple-element.22), channel_id=1, source_target_pairs={{0,16},{1,17},{2,18},{3,19},{4,20},{5,21},{6,22},{7,23},{8,24},{9,... | collective-permute-start | bytes 98312 | tf_op jit(solution)/shard_map/ppermute | solution.py:214
  16.2 3.4 %collective-permute-start.4 = (bf16[1,128,128]{2,1,0:T(8,128)(2,1)S(1)}, bf16[1,128,128]{2,1,0:T(8,128)(2,1)S(1)}, u32[]{:S(2)}, u32[]{:S(2)}) collective-permute-start(bf16[1,128,128]{2,1,0:T(8,128)(2,1)S(1)} %get-tuple-element.21), channel_id=1, source_target_pairs={{0,25},{1,24},{2,27},{3,26},{4,29},{5,28},{6,31},{7,30},{8,1},{9,0... | collective-permute-start | bytes 98312 | tf_op jit(solution)/shard_map/ppermute | solution.py:214
  19.7 1.3 %collective-permute-start.7 = (bf16[2,1,128,128]{3,2,1,0:T(8,128)(2,1)S(1)}, bf16[2,1,128,128]{3,2,1,0:T(8,128)(2,1)S(1)}, u32[]{:S(2)}, u32[]{:S(2)}) collective-permute-start(bf16[2,1,128,128]{3,2,1,0:T(8,128)(2,1)S(1)} %pad_maximum_fusion), channel_id=1, source_target_pairs={{0,1},{1,0},{2,3},{3,2},{4,5},{5,4},{6,7},{7,6},{8,9},{9,8},{10,11... | collective-permute-start | bytes 196616 | tf_op jit(solution)/shard_map/ppermute | solution.py:223

commit v5 on v4

--- a/solution.py
+++ b/solution.py
@@ -41,43 +41,42 @@
     return 1.0 / jnp.sqrt((HD * (positions + 1)).astype(F32))
 
 
-def states_kernel(q_hbm, k_hbm, v_hbm, o_hbm, keep_ref, send_ref, q_ref, k_ref, v_ref, o_ref, sems):
-    tokens = q_hbm.shape[0]
-    kv = k_hbm.shape[1] // HD
-    group = q_hbm.shape[1] // HD // kv
-    half = kv // 2
-    arrivals = [
-        pltpu.make_async_copy(source, place, sems.at[i])
+def half_states(k_ref, v_ref, o_ref, q_ref, out_ref):
+    tokens = q_ref.shape[0]
+    half = k_ref.shape[1] // HD
+    group = q_ref.shape[1] // k_ref.shape[1]
+    scale = row_scale(tokens, (tokens, HD), 0)
+    for g in range(half):
+        out_ref[0, g] = dot(v_ref[columns(g)], k_ref[columns(g)], TN).astype(BF16)
+    for g in range(half):
+        grad = jnp.zeros((HD, HD), F32)
+        for h in range(g * group, (g + 1) * group):
+            scaled = (scale * o_ref[columns(h)].astype(F32)).astype(BF16)
+            grad = grad + dot(scaled, q_ref[columns(h)], TN)
+        out_ref[1, g] = grad.astype(BF16)
+
+
+def half_columns(ref, side):
+    width = ref.shape[1] // 2
+    return ref.at[:, pl.ds(pl.multiple_of(side * width, HD), width)]
+
+
+def send_kernel(k_hbm, v_hbm, o_hbm, q_hbm, out_ref, k_ref, v_ref, o_ref, q_ref, sems):
+    side = 1 - side_of(device_index(), lax.axis_size(SEQ) * lax.axis_size(HEAD))
+    copies = [
+        pltpu.make_async_copy(half_columns(source, side), place, sems.at[i])
         for i, (source, place) in enumerate([(k_hbm, k_ref), (v_hbm, v_ref), (o_hbm, o_ref), (q_hbm, q_ref)])
     ]
-    for copy in arrivals:
+    for copy in copies:
         copy.start(priority=1)
+    for copy in copies:
+        copy.wait()
+    half_states(k_ref, v_ref, o_ref, q_ref, out_ref)
+
+
+def keep_kernel(k_ref, v_ref, o_ref, q_ref, out_ref):
     side = side_of(device_index(), lax.axis_size(SEQ) * lax.axis_size(HEAD))
-    scale = row_scale(tokens, (tokens, HD), 0)
-
-    def put(g, kind, state):
-        mine = side == g // half
-
-        @pl.when(mine)
-        def _():
-            keep_ref[kind, g % half] = state
-
-        @pl.when(jnp.logical_not(mine))
-        def _():
-            send_ref[kind, g % half] = state
-
-    arrivals[0].wait()
-    arrivals[1].wait()
-    for g in range(kv):
-        put(g, 0, dot(v_ref[columns(g)], k_ref[columns(g)], TN).astype(BF16))
-    arrivals[2].wait()
-    scaled = [(scale * o_ref[columns(h)].astype(F32)).astype(BF16) for h in range(kv * group)]
-    arrivals[3].wait()
-    for g in range(kv):
-        grad = jnp.zeros((HD, HD), F32)
-        for h in range(g * group, (g + 1) * group):
-            grad = grad + dot(scaled[h], q_ref[columns(h)], TN)
-        put(g, 1, grad.astype(BF16))
+    half_states(*[half_columns(ref, side) for ref in (k_ref, v_ref, o_ref, q_ref)], out_ref)
 
 
 def local_kernel(q_ref, k_ref, v_ref, o_ref, keep_ref, got_ref, qg_ref, kg_ref, vg_ref, total_ref):
@@ -188,6 +187,7 @@
     index = device_index()
     swap = [(i, i ^ 1) for i in range(size)]
     got = lax.ppermute(send, DEVICES, swap)
+    keep = keep()
     *local, total = local_terms(keep, got)
     keep = keep.astype(F32)
     got = got.astype(F32)
@@ -230,17 +230,32 @@
     anywhere = pl.BlockSpec(memory_space=pltpu.HBM)
     inputs = (queries, keys, values, out_grad)
     tokens, wide, narrow = queries.shape[0], queries.shape[1], keys.shape[1]
-    keep, send = pl.pallas_call(
-        states_kernel,
-        out_shape=(jax.ShapeDtypeStruct(shape, BF16),) * 2,
+    ordered = (keys, values, out_grad, queries)
+    halves = [pltpu.VMEM((x.shape[0], x.shape[1] // 2), BF16) for x in ordered]
+    send = pl.pallas_call(
+        send_kernel,
+        out_shape=jax.ShapeDtypeStruct(shape, BF16),
         in_specs=[anywhere] * 4,
-        out_specs=[vmem] * 2,
-        scratch_shapes=[pltpu.VMEM(x.shape, BF16) for x in inputs] + [pltpu.SemaphoreType.DMA((4,))],
-        compiler_params=pltpu.CompilerParams(vmem_limit_bytes=55104 * 1024),
-    )(*inputs)
+        out_specs=vmem,
+        scratch_shapes=halves + [pltpu.SemaphoreType.DMA((4,))],
+        compiler_params=pltpu.CompilerParams(vmem_limit_bytes=55144 * 1024),
+    )(*ordered)
+
+    def keep():
+        return pl.pallas_call(
+            keep_kernel,
+            out_shape=jax.ShapeDtypeStruct(shape, BF16),
+            in_specs=[vmem] * 4,
+            out_specs=vmem,
+            cost_estimate=pl.CostEstimate(
+                flops=2 * tokens * HD * wide, bytes_accessed=4 * tokens * wide, transcendentals=0
+            ),
+            compiler_params=pltpu.CompilerParams(vmem_limit_bytes=24 * MIB),
+        )(*ordered)
+
     local_terms = pl.pallas_call(
         local_kernel,
-        out_shape=tuple(jax.ShapeDtypeStruct(x.shape, F32) for x in (queries, keys, values, keep)),
+        out_shape=tuple(jax.ShapeDtypeStruct(x.shape, F32) for x in (queries, keys, values, send)),
         in_specs=[vmem] * 6,
         out_specs=[vmem] * 4,
         cost_estimate=pl.CostEstimate(

time: 22 us -> 21.6 us (0.982)
  waiting for transfers between devices: 5.58 us -> 5.32 us
    ppermute x1, waiting for transfers between devices: 0.9 us -> 0.62 us  [carry_states(): got = lax.ppermute(send, DEVICES, swap)]
    pallas_call x1 -> x2, Pallas kernels: 1.85 us -> 1.64 us  [the longest x1 1.38 us: body(): pl.pallas_call(send_kernel, out_shape=jax.ShapeDtypeStruct(shape, BF16),...]
  transfers between devices with their start and end apart: 8 -> 8, of which waited for: 6 -> 6; matrix products, arithmetic and copies ran while one was open for 0% -> 0% of each run, Pallas kernels for 11% -> 13%
where the time goes in v5:
time: 21.6 us; the launch traced here: 21.4 us
  starting transfers between devices  9.99 us (46%)
  waiting for transfers between devices  5.32 us (25%)
  Pallas kernels  5.03 us (23%)
  between operations  0.81 us (4%)
  other arithmetic  0.25 us (1%)
    ppermute x6, starting transfers between devices, carry_states(): lax.ppermute(message, DEVICES, [(i, target(i, size, low, move)) for i in...  9.26 us
    ppermute x6, waiting for transfers between devices, carry_states(): lax.ppermute(message, DEVICES, [(i, target(i, size, low, move)) for i in...  4.52 us
    pallas_call x2, Pallas kernels, finish(): pl.pallas_call(functools.partial(finish_kernel, mine), out_shape=tuple((j...  1.83 us
    pallas_call x1, Pallas kernels, carry_states(): *local, total = local_terms(keep, got)  1.56 us
    pallas_call x1, Pallas kernels, body(): pl.pallas_call(send_kernel, out_shape=jax.ShapeDtypeStruct(shape, BF16),...  1.38 us
    ppermute x1, waiting for transfers between devices, carry_states(): got = lax.ppermute(send, DEVICES, swap)  0.62 us
    ppermute x1, starting transfers between devices, carry_states(): got = lax.ppermute(send, DEVICES, swap)  0.52 us
  transfers between devices with their start and end apart: 8, of which 6 were waited for; matrix products, arithmetic and copies ran while one was open for 0% of the time, Pallas kernels for 13%

profile of v5, /device:TPU:0, one launch (start us, length us, event | category | flops | bytes accessed | tf_op | source)
XLA Modules:
  0.0 21.4 jit_solution(14297731349467939813)
XLA Ops:
  0.6 0.0 copy-start.2
  0.6 0.0 copy-start.3
  0.7 0.0 copy-start
  0.7 0.0 copy-start.1
  0.7 1.4 %shard_map.68 = bf16[2,1,128,128]{3,2,1,0:T(8,128)(2,1)S(1)} custom-call(bf16[128,256]{1,0:T(8,128)(2,1)} %k_ref.7, bf16[128,256]{1,0:T(8,128)(2,1)} %v_ref.7, bf16[128,1024]{1,0:T(8,128)(2,1)} %o_ref.7, bf16[128,1024]{1,0:T(8,128)(2,1)} %q_ref.3), custom_call_target="tpu_custom_call" | custom-call | tf_op jit(solution)/shard_map/pallas_call | solution.py:235
  2.1 0.5 %collective-permute-start = (bf16[2,1,128,128]{3,2,1,0:T(8,128)(2,1)S(1)}, bf16[2,1,128,128]{3,2,1,0:T(8,128)(2,1)S(1)}, u32[]{:S(2)}, u32[]{:S(2)}) collective-permute-start(bf16[2,1,128,128]{3,2,1,0:T(8,128)(2,1)S(1)} %shard_map.68), channel_id=1, source_target_pairs={{0,1},{1,0},{2,3},{3,2},{4,5},{5,4},{6,7},{7,6},{8,9},{9,8},{10,11... | collective-permute-start | bytes 196616 | tf_op jit(solution)/shard_map/ppermute | solution.py:189
  2.6 0.0 copy-done.2
  2.6 0.0 copy-done.3
  2.6 0.0 copy-done
  2.6 0.0 copy-done.1
  2.6 0.3 %shard_map.67.keep_ref = bf16[2,1,128,128]{3,2,1,0:T(8,128)(2,1)S(1)} custom-call(bf16[128,256]{1,0:T(8,128)(2,1)S(1)} %copy-done.2, bf16[128,256]{1,0:T(8,128)(2,1)S(1)} %copy-done.3, bf16[128,1024]{1,0:T(8,128)(2,1)S(1)} %copy-done, bf16[128,1024]{1,0:T(8,128)(2,1)S(1)} %copy-done.1), custom_call_target="tpu_custom_call" | custom-call | flops 33554432 | bytes 524288 | tf_op jit(solution)/shard_map/pallas_call | solution.py:245
  2.9 0.6 %collective-permute-done.got_ref = bf16[2,1,128,128]{3,2,1,0:T(8,128)(2,1)S(1)} collective-permute-done((bf16[2,1,128,128]{3,2,1,0:T(8,128)(2,1)S(1)}, bf16[2,1,128,128]{3,2,1,0:T(8,128)(2,1)S(1)}, u32[]{:S(2)}, u32[]{:S(2)}) %collective-permute-start) | collective-permute-done | bytes 65568 | tf_op jit(solution)/shard_map/ppermute | solution.py:189
  3.5 3.9 %collective-permute-start.3 = (bf16[2,1,128,128]{3,2,1,0:T(8,128)(2,1)S(1)}, bf16[2,1,128,128]{3,2,1,0:T(8,128)(2,1)S(1)}, u32[]{:S(2)}, u32[]{:S(2)}) collective-permute-start(bf16[2,1,128,128]{3,2,1,0:T(8,128)(2,1)S(1)} %add_convert_fusion.1), channel_id=1, source_target_pairs={{0,6},{1,7},{2,4},{3,5},{4,2},{5,3},{6,0},{7,1},{8,14},{9,15},{10,... | collective-permute-start | bytes 196616 | tf_op jit(solution)/shard_map/ppermute | solution.py:201
  7.4 0.0 collective-permute-start.2
  7.4 0.4 %collective-permute-start.1 = (bf16[2,1,128,128]{3,2,1,0:T(8,128)(2,1)S(1)}, bf16[2,1,128,128]{3,2,1,0:T(8,128)(2,1)S(1)}, u32[]{:S(2)}, u32[]{:S(2)}) collective-permute-start(bf16[2,1,128,128]{3,2,1,0:T(8,128)(2,1)S(1)} %add_convert_fusion.1), channel_id=1, source_target_pairs={{0,3},{1,2},{2,1},{3,0},{4,7},{5,6},{6,5},{7,4},{8,11},{9,10},{10,... | collective-permute-start | bytes 196616 | tf_op jit(solution)/shard_map/ppermute | solution.py:201
  7.7 1.6 %shard_map.69 = (f32[128,1024]{1,0:T(8,128)S(1)}, f32[128,256]{1,0:T(8,128)S(1)}, f32[128,256]{1,0:T(8,128)S(1)}, f32[2,1,128,128]{3,2,1,0:T(8,128)S(1)}) custom-call(bf16[128,1024]{1,0:T(8,128)(2,1)S(1)} %copy-done.1, bf16[128,256]{1,0:T(8,128)(2,1)S(1)} %copy-done.2, bf16[128,256]{1,0:T(8,128)(2,1)S(1)} %copy-done.3, bf16[128,1024]{1,0:T(8,128)(2,1)S(1)} %copy-done, ...), custom_call_target="tpu_custom_call" | custom-call | flops 201326592 | bytes 1572864 | tf_op jit(solution)/shard_map/pallas_call | solution.py:191
  9.3 0.6 %collective-permute-done.3 = bf16[2,1,128,128]{3,2,1,0:T(8,128)(2,1)S(1)} collective-permute-done((bf16[2,1,128,128]{3,2,1,0:T(8,128)(2,1)S(1)}, bf16[2,1,128,128]{3,2,1,0:T(8,128)(2,1)S(1)}, u32[]{:S(2)}, u32[]{:S(2)}) %collective-permute-start.3) | collective-permute-done | bytes 65568 | tf_op jit(solution)/shard_map/ppermute | solution.py:201
  9.8 1.8 %collective-permute-done.2 = bf16[2,1,128,128]{3,2,1,0:T(8,128)(2,1)S(1)} collective-permute-done((bf16[2,1,128,128]{3,2,1,0:T(8,128)(2,1)S(1)}, bf16[2,1,128,128]{3,2,1,0:T(8,128)(2,1)S(1)}, u32[]{:S(2)}, u32[]{:S(2)}) %collective-permute-start.2) | collective-permute-done | bytes 65568 | tf_op jit(solution)/shard_map/ppermute | solution.py:201
  11.7 0.0 collective-permute-done.1
  11.8 1.3 %collective-permute-start.6 = (bf16[1,128,128]{2,1,0:T(8,128)(2,1)S(1)}, bf16[1,128,128]{2,1,0:T(8,128)(2,1)S(1)}, u32[]{:S(2)}, u32[]{:S(2)}) collective-permute-start(bf16[1,128,128]{2,1,0:T(8,128)(2,1)S(1)} %get-tuple-element.19), channel_id=1, source_target_pairs={{0,9},{1,8},{2,11},{3,10},{4,13},{5,12},{6,15},{7,14},{8,17},{9,16... | collective-permute-start | bytes 98312 | tf_op jit(solution)/shard_map/ppermute | solution.py:214
  13.1 2.6 %collective-permute-start.5 = (bf16[1,128,128]{2,1,0:T(8,128)(2,1)S(1)}, bf16[1,128,128]{2,1,0:T(8,128)(2,1)S(1)}, u32[]{:S(2)}, u32[]{:S(2)}) collective-permute-start(bf16[1,128,128]{2,1,0:T(8,128)(2,1)S(1)} %get-tuple-element.18), channel_id=1, source_target_pairs={{0,16},{1,17},{2,18},{3,19},{4,20},{5,21},{6,22},{7,23},{8,24},{9,... | collective-permute-start | bytes 98312 | tf_op jit(solution)/shard_map/ppermute | solution.py:214
  15.7 1.1 %collective-permute-start.4 = (bf16[1,128,128]{2,1,0:T(8,128)(2,1)S(1)}, bf16[1,128,128]{2,1,0:T(8,128)(2,1)S(1)}, u32[]{:S(2)}, u32[]{:S(2)}) collective-permute-start(bf16[1,128,128]{2,1,0:T(8,128)(2,1)S(1)} %get-tuple-element.17), channel_id=1, source_target_pairs={{0,25},{1,24},{2,27},{3,26},{4,29},{5,28},{6,31},{7,30},{8,1},{9,0... | collective-permute-start | bytes 98312 | tf_op jit(solution)/shard_map/ppermute | solution.py:214
  16.9 0.0 collective-permute-done.6
  17.0 1.1 %collective-permute-done.5 = bf16[1,128,128]{2,1,0:T(8,128)(2,1)S(1)} collective-permute-done((bf16[1,128,128]{2,1,0:T(8,128)(2,1)S(1)}, bf16[1,128,128]{2,1,0:T(8,128)(2,1)S(1)}, u32[]{:S(2)}, u32[]{:S(2)}) %collective-permute-start.5) | collective-permute-done | bytes 32800 | tf_op jit(solution)/shard_map/ppermute | solution.py:214
  18.0 1.0 %collective-permute-done.4 = bf16[1,128,128]{2,1,0:T(8,128)(2,1)S(1)} collective-permute-done((bf16[1,128,128]{2,1,0:T(8,128)(2,1)S(1)}, bf16[1,128,128]{2,1,0:T(8,128)(2,1)S(1)}, u32[]{:S(2)}, u32[]{:S(2)}) %collective-permute-start.4) | collective-permute-done | bytes 32800 | tf_op jit(solution)/shard_map/ppermute | solution.py:214
  19.1 0.1 fusion.26
  19.2 0.2 %collective-permute-start.7 = (bf16[2,1,128,128]{3,2,1,0:T(8,128)(2,1)S(1)}, bf16[2,1,128,128]{3,2,1,0:T(8,128)(2,1)S(1)}, u32[]{:S(2)}, u32[]{:S(2)}) collective-permute-start(bf16[2,1,128,128]{3,2,1,0:T(8,128)(2,1)S(1)} %pad_maximum_fusion), channel_id=1, source_target_pairs={{0,1},{1,0},{2,3},{3,2},{4,5},{5,4},{6,7},{7,6},{8,9},{9,8},{10,11... | collective-permute-start | bytes 196616 | tf_op jit(solution)/shard_map/ppermute | solution.py:223
  19.4 0.9 %shard_map.70 = (bf16[128,1024]{1,0:T(8,128)(2,1)}, bf16[128,256]{1,0:T(8,128)(2,1)}, bf16[128,256]{1,0:T(8,128)(2,1)}) custom-call(bf16[128,256]{1,0:T(8,128)(2,1)S(1)} %copy-done.2, bf16[128,256]{1,0:T(8,128)(2,1)S(1)} %copy-done.3, bf16[128,1024]{1,0:T(8,128)(2,1)S(1)} %copy-done, f32[128,1024]{1,0:T(8,128)S(1)} %get-tuple-element.13.ql_ref, ...), custom_call_target="tpu_custom_call" | custom-call | flops 67108864 | bytes 524288 | tf_op jit(solution)/shard_map/pallas_call | solution.py:269
  20.3 0.2 collective-permute-done.7.state_ref
  20.5 0.9 %shard_map.71 = (bf16[128,1024]{1,0:T(8,128)(2,1)}, bf16[128,256]{1,0:T(8,128)(2,1)}, bf16[128,256]{1,0:T(8,128)(2,1)}) custom-call(bf16[128,256]{1,0:T(8,128)(2,1)S(1)} %copy-done.2, bf16[128,256]{1,0:T(8,128)(2,1)S(1)} %copy-done.3, bf16[128,1024]{1,0:T(8,128)(2,1)S(1)} %copy-done, ...), custom_call_target="tpu_custom_call", output_to_operand_aliasing={{0}: (7, {}), {1}: (8, {}), {2}: (9, {})} | custom-call | flops 67108864 | bytes 524288 | tf_op jit(solution)/shard_map/pallas_call | solution.py:269
  (11 shorter events, 0.2 us)
Async XLA Ops:
  0.6 1.9 %copy-start.2 = (bf16[128,256]{1,0:T(8,128)(2,1)S(1)}, bf16[128,256]{1,0:T(8,128)(2,1)}, u32[]{:S(2)}) copy-start(bf16[128,256]{1,0:T(8,128)(2,1)} %k_ref.7) | copy-start | bytes 196612
  0.6 1.9 %copy-start.3 = (bf16[128,256]{1,0:T(8,128)(2,1)S(1)}, bf16[128,256]{1,0:T(8,128)(2,1)}, u32[]{:S(2)}) copy-start(bf16[128,256]{1,0:T(8,128)(2,1)} %v_ref.7) | copy-start | bytes 196612
  0.7 1.9 %copy-start = (bf16[128,1024]{1,0:T(8,128)(2,1)S(1)}, bf16[128,1024]{1,0:T(8,128)(2,1)}, u32[]{:S(2)}) copy-start(bf16[128,1024]{1,0:T(8,128)(2,1)} %o_ref.7) | copy-start | bytes 786436
  0.7 1.9 %copy-start.1 = (bf16[128,1024]{1,0:T(8,128)(2,1)S(1)}, bf16[128,1024]{1,0:T(8,128)(2,1)}, u32[]{:S(2)}) copy-start(bf16[128,1024]{1,0:T(8,128)(2,1)} %q_ref.3) | copy-start | bytes 786436
  2.1 1.4 %collective-permute-start = (bf16[2,1,128,128]{3,2,1,0:T(8,128)(2,1)S(1)}, bf16[2,1,128,128]{3,2,1,0:T(8,128)(2,1)S(1)}, u32[]{:S(2)}, u32[]{:S(2)}) collective-permute-start(bf16[2,1,128,128]{3,2,1,0:T(8,128)(2,1)S(1)} %shard_map.68), channel_id=1, source_target_pairs={{0,1},{1,0},{2,3},{3,2},{4,5},{5,4},{6,7},{7,6},{8,9},{9,8},{10,11... | collective-permute-start | bytes 196616 | tf_op jit(solution)/shard_map/ppermute | solution.py:189
  3.5 6.3 %collective-permute-start.3 = (bf16[2,1,128,128]{3,2,1,0:T(8,128)(2,1)S(1)}, bf16[2,1,128,128]{3,2,1,0:T(8,128)(2,1)S(1)}, u32[]{:S(2)}, u32[]{:S(2)}) collective-permute-start(bf16[2,1,128,128]{3,2,1,0:T(8,128)(2,1)S(1)} %add_convert_fusion.1), channel_id=1, source_target_pairs={{0,6},{1,7},{2,4},{3,5},{4,2},{5,3},{6,0},{7,1},{8,14},{9,15},{10,... | collective-permute-start | bytes 196616 | tf_op jit(solution)/shard_map/ppermute | solution.py:201
  7.4 4.3 %collective-permute-start.2 = (bf16[2,1,128,128]{3,2,1,0:T(8,128)(2,1)S(1)}, bf16[2,1,128,128]{3,2,1,0:T(8,128)(2,1)S(1)}, u32[]{:S(2)}, u32[]{:S(2)}) collective-permute-start(bf16[2,1,128,128]{3,2,1,0:T(8,128)(2,1)S(1)} %add_convert_fusion.1), channel_id=1, source_target_pairs={{0,5},{1,4},{2,7},{3,6},{4,1},{5,0},{6,3},{7,2},{8,13},{9,12},{10,... | collective-permute-start | bytes 196616 | tf_op jit(solution)/shard_map/ppermute | solution.py:201
  7.4 4.3 %collective-permute-start.1 = (bf16[2,1,128,128]{3,2,1,0:T(8,128)(2,1)S(1)}, bf16[2,1,128,128]{3,2,1,0:T(8,128)(2,1)S(1)}, u32[]{:S(2)}, u32[]{:S(2)}) collective-permute-start(bf16[2,1,128,128]{3,2,1,0:T(8,128)(2,1)S(1)} %add_convert_fusion.1), channel_id=1, source_target_pairs={{0,3},{1,2},{2,1},{3,0},{4,7},{5,6},{6,5},{7,4},{8,11},{9,10},{10,... | collective-permute-start | bytes 196616 | tf_op jit(solution)/shard_map/ppermute | solution.py:201
  11.8 5.2 %collective-permute-start.6 = (bf16[1,128,128]{2,1,0:T(8,128)(2,1)S(1)}, bf16[1,128,128]{2,1,0:T(8,128)(2,1)S(1)}, u32[]{:S(2)}, u32[]{:S(2)}) collective-permute-start(bf16[1,128,128]{2,1,0:T(8,128)(2,1)S(1)} %get-tuple-element.19), channel_id=1, source_target_pairs={{0,9},{1,8},{2,11},{3,10},{4,13},{5,12},{6,15},{7,14},{8,17},{9,16... | collective-permute-start | bytes 98312 | tf_op jit(solution)/shard_map/ppermute | solution.py:214
  13.1 4.9 %collective-permute-start.5 = (bf16[1,128,128]{2,1,0:T(8,128)(2,1)S(1)}, bf16[1,128,128]{2,1,0:T(8,128)(2,1)S(1)}, u32[]{:S(2)}, u32[]{:S(2)}) collective-permute-start(bf16[1,128,128]{2,1,0:T(8,128)(2,1)S(1)} %get-tuple-element.18), channel_id=1, source_target_pairs={{0,16},{1,17},{2,18},{3,19},{4,20},{5,21},{6,22},{7,23},{8,24},{9,... | collective-permute-start | bytes 98312 | tf_op jit(solution)/shard_map/ppermute | solution.py:214
  15.7 3.4 %collective-permute-start.4 = (bf16[1,128,128]{2,1,0:T(8,128)(2,1)S(1)}, bf16[1,128,128]{2,1,0:T(8,128)(2,1)S(1)}, u32[]{:S(2)}, u32[]{:S(2)}) collective-permute-start(bf16[1,128,128]{2,1,0:T(8,128)(2,1)S(1)} %get-tuple-element.17), channel_id=1, source_target_pairs={{0,25},{1,24},{2,27},{3,26},{4,29},{5,28},{6,31},{7,30},{8,1},{9,0... | collective-permute-start | bytes 98312 | tf_op jit(solution)/shard_map/ppermute | solution.py:214
  19.2 1.3 %collective-permute-start.7 = (bf16[2,1,128,128]{3,2,1,0:T(8,128)(2,1)S(1)}, bf16[2,1,128,128]{3,2,1,0:T(8,128)(2,1)S(1)}, u32[]{:S(2)}, u32[]{:S(2)}) collective-permute-start(bf16[2,1,128,128]{3,2,1,0:T(8,128)(2,1)S(1)} %pad_maximum_fusion), channel_id=1, source_target_pairs={{0,1},{1,0},{2,3},{3,2},{4,5},{5,4},{6,7},{7,6},{8,9},{9,8},{10,11... | collective-permute-start | bytes 196616 | tf_op jit(solution)/shard_map/ppermute | solution.py:223

commit v6 on v5

--- a/solution.py
+++ b/solution.py
@@ -41,13 +41,17 @@
     return 1.0 / jnp.sqrt((HD * (positions + 1)).astype(F32))
 
 
-def half_states(k_ref, v_ref, o_ref, q_ref, out_ref):
+def half_states(k_ref, v_ref, o_ref, q_ref, out_ref, copies=()):
     tokens = q_ref.shape[0]
     half = k_ref.shape[1] // HD
     group = q_ref.shape[1] // k_ref.shape[1]
     scale = row_scale(tokens, (tokens, HD), 0)
+    for copy in copies[:2]:
+        copy.wait()
     for g in range(half):
         out_ref[0, g] = dot(v_ref[columns(g)], k_ref[columns(g)], TN).astype(BF16)
+    for copy in copies[2:]:
+        copy.wait()
     for g in range(half):
         grad = jnp.zeros((HD, HD), F32)
         for h in range(g * group, (g + 1) * group):
@@ -69,9 +73,7 @@
     ]
     for copy in copies:
         copy.start(priority=1)
-    for copy in copies:
-        copy.wait()
-    half_states(k_ref, v_ref, o_ref, q_ref, out_ref)
+    half_states(k_ref, v_ref, o_ref, q_ref, out_ref, copies)
 
 
 def keep_kernel(k_ref, v_ref, o_ref, q_ref, out_ref):
@@ -79,7 +81,9 @@
     half_states(*[half_columns(ref, side) for ref in (k_ref, v_ref, o_ref, q_ref)], out_ref)
 
 
-def local_kernel(q_ref, k_ref, v_ref, o_ref, keep_ref, got_ref, qg_ref, kg_ref, vg_ref, total_ref):
+def local_kernel(
+    q_ref, k_ref, v_ref, o_ref, keep_ref, got_ref, qg_ref, kg_ref, vg_ref, scaled_ref, total_ref
+):
     total_ref[...] = keep_ref[...].astype(F32) + got_ref[...].astype(F32)
     tokens = q_ref.shape[0]
     kv = k_ref.shape[1] // HD
@@ -99,6 +103,7 @@
             query = q_ref[columns(h)]
             cot = o_ref[columns(h)]
             scaled = (scale * cot.astype(F32)).astype(BF16)
+            scaled_ref[columns(h)] = scaled
             backward = jnp.where(causal, dot(scaled, value, NT), 0.0).astype(BF16)
             backward_t = jnp.where(causal_t, dot(value, scaled, NT), 0.0).astype(BF16)
             forward_t = jnp.where(causal_t, scale_row * dot(key, query, NT), 0.0).astype(BF16)
@@ -109,38 +114,37 @@
         vg_ref[columns(g)] = value_grad
 
 
-def finish_kernel(mine, k_ref, v_ref, o_ref, ql_ref, kl_ref, vl_ref, state_ref, *refs):
+def finish_kernel(mine, k_ref, v_ref, scaled_ref, ql_ref, kl_ref, vl_ref, state_ref, *refs):
     qg_hbm, kg_hbm, vg_hbm, qg_ref, kg_ref, vg_ref, sems = refs[-7:]
-    tokens = o_ref.shape[0]
+    tokens = scaled_ref.shape[0]
     kv = k_ref.shape[1] // HD
-    width = o_ref.shape[1] // kv
+    width = scaled_ref.shape[1] // kv
     group = width // HD
     half = kv // 2
     side = side_of(device_index(), lax.axis_size(SEQ) * lax.axis_size(HEAD))
-    scale = row_scale(tokens, (tokens, HD), 0)
 
     def finish(part):
         copies = []
 
-        def send(ref, hbm, size):
-            at = (slice(None), slice(part * half * size, (part + 1) * half * size))
+        def send(ref, hbm, low, size):
+            at = (slice(None), slice(low, low + size))
             copies.append(pltpu.make_async_copy(ref.at[at], hbm.at[at], sems.at[len(copies)]))
             copies[-1].start()
 
         for g in range(part * half, (part + 1) * half):
             prior = state_ref[0, g % half]
             for h in range(g * group, (g + 1) * group):
-                scaled = (scale * o_ref[columns(h)].astype(F32)).astype(BF16)
+                scaled = scaled_ref[columns(h)]
                 qg_ref[columns(h)] = (ql_ref[columns(h)] + dot(scaled, prior, NN)).astype(BF16)
-        send(qg_ref, qg_hbm, width)
+        send(qg_ref, qg_hbm, part * half * width, half * width)
         for g in range(part * half, (part + 1) * half):
             future = state_ref[1, g % half]
             key_grad = kl_ref[columns(g)] + dot(v_ref[columns(g)], future, NN)
             value_grad = vl_ref[columns(g)] + dot(k_ref[columns(g)], future, NT)
             kg_ref[columns(g)] = key_grad.astype(BF16)
             vg_ref[columns(g)] = value_grad.astype(BF16)
-        send(kg_ref, kg_hbm, HD)
-        send(vg_ref, vg_hbm, HD)
+        send(kg_ref, kg_hbm, part * half * HD, half * HD)
+        send(vg_ref, vg_hbm, part * half * HD, half * HD)
         for copy in copies:
             copy.wait()
 
@@ -255,15 +259,16 @@
 
     local_terms = pl.pallas_call(
         local_kernel,
-        out_shape=tuple(jax.ShapeDtypeStruct(x.shape, F32) for x in (queries, keys, values, send)),
+        out_shape=tuple(jax.ShapeDtypeStruct(x.shape, F32) for x in (queries, keys, values))
+        + (jax.ShapeDtypeStruct(out_grad.shape, BF16), jax.ShapeDtypeStruct(shape, F32)),
         in_specs=[vmem] * 6,
-        out_specs=[vmem] * 4,
+        out_specs=[vmem] * 5,
         cost_estimate=pl.CostEstimate(
             flops=12 * tokens * tokens * wide, bytes_accessed=12 * tokens * wide, transcendentals=0
         ),
         compiler_params=pltpu.CompilerParams(vmem_limit_bytes=24 * MIB),
     )
-    local, mine, other = carry_states(keep, send, functools.partial(local_terms, *inputs))
+    (*local, scaled), mine, other = carry_states(keep, send, functools.partial(local_terms, *inputs))
 
     def finish(mine, state, *written):
         return pl.pallas_call(
@@ -278,7 +283,7 @@
                 flops=4 * tokens * HD * wide, bytes_accessed=4 * tokens * wide, transcendentals=0
             ),
             compiler_params=pltpu.CompilerParams(vmem_limit_bytes=24 * MIB),
-        )(keys, values, out_grad, *local, state, *written)
+        )(keys, values, scaled, *local, state, *written)
 
     return finish(False, other, *finish(True, mine))
 

time: 21.6 us -> 21.5 us (level)
  no operation moved by 1% of the time
where the time goes in v6:
time: 21.5 us; the launch traced here: 21.3 us
  starting transfers between devices  9.99 us (46%)
  waiting for transfers between devices  5.33 us (25%)
  Pallas kernels  4.95 us (23%)
  between operations  0.81 us (4%)
  other arithmetic  0.24 us (1%)
    ppermute x6, starting transfers between devices, carry_states(): lax.ppermute(message, DEVICES, [(i, target(i, size, low, move)) for i in...  9.26 us
    ppermute x6, waiting for transfers between devices, carry_states(): lax.ppermute(message, DEVICES, [(i, target(i, size, low, move)) for i in...  4.51 us
    pallas_call x2, Pallas kernels, finish(): pl.pallas_call(functools.partial(finish_kernel, mine), out_shape=tuple((j...  1.77 us
    pallas_call x1, Pallas kernels, carry_states(): *local, total = local_terms(keep, got)  1.57 us
    pallas_call x1, Pallas kernels, body(): pl.pallas_call(send_kernel, out_shape=jax.ShapeDtypeStruct(shape, BF16),...  1.35 us
    ppermute x1, waiting for transfers between devices, carry_states(): got = lax.ppermute(send, DEVICES, swap)  0.62 us
    ppermute x1, starting transfers between devices, carry_states(): got = lax.ppermute(send, DEVICES, swap)  0.52 us
  transfers between devices with their start and end apart: 8, of which 6 were waited for; matrix products, arithmetic and copies ran while one was open for 0% of the time, Pallas kernels for 13%

profile of v6, /device:TPU:0, one launch (start us, length us, event | category | flops | bytes accessed | tf_op | source)
XLA Modules:
  0.0 21.3 jit_solution(16310814080707194879)
XLA Ops:
  0.6 0.0 copy-start.2
  0.6 0.0 copy-start.3
  0.7 0.0 copy-start
  0.7 0.0 copy-start.1
  0.7 1.3 %shard_map.68 = bf16[2,1,128,128]{3,2,1,0:T(8,128)(2,1)S(1)} custom-call(bf16[128,256]{1,0:T(8,128)(2,1)} %k_ref.7, bf16[128,256]{1,0:T(8,128)(2,1)} %v_ref.7, bf16[128,1024]{1,0:T(8,128)(2,1)} %o_ref.3, bf16[128,1024]{1,0:T(8,128)(2,1)} %q_ref.3), custom_call_target="tpu_custom_call" | custom-call | tf_op jit(solution)/shard_map/pallas_call | solution.py:239
  2.0 0.5 %collective-permute-start = (bf16[2,1,128,128]{3,2,1,0:T(8,128)(2,1)S(1)}, bf16[2,1,128,128]{3,2,1,0:T(8,128)(2,1)S(1)}, u32[]{:S(2)}, u32[]{:S(2)}) collective-permute-start(bf16[2,1,128,128]{3,2,1,0:T(8,128)(2,1)S(1)} %shard_map.68), channel_id=1, source_target_pairs={{0,1},{1,0},{2,3},{3,2},{4,5},{5,4},{6,7},{7,6},{8,9},{9,8},{10,11... | collective-permute-start | bytes 196616 | tf_op jit(solution)/shard_map/ppermute | solution.py:193
  2.5 0.0 copy-done.2
  2.5 0.0 copy-done.3
  2.6 0.0 copy-done
  2.6 0.0 copy-done.1
  2.6 0.3 %shard_map.67.keep_ref = bf16[2,1,128,128]{3,2,1,0:T(8,128)(2,1)S(1)} custom-call(bf16[128,256]{1,0:T(8,128)(2,1)S(1)} %copy-done.2, bf16[128,256]{1,0:T(8,128)(2,1)S(1)} %copy-done.3, bf16[128,1024]{1,0:T(8,128)(2,1)S(1)} %copy-done.1, bf16[128,1024]{1,0:T(8,128)(2,1)S(1)} %copy-done), custom_call_target="tpu_custom_call" | custom-call | flops 33554432 | bytes 524288 | tf_op jit(solution)/shard_map/pallas_call | solution.py:249
  2.8 0.6 %collective-permute-done.got_ref = bf16[2,1,128,128]{3,2,1,0:T(8,128)(2,1)S(1)} collective-permute-done((bf16[2,1,128,128]{3,2,1,0:T(8,128)(2,1)S(1)}, bf16[2,1,128,128]{3,2,1,0:T(8,128)(2,1)S(1)}, u32[]{:S(2)}, u32[]{:S(2)}) %collective-permute-start) | collective-permute-done | bytes 65568 | tf_op jit(solution)/shard_map/ppermute | solution.py:193
  3.5 3.9 %collective-permute-start.3 = (bf16[2,1,128,128]{3,2,1,0:T(8,128)(2,1)S(1)}, bf16[2,1,128,128]{3,2,1,0:T(8,128)(2,1)S(1)}, u32[]{:S(2)}, u32[]{:S(2)}) collective-permute-start(bf16[2,1,128,128]{3,2,1,0:T(8,128)(2,1)S(1)} %add_convert_fusion.1), channel_id=1, source_target_pairs={{0,6},{1,7},{2,4},{3,5},{4,2},{5,3},{6,0},{7,1},{8,14},{9,15},{10,... | collective-permute-start | bytes 196616 | tf_op jit(solution)/shard_map/ppermute | solution.py:205
  7.3 0.0 collective-permute-start.2
  7.3 0.4 %collective-permute-start.1 = (bf16[2,1,128,128]{3,2,1,0:T(8,128)(2,1)S(1)}, bf16[2,1,128,128]{3,2,1,0:T(8,128)(2,1)S(1)}, u32[]{:S(2)}, u32[]{:S(2)}) collective-permute-start(bf16[2,1,128,128]{3,2,1,0:T(8,128)(2,1)S(1)} %add_convert_fusion.1), channel_id=1, source_target_pairs={{0,3},{1,2},{2,1},{3,0},{4,7},{5,6},{6,5},{7,4},{8,11},{9,10},{10,... | collective-permute-start | bytes 196616 | tf_op jit(solution)/shard_map/ppermute | solution.py:205
  7.7 1.6 %shard_map.69 = (f32[128,1024]{1,0:T(8,128)S(1)}, f32[128,256]{1,0:T(8,128)S(1)}, f32[128,256]{1,0:T(8,128)S(1)}, bf16[128,1024]{1,0:T(8,128)(2,1)S(1)}, f32[2,1,128,128]{3,2,1,0:T(8,128)S(1)}) custom-call(bf16[128,1024]{1,0:T(8,128)(2,1)S(1)} %copy-done, bf16[128,256]{1,0:T(8,128)(2,1)S(1)} %copy-done.2, bf16[128,256]{1,0:T(8,128)(2,1)S(1)} %copy-done.3, ...), custom_call_target="tpu_custom_call" | custom-call | flops 201326592 | bytes 1572864 | tf_op jit(solution)/shard_map/pallas_call | solution.py:195
  9.3 0.5 %collective-permute-done.3 = bf16[2,1,128,128]{3,2,1,0:T(8,128)(2,1)S(1)} collective-permute-done((bf16[2,1,128,128]{3,2,1,0:T(8,128)(2,1)S(1)}, bf16[2,1,128,128]{3,2,1,0:T(8,128)(2,1)S(1)}, u32[]{:S(2)}, u32[]{:S(2)}) %collective-permute-start.3) | collective-permute-done | bytes 65568 | tf_op jit(solution)/shard_map/ppermute | solution.py:205
  9.8 1.8 %collective-permute-done.2 = bf16[2,1,128,128]{3,2,1,0:T(8,128)(2,1)S(1)} collective-permute-done((bf16[2,1,128,128]{3,2,1,0:T(8,128)(2,1)S(1)}, bf16[2,1,128,128]{3,2,1,0:T(8,128)(2,1)S(1)}, u32[]{:S(2)}, u32[]{:S(2)}) %collective-permute-start.2) | collective-permute-done | bytes 65568 | tf_op jit(solution)/shard_map/ppermute | solution.py:205
  11.7 0.0 collective-permute-done.1
  11.7 1.3 %collective-permute-start.6 = (bf16[1,128,128]{2,1,0:T(8,128)(2,1)S(1)}, bf16[1,128,128]{2,1,0:T(8,128)(2,1)S(1)}, u32[]{:S(2)}, u32[]{:S(2)}) collective-permute-start(bf16[1,128,128]{2,1,0:T(8,128)(2,1)S(1)} %get-tuple-element.21), channel_id=1, source_target_pairs={{0,9},{1,8},{2,11},{3,10},{4,13},{5,12},{6,15},{7,14},{8,17},{9,16... | collective-permute-start | bytes 98312 | tf_op jit(solution)/shard_map/ppermute | solution.py:218
  13.1 2.6 %collective-permute-start.5 = (bf16[1,128,128]{2,1,0:T(8,128)(2,1)S(1)}, bf16[1,128,128]{2,1,0:T(8,128)(2,1)S(1)}, u32[]{:S(2)}, u32[]{:S(2)}) collective-permute-start(bf16[1,128,128]{2,1,0:T(8,128)(2,1)S(1)} %get-tuple-element.20), channel_id=1, source_target_pairs={{0,16},{1,17},{2,18},{3,19},{4,20},{5,21},{6,22},{7,23},{8,24},{9,... | collective-permute-start | bytes 98312 | tf_op jit(solution)/shard_map/ppermute | solution.py:218
  15.7 1.1 %collective-permute-start.4 = (bf16[1,128,128]{2,1,0:T(8,128)(2,1)S(1)}, bf16[1,128,128]{2,1,0:T(8,128)(2,1)S(1)}, u32[]{:S(2)}, u32[]{:S(2)}) collective-permute-start(bf16[1,128,128]{2,1,0:T(8,128)(2,1)S(1)} %get-tuple-element.19), channel_id=1, source_target_pairs={{0,25},{1,24},{2,27},{3,26},{4,29},{5,28},{6,31},{7,30},{8,1},{9,0... | collective-permute-start | bytes 98312 | tf_op jit(solution)/shard_map/ppermute | solution.py:218
  16.9 0.0 collective-permute-done.6
  16.9 1.1 %collective-permute-done.5 = bf16[1,128,128]{2,1,0:T(8,128)(2,1)S(1)} collective-permute-done((bf16[1,128,128]{2,1,0:T(8,128)(2,1)S(1)}, bf16[1,128,128]{2,1,0:T(8,128)(2,1)S(1)}, u32[]{:S(2)}, u32[]{:S(2)}) %collective-permute-start.5) | collective-permute-done | bytes 32800 | tf_op jit(solution)/shard_map/ppermute | solution.py:218
  18.0 1.0 %collective-permute-done.4 = bf16[1,128,128]{2,1,0:T(8,128)(2,1)S(1)} collective-permute-done((bf16[1,128,128]{2,1,0:T(8,128)(2,1)S(1)}, bf16[1,128,128]{2,1,0:T(8,128)(2,1)S(1)}, u32[]{:S(2)}, u32[]{:S(2)}) %collective-permute-start.4) | collective-permute-done | bytes 32800 | tf_op jit(solution)/shard_map/ppermute | solution.py:218
  19.0 0.1 fusion.26
  19.2 0.2 %collective-permute-start.7 = (bf16[2,1,128,128]{3,2,1,0:T(8,128)(2,1)S(1)}, bf16[2,1,128,128]{3,2,1,0:T(8,128)(2,1)S(1)}, u32[]{:S(2)}, u32[]{:S(2)}) collective-permute-start(bf16[2,1,128,128]{3,2,1,0:T(8,128)(2,1)S(1)} %pad_maximum_fusion), channel_id=1, source_target_pairs={{0,1},{1,0},{2,3},{3,2},{4,5},{5,4},{6,7},{7,6},{8,9},{9,8},{10,11... | collective-permute-start | bytes 196616 | tf_op jit(solution)/shard_map/ppermute | solution.py:227
  19.4 0.9 %shard_map.70 = (bf16[128,1024]{1,0:T(8,128)(2,1)}, bf16[128,256]{1,0:T(8,128)(2,1)}, bf16[128,256]{1,0:T(8,128)(2,1)}) custom-call(bf16[128,256]{1,0:T(8,128)(2,1)S(1)} %copy-done.2, bf16[128,256]{1,0:T(8,128)(2,1)S(1)} %copy-done.3, bf16[128,1024]{1,0:T(8,128)(2,1)S(1)} %get-tuple-element.14.scaled_ref, f32[128,1024]{1,0:T(8,128)S(1)} %get-tuple-element.15.ql_ref, ...), custom_call_target="tpu_custom_call" | custom-call | flops 67108864 | bytes 524288 | tf_op jit(solution)/shard_map/pallas_call | solution.py:274
  20.3 0.2 collective-permute-done.7.state_ref
  20.5 0.9 %shard_map.71 = (bf16[128,1024]{1,0:T(8,128)(2,1)}, bf16[128,256]{1,0:T(8,128)(2,1)}, bf16[128,256]{1,0:T(8,128)(2,1)}) custom-call(bf16[128,256]{1,0:T(8,128)(2,1)S(1)} %copy-done.2, bf16[128,256]{1,0:T(8,128)(2,1)S(1)} %copy-done.3, bf16[128,1024]{1,0:T(8,128)(2,1)S(1)} %get-tuple-element.14.scaled_ref, ...), custom_call_target="tpu_custom_call", output_to_operand_aliasing={{0}: (7, {}), {1}: (8, {}), {2}: (9, {})} | custom-call | flops 67108864 | bytes 524288 | tf_op jit(solution)/shard_map/pallas_call | solution.py:274
  (11 shorter events, 0.2 us)
Async XLA Ops:
  0.6 1.9 %copy-start.2 = (bf16[128,256]{1,0:T(8,128)(2,1)S(1)}, bf16[128,256]{1,0:T(8,128)(2,1)}, u32[]{:S(2)}) copy-start(bf16[128,256]{1,0:T(8,128)(2,1)} %k_ref.7) | copy-start | bytes 196612
  0.6 1.9 %copy-start.3 = (bf16[128,256]{1,0:T(8,128)(2,1)S(1)}, bf16[128,256]{1,0:T(8,128)(2,1)}, u32[]{:S(2)}) copy-start(bf16[128,256]{1,0:T(8,128)(2,1)} %v_ref.7) | copy-start | bytes 196612
  0.7 1.9 %copy-start = (bf16[128,1024]{1,0:T(8,128)(2,1)S(1)}, bf16[128,1024]{1,0:T(8,128)(2,1)}, u32[]{:S(2)}) copy-start(bf16[128,1024]{1,0:T(8,128)(2,1)} %q_ref.3) | copy-start | bytes 786436
  0.7 1.9 %copy-start.1 = (bf16[128,1024]{1,0:T(8,128)(2,1)S(1)}, bf16[128,1024]{1,0:T(8,128)(2,1)}, u32[]{:S(2)}) copy-start(bf16[128,1024]{1,0:T(8,128)(2,1)} %o_ref.3) | copy-start | bytes 786436
  2.0 1.4 %collective-permute-start = (bf16[2,1,128,128]{3,2,1,0:T(8,128)(2,1)S(1)}, bf16[2,1,128,128]{3,2,1,0:T(8,128)(2,1)S(1)}, u32[]{:S(2)}, u32[]{:S(2)}) collective-permute-start(bf16[2,1,128,128]{3,2,1,0:T(8,128)(2,1)S(1)} %shard_map.68), channel_id=1, source_target_pairs={{0,1},{1,0},{2,3},{3,2},{4,5},{5,4},{6,7},{7,6},{8,9},{9,8},{10,11... | collective-permute-start | bytes 196616 | tf_op jit(solution)/shard_map/ppermute | solution.py:193
  3.5 6.3 %collective-permute-start.3 = (bf16[2,1,128,128]{3,2,1,0:T(8,128)(2,1)S(1)}, bf16[2,1,128,128]{3,2,1,0:T(8,128)(2,1)S(1)}, u32[]{:S(2)}, u32[]{:S(2)}) collective-permute-start(bf16[2,1,128,128]{3,2,1,0:T(8,128)(2,1)S(1)} %add_convert_fusion.1), channel_id=1, source_target_pairs={{0,6},{1,7},{2,4},{3,5},{4,2},{5,3},{6,0},{7,1},{8,14},{9,15},{10,... | collective-permute-start | bytes 196616 | tf_op jit(solution)/shard_map/ppermute | solution.py:205
  7.3 4.3 %collective-permute-start.2 = (bf16[2,1,128,128]{3,2,1,0:T(8,128)(2,1)S(1)}, bf16[2,1,128,128]{3,2,1,0:T(8,128)(2,1)S(1)}, u32[]{:S(2)}, u32[]{:S(2)}) collective-permute-start(bf16[2,1,128,128]{3,2,1,0:T(8,128)(2,1)S(1)} %add_convert_fusion.1), channel_id=1, source_target_pairs={{0,5},{1,4},{2,7},{3,6},{4,1},{5,0},{6,3},{7,2},{8,13},{9,12},{10,... | collective-permute-start | bytes 196616 | tf_op jit(solution)/shard_map/ppermute | solution.py:205
  7.3 4.3 %collective-permute-start.1 = (bf16[2,1,128,128]{3,2,1,0:T(8,128)(2,1)S(1)}, bf16[2,1,128,128]{3,2,1,0:T(8,128)(2,1)S(1)}, u32[]{:S(2)}, u32[]{:S(2)}) collective-permute-start(bf16[2,1,128,128]{3,2,1,0:T(8,128)(2,1)S(1)} %add_convert_fusion.1), channel_id=1, source_target_pairs={{0,3},{1,2},{2,1},{3,0},{4,7},{5,6},{6,5},{7,4},{8,11},{9,10},{10,... | collective-permute-start | bytes 196616 | tf_op jit(solution)/shard_map/ppermute | solution.py:205
  11.7 5.2 %collective-permute-start.6 = (bf16[1,128,128]{2,1,0:T(8,128)(2,1)S(1)}, bf16[1,128,128]{2,1,0:T(8,128)(2,1)S(1)}, u32[]{:S(2)}, u32[]{:S(2)}) collective-permute-start(bf16[1,128,128]{2,1,0:T(8,128)(2,1)S(1)} %get-tuple-element.21), channel_id=1, source_target_pairs={{0,9},{1,8},{2,11},{3,10},{4,13},{5,12},{6,15},{7,14},{8,17},{9,16... | collective-permute-start | bytes 98312 | tf_op jit(solution)/shard_map/ppermute | solution.py:218
  13.1 4.9 %collective-permute-start.5 = (bf16[1,128,128]{2,1,0:T(8,128)(2,1)S(1)}, bf16[1,128,128]{2,1,0:T(8,128)(2,1)S(1)}, u32[]{:S(2)}, u32[]{:S(2)}) collective-permute-start(bf16[1,128,128]{2,1,0:T(8,128)(2,1)S(1)} %get-tuple-element.20), channel_id=1, source_target_pairs={{0,16},{1,17},{2,18},{3,19},{4,20},{5,21},{6,22},{7,23},{8,24},{9,... | collective-permute-start | bytes 98312 | tf_op jit(solution)/shard_map/ppermute | solution.py:218
  15.7 3.4 %collective-permute-start.4 = (bf16[1,128,128]{2,1,0:T(8,128)(2,1)S(1)}, bf16[1,128,128]{2,1,0:T(8,128)(2,1)S(1)}, u32[]{:S(2)}, u32[]{:S(2)}) collective-permute-start(bf16[1,128,128]{2,1,0:T(8,128)(2,1)S(1)} %get-tuple-element.19), channel_id=1, source_target_pairs={{0,25},{1,24},{2,27},{3,26},{4,29},{5,28},{6,31},{7,30},{8,1},{9,0... | collective-permute-start | bytes 98312 | tf_op jit(solution)/shard_map/ppermute | solution.py:218
  19.2 1.3 %collective-permute-start.7 = (bf16[2,1,128,128]{3,2,1,0:T(8,128)(2,1)S(1)}, bf16[2,1,128,128]{3,2,1,0:T(8,128)(2,1)S(1)}, u32[]{:S(2)}, u32[]{:S(2)}) collective-permute-start(bf16[2,1,128,128]{3,2,1,0:T(8,128)(2,1)S(1)} %pad_maximum_fusion), channel_id=1, source_target_pairs={{0,1},{1,0},{2,3},{3,2},{4,5},{5,4},{6,7},{7,6},{8,9},{9,8},{10,11... | collective-permute-start | bytes 196616 | tf_op jit(solution)/shard_map/ppermute | solution.py:227

commit v7 on v6

v7 whole, which is shorter than its diff:
```python
import functools

import jax
import jax.numpy as jnp
from jax import lax
from jax.experimental import pallas as pl
from jax.experimental.pallas import tpu as pltpu
from jax.sharding import PartitionSpec as P

HD = 128
SEQ = "seq"
HEAD = "head"
DEVICES = (SEQ, HEAD)
LOW_MOVES = ((1, 0, 3, 2), (3, 2, 1, 0), (2, 3, 0, 1)), ((3, 2, 1, 0), (2, 3, 0, 1), (1, 0, 3, 2))
TOP_MOVES = ((1, 2, 3, 0), (2, 3, 0, 1), (3, 0, 1, 2)), ((1, 3, 0, 2), (3, 2, 0, 1), (2, 0, 3, 1))
LOW_ODD = (0, 1, 1, 0)
TOP_ODD = (0, 1, 0, 1)
MIB = 1024 * 1024
BF16 = jnp.bfloat16
F32 = jnp.float32

NN = (((1,), (0,)), ((), ()))
NT = (((1,), (1,)), ((), ()))
TN = (((0,), (0,)), ((), ()))


def dot(left, right, dims):
    return lax.dot_general(left, right, dims, preferred_element_type=F32)


def columns(index):
    return (slice(None), slice(index * HD, (index + 1) * HD))


def device_index():
    return lax.axis_index(SEQ) * lax.axis_size(HEAD) + lax.axis_index(HEAD)


def row_scale(tokens, shape, axis):
    positions = device_index() * tokens + lax.broadcasted_iota(jnp.int32, shape, axis)
    return 1.0 / jnp.sqrt((HD * (positions + 1)).astype(F32))


def prior_terms(k_ref, v_ref, out_ref):
    for g in range(out_ref.shape[0]):
        out_ref[g] = dot(v_ref[columns(g)], k_ref[columns(g)], TN).astype(BF16)


def future_terms(o_ref, q_ref, out_ref):
    tokens = q_ref.shape[0]
    kv = out_ref.shape[0]
    group = q_ref.shape[1] // HD // kv
    scale = row_scale(tokens, (tokens, HD), 0)
    for g in range(kv):
        grad = jnp.zeros((HD, HD), F32)
        for h in range(g * group, (g + 1) * group):
            scaled = (scale * o_ref[columns(h)].astype(F32)).astype(BF16)
            grad = grad + dot(scaled, q_ref[columns(h)], TN)
        out_ref[g] = grad.astype(BF16)


def my_side():
    return side_of(device_index(), lax.axis_size(SEQ) * lax.axis_size(HEAD))


def fetch(pairs, sems):
    copies = [pltpu.make_async_copy(source, place, sems.at[i]) for i, (source, place) in enumerate(pairs)]
    for copy in copies:
        copy.start(priority=1)
    for copy in copies:
        copy.wait()


def send_kernel(k_hbm, v_hbm, o_hbm, q_hbm, out_ref, k_ref, v_ref, o_ref, q_ref, sems):
    side = my_side()

    @pl.when(side == 1)
    def _():
        fetch([(o_hbm, o_ref), (q_hbm, q_ref)], sems)
        future_terms(o_ref, q_ref, out_ref)

    @pl.when(side == 0)
    def _():
        fetch([(k_hbm, k_ref), (v_hbm, v_ref)], sems)
        prior_terms(k_ref, v_ref, out_ref)


def keep_kernel(k_ref, v_ref, o_ref, q_ref, out_ref):
    side = my_side()

    @pl.when(side == 1)
    def _():
        prior_terms(k_ref, v_ref, out_ref)

    @pl.when(side == 0)
    def _():
        future_terms(o_ref, q_ref, out_ref)


def local_kernel(
    q_ref, k_ref, v_ref, o_ref, keep_ref, got_ref, qg_ref, kg_ref, vg_ref, scaled_ref, total_ref
):
    total_ref[...] = keep_ref[...].astype(F32) + got_ref[...].astype(F32)
    tokens = q_ref.shape[0]
    kv = k_ref.shape[1] // HD
    group = q_ref.shape[1] // HD // kv
    scale = row_scale(tokens, (tokens, HD), 0)
    scale_row = row_scale(tokens, (HD, tokens), 1)
    rows = lax.broadcasted_iota(jnp.int32, (tokens, tokens), 0)
    cols = lax.broadcasted_iota(jnp.int32, (tokens, tokens), 1)
    causal = rows >= cols
    causal_t = rows <= cols
    for g in range(kv):
        key = k_ref[columns(g)]
        value = v_ref[columns(g)]
        key_grad = jnp.zeros((tokens, HD), F32)
        value_grad = jnp.zeros((tokens, HD), F32)
        for h in range(g * group, (g + 1) * group):
            query = q_ref[columns(h)]
            cot = o_ref[columns(h)]
            scaled = (scale * cot.astype(F32)).astype(BF16)
            scaled_ref[columns(h)] = scaled
            backward = jnp.where(causal, dot(scaled, value, NT), 0.0).astype(BF16)
            backward_t = jnp.where(causal_t, dot(value, scaled, NT), 0.0).astype(BF16)
            forward_t = jnp.where(causal_t, scale_row * dot(key, query, NT), 0.0).astype(BF16)
            qg_ref[columns(h)] = dot(backward, key, NN)
            key_grad = key_grad + dot(backward_t, query, NN)
            value_grad = value_grad + dot(forward_t, cot, NN)
        kg_ref[columns(g)] = key_grad
        vg_ref[columns(g)] = value_grad


def finish_kernel(mine, k_ref, v_ref, scaled_ref, ql_ref, kl_ref, vl_ref, state_ref, *refs):
    qg_hbm, kg_hbm, vg_hbm, qg_ref, kg_ref, vg_ref, sems = refs[-7:]
    kv = k_ref.shape[1] // HD
    width = scaled_ref.shape[1] // kv
    side = my_side()

    def send(ref, hbm, at, sem):
        copy = pltpu.make_async_copy(ref.at[at], hbm.at[at], sems.at[sem])
        copy.start()
        return copy

    @pl.when(side == (1 if mine else 0))
    def _():
        copies = []
        for g in range(kv):
            for h in range(g * width // HD, (g + 1) * width // HD):
                qg_ref[columns(h)] = (
                    ql_ref[columns(h)] + dot(scaled_ref[columns(h)], state_ref[g], NN)
                ).astype(BF16)
            copies.append(send(qg_ref, qg_hbm, (slice(None), slice(g * width, (g + 1) * width)), g))
        for copy in copies:
            copy.wait()

    @pl.when(side == (0 if mine else 1))
    def _():
        for g in range(kv):
            key_grad = kl_ref[columns(g)] + dot(v_ref[columns(g)], state_ref[g], NN)
            value_grad = vl_ref[columns(g)] + dot(k_ref[columns(g)], state_ref[g], NT)
            kg_ref[columns(g)] = key_grad.astype(BF16)
            vg_ref[columns(g)] = value_grad.astype(BF16)
        copies = [send(kg_ref, kg_hbm, (slice(None),), 0), send(vg_ref, vg_hbm, (slice(None),), 1)]
        for copy in copies:
            copy.wait()


def digits(size):
    bits = size.bit_length() - 1
    assert 1 << bits == size
    return [(low, min(2, bits - low)) for low in range(1, bits, 2)]


def tables(size):
    found = []
    for low, width in digits(size):
        moves, odd = (LOW_MOVES, LOW_ODD) if low + width < size.bit_length() - 1 else (TOP_MOVES, TOP_ODD)
        found.append((low, moves, odd) if width == 2 else (low, (((1, 0),),) * 2, (0, 1)))
    return found


def side_of(index, size):
    side = index & 1
    for low, _, odd in tables(size):
        digit = index >> low & len(odd) - 1
        for place in range(len(odd)):
            if odd[place]:
                side = side ^ (digit == place)
    return side


def target(index, size, low, move):
    digit = index >> low & len(move) - 1
    other = index ^ (digit ^ move[digit]) << low
    return other ^ side_of(other, size) ^ side_of(index, size)


def place_among(digit, places):
    found = places[0]
    for place, other in enumerate(places):
        found = jnp.where(digit == place, other, found)
    return found


def new_pairs(moves, n):
    return [all(move[place] != moves[n][place] for move in moves[:n]) for place in range(len(moves[n]))]


def carry_states(send, keep_states, local_terms):
    size = lax.axis_size(SEQ) * lax.axis_size(HEAD)
    index = device_index()
    side = side_of(index, size)
    future = side == 0
    swap = [(i, i ^ 1) for i in range(size)]
    got = lax.ppermute(send, DEVICES, swap)
    keep = keep_states()
    *local, chip = local_terms(keep, got)
    keep = keep.astype(F32)
    got = got.astype(F32)
    own = keep + got
    total = own
    carried = 0.0
    rounds = tables(size)
    for step, ways in enumerate(zip(rounds, rounds[::-1])):
        (future_low, (future_moves, _), _), (prior_low, (_, prior_moves), _) = ways
        future_digit = index >> future_low & len(future_moves[0]) - 1
        prior_digit = index >> prior_low & len(prior_moves[0]) - 1
        messages = []
        for n in range(max(len(future_moves), len(prior_moves))):
            message = total
            if n < len(prior_moves):
                wanted = new_pairs(prior_moves, n)
                earlier = (prior_digit < place_among(prior_digit, prior_moves[n])) & place_among(prior_digit, wanted)
                message = jnp.where(future, total, carried + jnp.where(earlier, own, 0.0))
                if step > 0:
                    message = jnp.where(future | place_among(prior_digit, wanted), message, 0.0)
            messages.append(message.astype(BF16))
        messages = lax.optimization_barrier(tuple(messages))
        if step == 0:
            total = chip
            own = chip
        for n, message in enumerate(messages):
            perm = []
            for i in range(size):
                at = side_of(i, size)
                low, moves = ways[at][0], ways[at][1][at]
                if n < len(moves):
                    perm.append((i, target(i, size, low, moves[n])))
            arrived = lax.ppermute(message, DEVICES, perm).astype(F32)
            wanted = side == 1
            if n < len(future_moves):
                source = [future_moves[n].index(place) for place in range(len(future_moves[n]))]
                new = [new_pairs(future_moves, n)[place] for place in source]
                fresh = place_among(future_digit, new)
                wanted = wanted | (place_among(future_digit, source) > future_digit) & fresh
                total = total + jnp.where(fresh, arrived, 0.0)
            carried = carried + jnp.where(wanted, arrived, 0.0)
    first = index & 1 == 0
    mine = carried + jnp.where(first == future, got, 0.0)
    theirs = carried + jnp.where(first == (side == 1), keep, 0.0)
    return local, mine.astype(BF16), lax.ppermute(theirs.astype(BF16), DEVICES, swap)


def body(queries, keys, values, out_grad):
    kv = keys.shape[1] // HD
    shape = (kv, HD, HD)
    vmem = pl.BlockSpec(memory_space=pltpu.VMEM)
    anywhere = pl.BlockSpec(memory_space=pltpu.HBM)
    inputs = (queries, keys, values, out_grad)
    tokens, wide, narrow = queries.shape[0], queries.shape[1], keys.shape[1]
    ordered = (keys, values, out_grad, queries)
    send = pl.pallas_call(
        send_kernel,
        out_shape=jax.ShapeDtypeStruct(shape, BF16),
        in_specs=[anywhere] * 4,
        out_specs=vmem,
        scratch_shapes=[pltpu.VMEM(x.shape, BF16) for x in ordered] + [pltpu.SemaphoreType.DMA((2,))],
        compiler_params=pltpu.CompilerParams(vmem_limit_bytes=55144 * 1024),
    )(*ordered)

    def keep_states():
        return pl.pallas_call(
            keep_kernel,
            out_shape=jax.ShapeDtypeStruct(shape, BF16),
            in_specs=[vmem] * 4,
            out_specs=vmem,
            cost_estimate=pl.CostEstimate(
                flops=2 * tokens * HD * wide, bytes_accessed=4 * tokens * wide, transcendentals=0
            ),
            compiler_params=pltpu.CompilerParams(vmem_limit_bytes=24 * MIB),
        )(*ordered)

    local_terms = pl.pallas_call(
        local_kernel,
        out_shape=tuple(jax.ShapeDtypeStruct(x.shape, F32) for x in (queries, keys, values))
        + (jax.ShapeDtypeStruct(out_grad.shape, BF16), jax.ShapeDtypeStruct(shape, F32)),
        in_specs=[vmem] * 6,
        out_specs=[vmem] * 5,
        cost_estimate=pl.CostEstimate(
            flops=12 * tokens * tokens * wide, bytes_accessed=12 * tokens * wide, transcendentals=0
        ),
        compiler_params=pltpu.CompilerParams(vmem_limit_bytes=24 * MIB),
    )
    (*local, scaled), mine, other = carry_states(send, keep_states, functools.partial(local_terms, *inputs))

    def finish(mine, state, *written):
        return pl.pallas_call(
            functools.partial(finish_kernel, mine),
            out_shape=tuple(jax.ShapeDtypeStruct(x.shape, BF16) for x in (queries, keys, values)),
            in_specs=[vmem] * 7 + [anywhere] * len(written),
            out_specs=[anywhere] * 3,
            scratch_shapes=[pltpu.VMEM(x.shape, BF16) for x in (queries, keys, values)]
            + [pltpu.SemaphoreType.DMA((kv,))],
            input_output_aliases={7 + i: i for i in range(len(written))},
            cost_estimate=pl.CostEstimate(
                flops=4 * tokens * HD * wide, bytes_accessed=4 * tokens * wide, transcendentals=0
            ),
            compiler_params=pltpu.CompilerParams(vmem_limit_bytes=24 * MIB),
        )(keys, values, scaled, *local, state, *written)

    return finish(False, other, *finish(True, mine))


def solution(mesh):
    spec = P(DEVICES, None)
    return jax.shard_map(
        body, mesh=mesh, in_specs=(spec,) * 4, out_specs=(spec,) * 3, check_vma=False
    )
```

time: 21.5 us -> 21.7 us (level)
    ppermute x1, starting transfers between devices: 0.52 us -> 0.77 us  [carry_states(): got = lax.ppermute(send, DEVICES, swap)]
  transfers between devices with their start and end apart: 8 -> 8, of which waited for: 6 -> 7; matrix products, arithmetic and copies ran while one was open for 0% -> 0% of each run, Pallas kernels for 13% -> 13%
where the time goes in v7:
time: 21.7 us; the launch traced here: 21.5 us
  starting transfers between devices  10.2 us (47%)
  waiting for transfers between devices  5.46 us (25%)
  Pallas kernels  4.76 us (22%)
  between operations  0.72 us (3%)
  other arithmetic  0.25 us (1%)
    ppermute x6, starting transfers between devices, carry_states(): arrived = lax.ppermute(message, DEVICES, perm).astype(F32)  9.16 us
    ppermute x6, waiting for transfers between devices, carry_states(): arrived = lax.ppermute(message, DEVICES, perm).astype(F32)  4.72 us
    pallas_call x2, Pallas kernels, finish(): pl.pallas_call(functools.partial(finish_kernel, mine), out_shape=tuple((j...  1.74 us
    pallas_call x1, Pallas kernels, carry_states(): *local, chip = local_terms(keep, got)  1.57 us
    pallas_call x1, Pallas kernels, body(): pl.pallas_call(send_kernel, out_shape=jax.ShapeDtypeStruct(shape, BF16),...  1.16 us
    ppermute x1, starting transfers between devices, carry_states(): got = lax.ppermute(send, DEVICES, swap)  0.77 us
    ppermute x1, waiting for transfers between devices, carry_states(): got = lax.ppermute(send, DEVICES, swap)  0.54 us
  transfers between devices with their start and end apart: 8, of which 7 were waited for; matrix products, arithmetic and copies ran while one was open for 0% of the time, Pallas kernels for 13%

profile of v7, /device:TPU:0, one launch (start us, length us, event | category | flops | bytes accessed | tf_op | source)
XLA Modules:
  0.0 21.5 jit_solution(8097943834426763909)
XLA Ops:
  0.6 0.0 copy-start.1
  0.6 0.0 copy-start
  0.7 0.0 copy-start.3
  0.7 1.2 %shard_map.68 = bf16[2,128,128]{2,1,0:T(8,128)(2,1)S(1)} custom-call(bf16[128,256]{1,0:T(8,128)(2,1)} %k_ref.7, bf16[128,256]{1,0:T(8,128)(2,1)} %v_ref.7, bf16[128,1024]{1,0:T(8,128)(2,1)} %o_ref.3, bf16[128,1024]{1,0:T(8,128)(2,1)} %q_ref.3), custom_call_target="tpu_custom_call" | custom-call | tf_op jit(solution)/shard_map/pallas_call | solution.py:272
  1.8 0.0 copy-start.2
  1.8 0.8 %collective-permute-start = (bf16[2,128,128]{2,1,0:T(8,128)(2,1)S(1)}, bf16[2,128,128]{2,1,0:T(8,128)(2,1)S(1)}, u32[]{:S(2)}, u32[]{:S(2)}) collective-permute-start(bf16[2,128,128]{2,1,0:T(8,128)(2,1)S(1)} %shard_map.68), channel_id=1, source_target_pairs={{0,1},{1,0},{2,3},{3,2},{4,5},{5,4},{6,7},{7,6},{8,9},{9,8},{10,11... | collective-permute-start | bytes 196616 | tf_op jit(solution)/shard_map/ppermute | solution.py:215
  2.6 0.0 copy-done.1
  2.6 0.0 copy-done
  2.6 0.0 copy-done.3
  2.6 0.1 copy-done.2
  2.7 0.3 %shard_map.67.keep_ref = bf16[2,128,128]{2,1,0:T(8,128)(2,1)S(1)} custom-call(bf16[128,256]{1,0:T(8,128)(2,1)S(1)} %copy-done.2, bf16[128,256]{1,0:T(8,128)(2,1)S(1)} %copy-done.3, bf16[128,1024]{1,0:T(8,128)(2,1)S(1)} %copy-done.1, bf16[128,1024]{1,0:T(8,128)(2,1)S(1)} %copy-done), custom_call_target="tpu_custom_call" | custom-call | flops 33554432 | bytes 524288 | tf_op jit(solution)/shard_map/pallas_call | solution.py:282
  3.0 0.5 %collective-permute-done.got_ref = bf16[2,128,128]{2,1,0:T(8,128)(2,1)S(1)} collective-permute-done((bf16[2,128,128]{2,1,0:T(8,128)(2,1)S(1)}, bf16[2,128,128]{2,1,0:T(8,128)(2,1)S(1)}, u32[]{:S(2)}, u32[]{:S(2)}) %collective-permute-start) | collective-permute-done | bytes 65568 | tf_op jit(solution)/shard_map/ppermute | solution.py:215
  3.5 0.1 fusion.8
  3.6 2.7 %collective-permute-start.1 = (bf16[2,128,128]{2,1,0:T(8,128)(2,1)S(1)}, bf16[2,128,128]{2,1,0:T(8,128)(2,1)S(1)}, u32[]{:S(2)}, u32[]{:S(2)}) collective-permute-start(bf16[2,128,128]{2,1,0:T(8,128)(2,1)S(1)} %get-tuple-element.21), channel_id=1, source_target_pairs={{0,3},{1,8},{2,11},{3,0},{4,13},{5,6},{6,5},{7,14},{8,24},{9,10},{... | collective-permute-start | bytes 196616 | tf_op jit(solution)/shard_map/ppermute | solution.py:249
  6.2 1.5 %collective-permute-start.2 = (bf16[2,128,128]{2,1,0:T(8,128)(2,1)S(1)}, bf16[2,128,128]{2,1,0:T(8,128)(2,1)S(1)}, u32[]{:S(2)}, u32[]{:S(2)}) collective-permute-start(bf16[2,128,128]{2,1,0:T(8,128)(2,1)S(1)} %get-tuple-element.22), channel_id=1, source_target_pairs={{0,6},{1,24},{2,27},{3,5},{4,29},{5,3},{6,0},{7,30},{8,17},{9,15},... | collective-permute-start | bytes 196616 | tf_op jit(solution)/shard_map/ppermute | solution.py:249
  7.7 0.0 collective-permute-start.3
  7.7 1.6 %shard_map.69 = (f32[128,1024]{1,0:T(8,128)S(1)}, f32[128,256]{1,0:T(8,128)S(1)}, f32[128,256]{1,0:T(8,128)S(1)}, bf16[128,1024]{1,0:T(8,128)(2,1)S(1)}, f32[2,128,128]{2,1,0:T(8,128)S(1)}) custom-call(bf16[128,1024]{1,0:T(8,128)(2,1)S(1)} %copy-done, bf16[128,256]{1,0:T(8,128)(2,1)S(1)} %copy-done.2, bf16[128,256]{1,0:T(8,128)(2,1)S(1)} %copy-done.3, ...), custom_call_target="tpu_custom_call" | custom-call | flops 201326592 | bytes 1572864 | tf_op jit(solution)/shard_map/pallas_call | solution.py:217
  9.3 0.0 collective-permute-done.1
  9.3 2.2 %collective-permute-done.2 = bf16[2,128,128]{2,1,0:T(8,128)(2,1)S(1)} collective-permute-done((bf16[2,128,128]{2,1,0:T(8,128)(2,1)S(1)}, bf16[2,128,128]{2,1,0:T(8,128)(2,1)S(1)}, u32[]{:S(2)}, u32[]{:S(2)}) %collective-permute-start.2) | collective-permute-done | bytes 65568 | tf_op jit(solution)/shard_map/ppermute | solution.py:249
  11.5 0.6 %collective-permute-done.3 = bf16[2,128,128]{2,1,0:T(8,128)(2,1)S(1)} collective-permute-done((bf16[2,128,128]{2,1,0:T(8,128)(2,1)S(1)}, bf16[2,128,128]{2,1,0:T(8,128)(2,1)S(1)}, u32[]{:S(2)}, u32[]{:S(2)}) %collective-permute-start.3) | collective-permute-done | bytes 65568 | tf_op jit(solution)/shard_map/ppermute | solution.py:249
  12.1 0.1 select_convert_fusion
  12.2 0.4 %collective-permute-start.4 = (bf16[2,128,128]{2,1,0:T(8,128)(2,1)S(1)}, bf16[2,128,128]{2,1,0:T(8,128)(2,1)S(1)}, u32[]{:S(2)}, u32[]{:S(2)}) collective-permute-start(bf16[2,128,128]{2,1,0:T(8,128)(2,1)S(1)} %get-tuple-element.25), channel_id=1, source_target_pairs={{0,9},{1,7},{2,4},{3,10},{4,2},{5,12},{6,15},{7,1},{8,14},{9,16},{... | collective-permute-start | bytes 196616 | tf_op jit(solution)/shard_map/ppermute | solution.py:249
  12.6 2.9 %collective-permute-start.5 = (bf16[2,128,128]{2,1,0:T(8,128)(2,1)S(1)}, bf16[2,128,128]{2,1,0:T(8,128)(2,1)S(1)}, u32[]{:S(2)}, u32[]{:S(2)}) collective-permute-start(bf16[2,128,128]{2,1,0:T(8,128)(2,1)S(1)} %get-tuple-element.26), channel_id=1, source_target_pairs={{0,16},{1,4},{2,7},{3,19},{4,1},{5,21},{6,22},{7,2},{8,13},{9,25},... | collective-permute-start | bytes 196616 | tf_op jit(solution)/shard_map/ppermute | solution.py:249
  15.5 1.8 %collective-permute-start.6 = (bf16[2,128,128]{2,1,0:T(8,128)(2,1)S(1)}, bf16[2,128,128]{2,1,0:T(8,128)(2,1)S(1)}, u32[]{:S(2)}, u32[]{:S(2)}) collective-permute-start(bf16[2,128,128]{2,1,0:T(8,128)(2,1)S(1)} %get-tuple-element.27), channel_id=1, source_target_pairs={{0,25},{1,2},{2,1},{3,26},{4,7},{5,28},{6,31},{7,4},{8,11},{9,0},{... | collective-permute-start | bytes 196616 | tf_op jit(solution)/shard_map/ppermute | solution.py:249
  17.2 0.6 %collective-permute-done.4 = bf16[2,128,128]{2,1,0:T(8,128)(2,1)S(1)} collective-permute-done((bf16[2,128,128]{2,1,0:T(8,128)(2,1)S(1)}, bf16[2,128,128]{2,1,0:T(8,128)(2,1)S(1)}, u32[]{:S(2)}, u32[]{:S(2)}) %collective-permute-start.4) | collective-permute-done | bytes 65568 | tf_op jit(solution)/shard_map/ppermute | solution.py:249
  17.9 0.6 %collective-permute-done.5 = bf16[2,128,128]{2,1,0:T(8,128)(2,1)S(1)} collective-permute-done((bf16[2,128,128]{2,1,0:T(8,128)(2,1)S(1)}, bf16[2,128,128]{2,1,0:T(8,128)(2,1)S(1)}, u32[]{:S(2)}, u32[]{:S(2)}) %collective-permute-start.5) | collective-permute-done | bytes 65568 | tf_op jit(solution)/shard_map/ppermute | solution.py:249
  18.5 0.7 %collective-permute-done.6 = bf16[2,128,128]{2,1,0:T(8,128)(2,1)S(1)} collective-permute-done((bf16[2,128,128]{2,1,0:T(8,128)(2,1)S(1)}, bf16[2,128,128]{2,1,0:T(8,128)(2,1)S(1)}, u32[]{:S(2)}, u32[]{:S(2)}) %collective-permute-start.6) | collective-permute-done | bytes 65568 | tf_op jit(solution)/shard_map/ppermute | solution.py:249
  19.2 0.1 fusion.3
  19.3 0.3 %collective-permute-start.7 = (bf16[2,128,128]{2,1,0:T(8,128)(2,1)S(1)}, bf16[2,128,128]{2,1,0:T(8,128)(2,1)S(1)}, u32[]{:S(2)}, u32[]{:S(2)}) collective-permute-start(bf16[2,128,128]{2,1,0:T(8,128)(2,1)S(1)} %get-tuple-element.35), channel_id=1, source_target_pairs={{0,1},{1,0},{2,3},{3,2},{4,5},{5,4},{6,7},{7,6},{8,9},{9,8},{10,11... | collective-permute-start | bytes 196616 | tf_op jit(solution)/shard_map/ppermute | solution.py:261
  19.5 0.8 %shard_map.70 = (bf16[128,1024]{1,0:T(8,128)(2,1)}, bf16[128,256]{1,0:T(8,128)(2,1)}, bf16[128,256]{1,0:T(8,128)(2,1)}) custom-call(bf16[128,256]{1,0:T(8,128)(2,1)S(1)} %copy-done.2, bf16[128,256]{1,0:T(8,128)(2,1)S(1)} %copy-done.3, bf16[128,1024]{1,0:T(8,128)(2,1)S(1)} %get-tuple-element.17.scaled_ref, f32[128,1024]{1,0:T(8,128)S(1)} %get-tuple-element.18.ql_ref, ...), custom_call_target="tpu_custom_call" | custom-call | flops 67108864 | bytes 524288 | tf_op jit(solution)/shard_map/pallas_call | solution.py:307
  20.4 0.2 collective-permute-done.7.state_ref
  20.6 0.9 %shard_map.71 = (bf16[128,1024]{1,0:T(8,128)(2,1)}, bf16[128,256]{1,0:T(8,128)(2,1)}, bf16[128,256]{1,0:T(8,128)(2,1)}) custom-call(bf16[128,256]{1,0:T(8,128)(2,1)S(1)} %copy-done.2, bf16[128,256]{1,0:T(8,128)(2,1)S(1)} %copy-done.3, bf16[128,1024]{1,0:T(8,128)(2,1)S(1)} %get-tuple-element.17.scaled_ref, ...), custom_call_target="tpu_custom_call", output_to_operand_aliasing={{0}: (7, {}), {1}: (8, {}), {2}: (9, {})} | custom-call | flops 67108864 | bytes 524288 | tf_op jit(solution)/shard_map/pallas_call | solution.py:307
  (1 shorter events, 0.0 us)
Async XLA Ops:
  0.6 2.0 %copy-start.1 = (bf16[128,1024]{1,0:T(8,128)(2,1)S(1)}, bf16[128,1024]{1,0:T(8,128)(2,1)}, u32[]{:S(2)}) copy-start(bf16[128,1024]{1,0:T(8,128)(2,1)} %o_ref.3) | copy-start | bytes 786436
  0.6 2.0 %copy-start = (bf16[128,1024]{1,0:T(8,128)(2,1)S(1)}, bf16[128,1024]{1,0:T(8,128)(2,1)}, u32[]{:S(2)}) copy-start(bf16[128,1024]{1,0:T(8,128)(2,1)} %q_ref.3) | copy-start | bytes 786436
  0.7 2.0 %copy-start.3 = (bf16[128,256]{1,0:T(8,128)(2,1)S(1)}, bf16[128,256]{1,0:T(8,128)(2,1)}, u32[]{:S(2)}) copy-start(bf16[128,256]{1,0:T(8,128)(2,1)} %v_ref.7) | copy-start | bytes 196612
  1.8 0.8 %copy-start.2 = (bf16[128,256]{1,0:T(8,128)(2,1)S(1)}, bf16[128,256]{1,0:T(8,128)(2,1)}, u32[]{:S(2)}) copy-start(bf16[128,256]{1,0:T(8,128)(2,1)} %k_ref.7) | copy-start | bytes 196612
  1.8 1.7 %collective-permute-start = (bf16[2,128,128]{2,1,0:T(8,128)(2,1)S(1)}, bf16[2,128,128]{2,1,0:T(8,128)(2,1)S(1)}, u32[]{:S(2)}, u32[]{:S(2)}) collective-permute-start(bf16[2,128,128]{2,1,0:T(8,128)(2,1)S(1)} %shard_map.68), channel_id=1, source_target_pairs={{0,1},{1,0},{2,3},{3,2},{4,5},{5,4},{6,7},{7,6},{8,9},{9,8},{10,11... | collective-permute-start | bytes 196616 | tf_op jit(solution)/shard_map/ppermute | solution.py:215
  3.6 5.7 %collective-permute-start.1 = (bf16[2,128,128]{2,1,0:T(8,128)(2,1)S(1)}, bf16[2,128,128]{2,1,0:T(8,128)(2,1)S(1)}, u32[]{:S(2)}, u32[]{:S(2)}) collective-permute-start(bf16[2,128,128]{2,1,0:T(8,128)(2,1)S(1)} %get-tuple-element.21), channel_id=1, source_target_pairs={{0,3},{1,8},{2,11},{3,0},{4,13},{5,6},{6,5},{7,14},{8,24},{9,10},{... | collective-permute-start | bytes 196616 | tf_op jit(solution)/shard_map/ppermute | solution.py:249
  6.2 5.2 %collective-permute-start.2 = (bf16[2,128,128]{2,1,0:T(8,128)(2,1)S(1)}, bf16[2,128,128]{2,1,0:T(8,128)(2,1)S(1)}, u32[]{:S(2)}, u32[]{:S(2)}) collective-permute-start(bf16[2,128,128]{2,1,0:T(8,128)(2,1)S(1)} %get-tuple-element.22), channel_id=1, source_target_pairs={{0,6},{1,24},{2,27},{3,5},{4,29},{5,3},{6,0},{7,30},{8,17},{9,15},... | collective-permute-start | bytes 196616 | tf_op jit(solution)/shard_map/ppermute | solution.py:249
  7.7 4.4 %collective-permute-start.3 = (bf16[2,128,128]{2,1,0:T(8,128)(2,1)S(1)}, bf16[2,128,128]{2,1,0:T(8,128)(2,1)S(1)}, u32[]{:S(2)}, u32[]{:S(2)}) collective-permute-start(bf16[2,128,128]{2,1,0:T(8,128)(2,1)S(1)} %get-tuple-element.23), channel_id=1, source_target_pairs={{0,5},{1,17},{2,18},{3,6},{4,20},{5,0},{6,3},{7,23},{8,1},{9,12},{... | collective-permute-start | bytes 196616 | tf_op jit(solution)/shard_map/ppermute | solution.py:249
  12.2 5.6 %collective-permute-start.4 = (bf16[2,128,128]{2,1,0:T(8,128)(2,1)S(1)}, bf16[2,128,128]{2,1,0:T(8,128)(2,1)S(1)}, u32[]{:S(2)}, u32[]{:S(2)}) collective-permute-start(bf16[2,128,128]{2,1,0:T(8,128)(2,1)S(1)} %get-tuple-element.25), channel_id=1, source_target_pairs={{0,9},{1,7},{2,4},{3,10},{4,2},{5,12},{6,15},{7,1},{8,14},{9,16},{... | collective-permute-start | bytes 196616 | tf_op jit(solution)/shard_map/ppermute | solution.py:249
  12.6 5.9 %collective-permute-start.5 = (bf16[2,128,128]{2,1,0:T(8,128)(2,1)S(1)}, bf16[2,128,128]{2,1,0:T(8,128)(2,1)S(1)}, u32[]{:S(2)}, u32[]{:S(2)}) collective-permute-start(bf16[2,128,128]{2,1,0:T(8,128)(2,1)S(1)} %get-tuple-element.26), channel_id=1, source_target_pairs={{0,16},{1,4},{2,7},{3,19},{4,1},{5,21},{6,22},{7,2},{8,13},{9,25},... | collective-permute-start | bytes 196616 | tf_op jit(solution)/shard_map/ppermute | solution.py:249
  15.5 3.7 %collective-permute-start.6 = (bf16[2,128,128]{2,1,0:T(8,128)(2,1)S(1)}, bf16[2,128,128]{2,1,0:T(8,128)(2,1)S(1)}, u32[]{:S(2)}, u32[]{:S(2)}) collective-permute-start(bf16[2,128,128]{2,1,0:T(8,128)(2,1)S(1)} %get-tuple-element.27), channel_id=1, source_target_pairs={{0,25},{1,2},{2,1},{3,26},{4,7},{5,28},{6,31},{7,4},{8,11},{9,0},{... | collective-permute-start | bytes 196616 | tf_op jit(solution)/shard_map/ppermute | solution.py:249
  19.3 1.3 %collective-permute-start.7 = (bf16[2,128,128]{2,1,0:T(8,128)(2,1)S(1)}, bf16[2,128,128]{2,1,0:T(8,128)(2,1)S(1)}, u32[]{:S(2)}, u32[]{:S(2)}) collective-permute-start(bf16[2,128,128]{2,1,0:T(8,128)(2,1)S(1)} %get-tuple-element.35), channel_id=1, source_target_pairs={{0,1},{1,0},{2,3},{3,2},{4,5},{5,4},{6,7},{7,6},{8,9},{9,8},{10,11... | collective-permute-start | bytes 196616 | tf_op jit(solution)/shard_map/ppermute | solution.py:261

commit v8 on v6

--- a/solution.py
+++ b/solution.py
@@ -11,7 +11,7 @@
 SEQ = "seq"
 HEAD = "head"
 DEVICES = (SEQ, HEAD)
-LOW_MOVES = ((1, 0, 3, 2), (2, 3, 0, 1), (3, 2, 1, 0))
+LOW_MOVES = ((1, 0, 3, 2), (3, 2, 1, 0), (2, 3, 0, 1))
 TOP_MOVES = ((3, 0, 1, 2), (2, 3, 0, 1), (1, 2, 3, 0))
 LOW_ODD = (0, 1, 1, 0)
 TOP_ODD = (0, 1, 0, 1)
@@ -196,31 +196,33 @@
     keep = keep.astype(F32)
     got = got.astype(F32)
     message = (keep + got).astype(BF16)
-    earlier = jnp.zeros_like(total[0])
-    later = jnp.zeros_like(total[1])
-    *low_rounds, top_round = tables(size)
-    for low, moves, _ in low_rounds:
+    low_rounds, (top, moves, _) = tables(size)[:-1], tables(size)[-1]
+
+    def exchange(messages, low, moves):
         digit = index >> low & len(moves)
-        for move in moves:
-            arrived = lax.ppermute(
-                message, DEVICES, [(i, target(i, size, low, move)) for i in range(size)]
-            ).astype(F32)
-            before = place_among(digit, [move.index(place) for place in range(len(move))]) < digit
-            earlier = earlier + jnp.where(before, arrived[0], 0.0)
-            later = later + jnp.where(before, 0.0, arrived[1])
-            total = total + arrived
-        message = total.astype(BF16)
-    low, moves, _ = top_round
-    digit = index >> low & len(moves)
-    messages = [jnp.where(place_among(digit, move) > digit, message[0], message[1]) for move in moves]
-    messages = lax.optimization_barrier(tuple(messages))
-    for move, message in zip(moves, messages):
-        arrived = lax.ppermute(
-            message, DEVICES, [(i, target(i, size, low, move)) for i in range(size)]
-        ).astype(F32)
-        before = place_among(digit, [move.index(place) for place in range(len(move))]) < digit
+        found = []
+        for move, message in zip(moves, lax.optimization_barrier(tuple(messages))):
+            perm = [(i, target(i, size, low, move)) for i in range(size)]
+            source = place_among(digit, [move.index(place) for place in range(len(move))])
+            found.append((source < digit, lax.ppermute(message, DEVICES, perm).astype(F32)))
+        return found
+
+    def upward(low, move):
+        digit = index >> low & len(move) - 1
+        return place_among(digit, move) > digit
+
+    messages = [jnp.where(upward(top, move), message[0], message[1]) for move in moves]
+    earlier, later = 0.0, 0.0
+    for before, arrived in exchange(messages, top, moves):
         earlier = earlier + jnp.where(before, arrived, 0.0)
         later = later + jnp.where(before, 0.0, arrived)
+    for low, moves, _ in low_rounds[::-1]:
+        up = jnp.stack([earlier + total[0], later]).astype(BF16)
+        down = jnp.stack([earlier, later + total[1]]).astype(BF16)
+        messages = [jnp.where(upward(low, move), up, down) for move in moves]
+        for _, arrived in exchange(messages, low, moves):
+            earlier = earlier + arrived[0]
+            later = later + arrived[1]
     first = index & 1 == 0
     mine = jnp.stack([earlier + jnp.where(first, 0.0, got[0]), later + jnp.where(first, got[1], 0.0)])
     theirs = jnp.stack([earlier + jnp.where(first, keep[0], 0.0), later + jnp.where(first, 0.0, keep[1])])

time: 21.5 us -> 21.6 us (level)
  no operation moved by 1% of the time
where the time goes in v8:
time: 21.6 us; the launch traced here: 21.5 us
  starting transfers between devices  10.1 us (47%)
  waiting for transfers between devices  5.35 us (25%)
  Pallas kernels  4.94 us (23%)
  between operations  0.78 us (4%)
  other arithmetic  0.26 us (1%)
    ppermute x6, starting transfers between devices, exchange(): lax.ppermute(message, DEVICES, perm).astype(F32)  9.38 us
    ppermute x6, waiting for transfers between devices, exchange(): lax.ppermute(message, DEVICES, perm).astype(F32)  4.52 us
    pallas_call x2, Pallas kernels, finish(): pl.pallas_call(functools.partial(finish_kernel, mine), out_shape=tuple((j...  1.77 us
    pallas_call x1, Pallas kernels, carry_states(): *local, total = local_terms(keep, got)  1.57 us
    pallas_call x1, Pallas kernels, body(): pl.pallas_call(send_kernel, out_shape=jax.ShapeDtypeStruct(shape, BF16),...  1.34 us
    ppermute x1, waiting for transfers between devices, carry_states(): got = lax.ppermute(send, DEVICES, swap)  0.63 us
    ppermute x1, starting transfers between devices, carry_states(): got = lax.ppermute(send, DEVICES, swap)  0.52 us
  transfers between devices with their start and end apart: 8, of which 6 were waited for; matrix products, arithmetic and copies ran while one was open for 0% of the time, Pallas kernels for 13%

profile of v8, /device:TPU:0, one launch (start us, length us, event | category | flops | bytes accessed | tf_op | source)
XLA Modules:
  0.0 21.5 jit_solution(12900580244183554357)
XLA Ops:
  0.6 0.0 copy-start
  0.6 0.0 copy-start.1
  0.7 0.0 copy-start.2
  0.7 0.0 copy-start.3
  0.7 1.3 %shard_map.68 = bf16[2,1,128,128]{3,2,1,0:T(8,128)(2,1)S(1)} custom-call(bf16[128,256]{1,0:T(8,128)(2,1)} %k_ref.7, bf16[128,256]{1,0:T(8,128)(2,1)} %v_ref.7, bf16[128,1024]{1,0:T(8,128)(2,1)} %o_ref.3, bf16[128,1024]{1,0:T(8,128)(2,1)} %q_ref.3), custom_call_target="tpu_custom_call" | custom-call | tf_op jit(solution)/shard_map/pallas_call | solution.py:241
  2.0 0.5 %collective-permute-start = (bf16[2,1,128,128]{3,2,1,0:T(8,128)(2,1)S(1)}, bf16[2,1,128,128]{3,2,1,0:T(8,128)(2,1)S(1)}, u32[]{:S(2)}, u32[]{:S(2)}) collective-permute-start(bf16[2,1,128,128]{3,2,1,0:T(8,128)(2,1)S(1)} %shard_map.68), channel_id=1, source_target_pairs={{0,1},{1,0},{2,3},{3,2},{4,5},{5,4},{6,7},{7,6},{8,9},{9,8},{10,11... | collective-permute-start | bytes 196616 | tf_op jit(solution)/shard_map/ppermute | solution.py:193
  2.5 0.0 copy-done
  2.5 0.0 copy-done.1
  2.5 0.0 copy-done.2
  2.5 0.0 copy-done.3
  2.6 0.3 %shard_map.67.keep_ref = bf16[2,1,128,128]{3,2,1,0:T(8,128)(2,1)S(1)} custom-call(bf16[128,256]{1,0:T(8,128)(2,1)S(1)} %copy-done.2, bf16[128,256]{1,0:T(8,128)(2,1)S(1)} %copy-done.3, bf16[128,1024]{1,0:T(8,128)(2,1)S(1)} %copy-done.1, bf16[128,1024]{1,0:T(8,128)(2,1)S(1)} %copy-done), custom_call_target="tpu_custom_call" | custom-call | flops 33554432 | bytes 524288 | tf_op jit(solution)/shard_map/pallas_call | solution.py:251
  2.8 0.6 %collective-permute-done.got_ref = bf16[2,1,128,128]{3,2,1,0:T(8,128)(2,1)S(1)} collective-permute-done((bf16[2,1,128,128]{3,2,1,0:T(8,128)(2,1)S(1)}, bf16[2,1,128,128]{3,2,1,0:T(8,128)(2,1)S(1)}, u32[]{:S(2)}, u32[]{:S(2)}) %collective-permute-start) | collective-permute-done | bytes 65568 | tf_op jit(solution)/shard_map/ppermute | solution.py:193
  3.5 2.7 %collective-permute-start.3 = (bf16[1,128,128]{2,1,0:T(8,128)(2,1)S(1)}, bf16[1,128,128]{2,1,0:T(8,128)(2,1)S(1)}, u32[]{:S(2)}, u32[]{:S(2)}) collective-permute-start(bf16[1,128,128]{2,1,0:T(8,128)(2,1)S(1)} %get-tuple-element.23), channel_id=1, source_target_pairs={{0,9},{1,8},{2,11},{3,10},{4,13},{5,12},{6,15},{7,14},{8,17},{9,16... | collective-permute-start | bytes 98312 | tf_op jit(solution)/shard_map/ppermute | solution.py:207
  6.2 2.6 %collective-permute-start.2 = (bf16[1,128,128]{2,1,0:T(8,128)(2,1)S(1)}, bf16[1,128,128]{2,1,0:T(8,128)(2,1)S(1)}, u32[]{:S(2)}, u32[]{:S(2)}) collective-permute-start(bf16[1,128,128]{2,1,0:T(8,128)(2,1)S(1)} %get-tuple-element.22), channel_id=1, source_target_pairs={{0,16},{1,17},{2,18},{3,19},{4,20},{5,21},{6,22},{7,23},{8,24},{9,... | collective-permute-start | bytes 98312 | tf_op jit(solution)/shard_map/ppermute | solution.py:207
  8.8 1.0 %collective-permute-start.1 = (bf16[1,128,128]{2,1,0:T(8,128)(2,1)S(1)}, bf16[1,128,128]{2,1,0:T(8,128)(2,1)S(1)}, u32[]{:S(2)}, u32[]{:S(2)}) collective-permute-start(bf16[1,128,128]{2,1,0:T(8,128)(2,1)S(1)} %get-tuple-element.21), channel_id=1, source_target_pairs={{0,25},{1,24},{2,27},{3,26},{4,29},{5,28},{6,31},{7,30},{8,1},{9,0... | collective-permute-start | bytes 98312 | tf_op jit(solution)/shard_map/ppermute | solution.py:207
  9.8 1.6 %shard_map.69 = (f32[128,1024]{1,0:T(8,128)S(1)}, f32[128,256]{1,0:T(8,128)S(1)}, f32[128,256]{1,0:T(8,128)S(1)}, bf16[128,1024]{1,0:T(8,128)(2,1)S(1)}, f32[2,1,128,128]{3,2,1,0:T(8,128)S(1)}) custom-call(bf16[128,1024]{1,0:T(8,128)(2,1)S(1)} %copy-done, bf16[128,256]{1,0:T(8,128)(2,1)S(1)} %copy-done.2, bf16[128,256]{1,0:T(8,128)(2,1)S(1)} %copy-done.3, ...), custom_call_target="tpu_custom_call" | custom-call | flops 201326592 | bytes 1572864 | tf_op jit(solution)/shard_map/pallas_call | solution.py:195
  11.4 0.0 collective-permute-done.3
  11.4 0.0 collective-permute-done.2
  11.4 0.8 %collective-permute-done.1 = bf16[1,128,128]{2,1,0:T(8,128)(2,1)S(1)} collective-permute-done((bf16[1,128,128]{2,1,0:T(8,128)(2,1)S(1)}, bf16[1,128,128]{2,1,0:T(8,128)(2,1)S(1)}, u32[]{:S(2)}, u32[]{:S(2)}) %collective-permute-start.1) | collective-permute-done | bytes 32800 | tf_op jit(solution)/shard_map/ppermute | solution.py:207
  12.3 1.3 %collective-permute-start.6 = (bf16[2,1,128,128]{3,2,1,0:T(8,128)(2,1)S(1)}, bf16[2,1,128,128]{3,2,1,0:T(8,128)(2,1)S(1)}, u32[]{:S(2)}, u32[]{:S(2)}) collective-permute-start(bf16[2,1,128,128]{3,2,1,0:T(8,128)(2,1)S(1)} %get-tuple-element.27), channel_id=1, source_target_pairs={{0,5},{1,4},{2,7},{3,6},{4,1},{5,0},{6,3},{7,2},{8,13},{9,12},{10,... | collective-permute-start | bytes 196616 | tf_op jit(solution)/shard_map/ppermute | solution.py:207
  13.6 1.4 %collective-permute-start.5 = (bf16[2,1,128,128]{3,2,1,0:T(8,128)(2,1)S(1)}, bf16[2,1,128,128]{3,2,1,0:T(8,128)(2,1)S(1)}, u32[]{:S(2)}, u32[]{:S(2)}) collective-permute-start(bf16[2,1,128,128]{3,2,1,0:T(8,128)(2,1)S(1)} %get-tuple-element.26), channel_id=1, source_target_pairs={{0,6},{1,7},{2,4},{3,5},{4,2},{5,3},{6,0},{7,1},{8,14},{9,15},{10,... | collective-permute-start | bytes 196616 | tf_op jit(solution)/shard_map/ppermute | solution.py:207
  15.1 0.3 %collective-permute-start.4 = (bf16[2,1,128,128]{3,2,1,0:T(8,128)(2,1)S(1)}, bf16[2,1,128,128]{3,2,1,0:T(8,128)(2,1)S(1)}, u32[]{:S(2)}, u32[]{:S(2)}) collective-permute-start(bf16[2,1,128,128]{3,2,1,0:T(8,128)(2,1)S(1)} %get-tuple-element.25), channel_id=1, source_target_pairs={{0,3},{1,2},{2,1},{3,0},{4,7},{5,6},{6,5},{7,4},{8,11},{9,10},{10,... | collective-permute-start | bytes 196616 | tf_op jit(solution)/shard_map/ppermute | solution.py:207
  15.4 1.1 %collective-permute-done.6 = bf16[2,1,128,128]{3,2,1,0:T(8,128)(2,1)S(1)} collective-permute-done((bf16[2,1,128,128]{3,2,1,0:T(8,128)(2,1)S(1)}, bf16[2,1,128,128]{3,2,1,0:T(8,128)(2,1)S(1)}, u32[]{:S(2)}, u32[]{:S(2)}) %collective-permute-start.6) | collective-permute-done | bytes 65568 | tf_op jit(solution)/shard_map/ppermute | solution.py:207
  16.5 2.5 %collective-permute-done.5 = bf16[2,1,128,128]{3,2,1,0:T(8,128)(2,1)S(1)} collective-permute-done((bf16[2,1,128,128]{3,2,1,0:T(8,128)(2,1)S(1)}, bf16[2,1,128,128]{3,2,1,0:T(8,128)(2,1)S(1)}, u32[]{:S(2)}, u32[]{:S(2)}) %collective-permute-start.5) | collective-permute-done | bytes 65568 | tf_op jit(solution)/shard_map/ppermute | solution.py:207
  19.0 0.2 collective-permute-done.4
  19.1 0.1 fusion.28
  19.3 0.2 %collective-permute-start.7 = (bf16[2,1,128,128]{3,2,1,0:T(8,128)(2,1)S(1)}, bf16[2,1,128,128]{3,2,1,0:T(8,128)(2,1)S(1)}, u32[]{:S(2)}, u32[]{:S(2)}) collective-permute-start(bf16[2,1,128,128]{3,2,1,0:T(8,128)(2,1)S(1)} %pad_maximum_fusion.2), channel_id=1, source_target_pairs={{0,1},{1,0},{2,3},{3,2},{4,5},{5,4},{6,7},{7,6},{8,9},{9,8},{10,11... | collective-permute-start | bytes 196616 | tf_op jit(solution)/shard_map/ppermute | solution.py:229
  19.5 0.9 %shard_map.70 = (bf16[128,1024]{1,0:T(8,128)(2,1)}, bf16[128,256]{1,0:T(8,128)(2,1)}, bf16[128,256]{1,0:T(8,128)(2,1)}) custom-call(bf16[128,256]{1,0:T(8,128)(2,1)S(1)} %copy-done.2, bf16[128,256]{1,0:T(8,128)(2,1)S(1)} %copy-done.3, bf16[128,1024]{1,0:T(8,128)(2,1)S(1)} %get-tuple-element.17.scaled_ref, f32[128,1024]{1,0:T(8,128)S(1)} %get-tuple-element.18.ql_ref, ...), custom_call_target="tpu_custom_call" | custom-call | flops 67108864 | bytes 524288 | tf_op jit(solution)/shard_map/pallas_call | solution.py:276
  20.4 0.2 collective-permute-done.7.state_ref
  20.6 0.9 %shard_map.71 = (bf16[128,1024]{1,0:T(8,128)(2,1)}, bf16[128,256]{1,0:T(8,128)(2,1)}, bf16[128,256]{1,0:T(8,128)(2,1)}) custom-call(bf16[128,256]{1,0:T(8,128)(2,1)S(1)} %copy-done.2, bf16[128,256]{1,0:T(8,128)(2,1)S(1)} %copy-done.3, bf16[128,1024]{1,0:T(8,128)(2,1)S(1)} %get-tuple-element.17.scaled_ref, ...), custom_call_target="tpu_custom_call", output_to_operand_aliasing={{0}: (7, {}), {1}: (8, {}), {2}: (9, {})} | custom-call | flops 67108864 | bytes 524288 | tf_op jit(solution)/shard_map/pallas_call | solution.py:276
  (12 shorter events, 0.2 us)
Async XLA Ops:
  0.6 1.9 %copy-start = (bf16[128,1024]{1,0:T(8,128)(2,1)S(1)}, bf16[128,1024]{1,0:T(8,128)(2,1)}, u32[]{:S(2)}) copy-start(bf16[128,1024]{1,0:T(8,128)(2,1)} %q_ref.3) | copy-start | bytes 786436
  0.6 1.9 %copy-start.1 = (bf16[128,1024]{1,0:T(8,128)(2,1)S(1)}, bf16[128,1024]{1,0:T(8,128)(2,1)}, u32[]{:S(2)}) copy-start(bf16[128,1024]{1,0:T(8,128)(2,1)} %o_ref.3) | copy-start | bytes 786436
  0.7 1.9 %copy-start.2 = (bf16[128,256]{1,0:T(8,128)(2,1)S(1)}, bf16[128,256]{1,0:T(8,128)(2,1)}, u32[]{:S(2)}) copy-start(bf16[128,256]{1,0:T(8,128)(2,1)} %k_ref.7) | copy-start | bytes 196612
  0.7 1.9 %copy-start.3 = (bf16[128,256]{1,0:T(8,128)(2,1)S(1)}, bf16[128,256]{1,0:T(8,128)(2,1)}, u32[]{:S(2)}) copy-start(bf16[128,256]{1,0:T(8,128)(2,1)} %v_ref.7) | copy-start | bytes 196612
  2.0 1.4 %collective-permute-start = (bf16[2,1,128,128]{3,2,1,0:T(8,128)(2,1)S(1)}, bf16[2,1,128,128]{3,2,1,0:T(8,128)(2,1)S(1)}, u32[]{:S(2)}, u32[]{:S(2)}) collective-permute-start(bf16[2,1,128,128]{3,2,1,0:T(8,128)(2,1)S(1)} %shard_map.68), channel_id=1, source_target_pairs={{0,1},{1,0},{2,3},{3,2},{4,5},{5,4},{6,7},{7,6},{8,9},{9,8},{10,11... | collective-permute-start | bytes 196616 | tf_op jit(solution)/shard_map/ppermute | solution.py:193
  3.5 7.9 %collective-permute-start.3 = (bf16[1,128,128]{2,1,0:T(8,128)(2,1)S(1)}, bf16[1,128,128]{2,1,0:T(8,128)(2,1)S(1)}, u32[]{:S(2)}, u32[]{:S(2)}) collective-permute-start(bf16[1,128,128]{2,1,0:T(8,128)(2,1)S(1)} %get-tuple-element.23), channel_id=1, source_target_pairs={{0,9},{1,8},{2,11},{3,10},{4,13},{5,12},{6,15},{7,14},{8,17},{9,16... | collective-permute-start | bytes 98312 | tf_op jit(solution)/shard_map/ppermute | solution.py:207
  6.2 5.2 %collective-permute-start.2 = (bf16[1,128,128]{2,1,0:T(8,128)(2,1)S(1)}, bf16[1,128,128]{2,1,0:T(8,128)(2,1)S(1)}, u32[]{:S(2)}, u32[]{:S(2)}) collective-permute-start(bf16[1,128,128]{2,1,0:T(8,128)(2,1)S(1)} %get-tuple-element.22), channel_id=1, source_target_pairs={{0,16},{1,17},{2,18},{3,19},{4,20},{5,21},{6,22},{7,23},{8,24},{9,... | collective-permute-start | bytes 98312 | tf_op jit(solution)/shard_map/ppermute | solution.py:207
  8.8 3.4 %collective-permute-start.1 = (bf16[1,128,128]{2,1,0:T(8,128)(2,1)S(1)}, bf16[1,128,128]{2,1,0:T(8,128)(2,1)S(1)}, u32[]{:S(2)}, u32[]{:S(2)}) collective-permute-start(bf16[1,128,128]{2,1,0:T(8,128)(2,1)S(1)} %get-tuple-element.21), channel_id=1, source_target_pairs={{0,25},{1,24},{2,27},{3,26},{4,29},{5,28},{6,31},{7,30},{8,1},{9,0... | collective-permute-start | bytes 98312 | tf_op jit(solution)/shard_map/ppermute | solution.py:207
  12.3 4.2 %collective-permute-start.6 = (bf16[2,1,128,128]{3,2,1,0:T(8,128)(2,1)S(1)}, bf16[2,1,128,128]{3,2,1,0:T(8,128)(2,1)S(1)}, u32[]{:S(2)}, u32[]{:S(2)}) collective-permute-start(bf16[2,1,128,128]{3,2,1,0:T(8,128)(2,1)S(1)} %get-tuple-element.27), channel_id=1, source_target_pairs={{0,5},{1,4},{2,7},{3,6},{4,1},{5,0},{6,3},{7,2},{8,13},{9,12},{10,... | collective-permute-start | bytes 196616 | tf_op jit(solution)/shard_map/ppermute | solution.py:207
  13.6 5.3 %collective-permute-start.5 = (bf16[2,1,128,128]{3,2,1,0:T(8,128)(2,1)S(1)}, bf16[2,1,128,128]{3,2,1,0:T(8,128)(2,1)S(1)}, u32[]{:S(2)}, u32[]{:S(2)}) collective-permute-start(bf16[2,1,128,128]{3,2,1,0:T(8,128)(2,1)S(1)} %get-tuple-element.26), channel_id=1, source_target_pairs={{0,6},{1,7},{2,4},{3,5},{4,2},{5,3},{6,0},{7,1},{8,14},{9,15},{10,... | collective-permute-start | bytes 196616 | tf_op jit(solution)/shard_map/ppermute | solution.py:207
  15.1 4.1 %collective-permute-start.4 = (bf16[2,1,128,128]{3,2,1,0:T(8,128)(2,1)S(1)}, bf16[2,1,128,128]{3,2,1,0:T(8,128)(2,1)S(1)}, u32[]{:S(2)}, u32[]{:S(2)}) collective-permute-start(bf16[2,1,128,128]{3,2,1,0:T(8,128)(2,1)S(1)} %get-tuple-element.25), channel_id=1, source_target_pairs={{0,3},{1,2},{2,1},{3,0},{4,7},{5,6},{6,5},{7,4},{8,11},{9,10},{10,... | collective-permute-start | bytes 196616 | tf_op jit(solution)/shard_map/ppermute | solution.py:207
  19.3 1.3 %collective-permute-start.7 = (bf16[2,1,128,128]{3,2,1,0:T(8,128)(2,1)S(1)}, bf16[2,1,128,128]{3,2,1,0:T(8,128)(2,1)S(1)}, u32[]{:S(2)}, u32[]{:S(2)}) collective-permute-start(bf16[2,1,128,128]{3,2,1,0:T(8,128)(2,1)S(1)} %pad_maximum_fusion.2), channel_id=1, source_target_pairs={{0,1},{1,0},{2,3},{3,2},{4,5},{5,4},{6,7},{7,6},{8,9},{9,8},{10,11... | collective-permute-start | bytes 196616 | tf_op jit(solution)/shard_map/ppermute | solution.py:229

commit v9 on v6

--- a/solution.py
+++ b/solution.py
@@ -11,7 +11,7 @@
 SEQ = "seq"
 HEAD = "head"
 DEVICES = (SEQ, HEAD)
-LOW_MOVES = ((1, 0, 3, 2), (2, 3, 0, 1), (3, 2, 1, 0))
+LOW_MOVES = ((1, 0, 3, 2), (3, 2, 1, 0), (2, 3, 0, 1))
 TOP_MOVES = ((3, 0, 1, 2), (2, 3, 0, 1), (1, 2, 3, 0))
 LOW_ODD = (0, 1, 1, 0)
 TOP_ODD = (0, 1, 0, 1)

time: 21.5 us -> 21.6 us (level)
  transfers between devices with their start and end apart: 8 -> 8, of which waited for: 6 -> 7; matrix products, arithmetic and copies ran while one was open for 0% -> 0% of each run, Pallas kernels for 13% -> 13%
where the time goes in v9:
time: 21.6 us; the launch traced here: 21.4 us
  starting transfers between devices  9.92 us (46%)
  waiting for transfers between devices  5.48 us (25%)
  Pallas kernels  4.95 us (23%)
  between operations  0.81 us (4%)
  other arithmetic  0.24 us (1%)
    ppermute x6, starting transfers between devices, carry_states(): lax.ppermute(message, DEVICES, [(i, target(i, size, low, move)) for i in...  9.19 us
    ppermute x6, waiting for transfers between devices, carry_states(): lax.ppermute(message, DEVICES, [(i, target(i, size, low, move)) for i in...  4.66 us
    pallas_call x2, Pallas kernels, finish(): pl.pallas_call(functools.partial(finish_kernel, mine), out_shape=tuple((j...  1.77 us
    pallas_call x1, Pallas kernels, carry_states(): *local, total = local_terms(keep, got)  1.57 us
    pallas_call x1, Pallas kernels, body(): pl.pallas_call(send_kernel, out_shape=jax.ShapeDtypeStruct(shape, BF16),...  1.35 us
    ppermute x1, waiting for transfers between devices, carry_states(): got = lax.ppermute(send, DEVICES, swap)  0.62 us
    ppermute x1, starting transfers between devices, carry_states(): got = lax.ppermute(send, DEVICES, swap)  0.52 us
  transfers between devices with their start and end apart: 8, of which 7 were waited for; matrix products, arithmetic and copies ran while one was open for 0% of the time, Pallas kernels for 13%

profile of v9, /device:TPU:0, one launch (start us, length us, event | category | flops | bytes accessed | tf_op | source)
XLA Modules:
  0.0 21.4 jit_solution(8059527398394989892)
XLA Ops:
  0.6 0.0 copy-start.2
  0.6 0.0 copy-start.3
  0.7 0.0 copy-start
  0.7 0.0 copy-start.1
  0.7 1.3 %shard_map.68 = bf16[2,1,128,128]{3,2,1,0:T(8,128)(2,1)S(1)} custom-call(bf16[128,256]{1,0:T(8,128)(2,1)} %k_ref.7, bf16[128,256]{1,0:T(8,128)(2,1)} %v_ref.7, bf16[128,1024]{1,0:T(8,128)(2,1)} %o_ref.3, bf16[128,1024]{1,0:T(8,128)(2,1)} %q_ref.3), custom_call_target="tpu_custom_call" | custom-call | tf_op jit(solution)/shard_map/pallas_call | solution.py:239
  2.0 0.5 %collective-permute-start = (bf16[2,1,128,128]{3,2,1,0:T(8,128)(2,1)S(1)}, bf16[2,1,128,128]{3,2,1,0:T(8,128)(2,1)S(1)}, u32[]{:S(2)}, u32[]{:S(2)}) collective-permute-start(bf16[2,1,128,128]{3,2,1,0:T(8,128)(2,1)S(1)} %shard_map.68), channel_id=1, source_target_pairs={{0,1},{1,0},{2,3},{3,2},{4,5},{5,4},{6,7},{7,6},{8,9},{9,8},{10,11... | collective-permute-start | bytes 196616 | tf_op jit(solution)/shard_map/ppermute | solution.py:193
  2.5 0.0 copy-done.2
  2.5 0.0 copy-done.3
  2.6 0.0 copy-done
  2.6 0.0 copy-done.1
  2.6 0.3 %shard_map.67.keep_ref = bf16[2,1,128,128]{3,2,1,0:T(8,128)(2,1)S(1)} custom-call(bf16[128,256]{1,0:T(8,128)(2,1)S(1)} %copy-done.2, bf16[128,256]{1,0:T(8,128)(2,1)S(1)} %copy-done.3, bf16[128,1024]{1,0:T(8,128)(2,1)S(1)} %copy-done.1, bf16[128,1024]{1,0:T(8,128)(2,1)S(1)} %copy-done), custom_call_target="tpu_custom_call" | custom-call | flops 33554432 | bytes 524288 | tf_op jit(solution)/shard_map/pallas_call | solution.py:249
  2.8 0.6 %collective-permute-done.got_ref = bf16[2,1,128,128]{3,2,1,0:T(8,128)(2,1)S(1)} collective-permute-done((bf16[2,1,128,128]{3,2,1,0:T(8,128)(2,1)S(1)}, bf16[2,1,128,128]{3,2,1,0:T(8,128)(2,1)S(1)}, u32[]{:S(2)}, u32[]{:S(2)}) %collective-permute-start) | collective-permute-done | bytes 65568 | tf_op jit(solution)/shard_map/ppermute | solution.py:193
  3.5 2.7 %collective-permute-start.3 = (bf16[2,1,128,128]{3,2,1,0:T(8,128)(2,1)S(1)}, bf16[2,1,128,128]{3,2,1,0:T(8,128)(2,1)S(1)}, u32[]{:S(2)}, u32[]{:S(2)}) collective-permute-start(bf16[2,1,128,128]{3,2,1,0:T(8,128)(2,1)S(1)} %add_convert_fusion.1), channel_id=1, source_target_pairs={{0,5},{1,4},{2,7},{3,6},{4,1},{5,0},{6,3},{7,2},{8,13},{9,12},{10,... | collective-permute-start | bytes 196616 | tf_op jit(solution)/shard_map/ppermute | solution.py:205
  6.2 1.4 %collective-permute-start.2 = (bf16[2,1,128,128]{3,2,1,0:T(8,128)(2,1)S(1)}, bf16[2,1,128,128]{3,2,1,0:T(8,128)(2,1)S(1)}, u32[]{:S(2)}, u32[]{:S(2)}) collective-permute-start(bf16[2,1,128,128]{3,2,1,0:T(8,128)(2,1)S(1)} %add_convert_fusion.1), channel_id=1, source_target_pairs={{0,6},{1,7},{2,4},{3,5},{4,2},{5,3},{6,0},{7,1},{8,14},{9,15},{10,... | collective-permute-start | bytes 196616 | tf_op jit(solution)/shard_map/ppermute | solution.py:205
  7.6 0.0 collective-permute-start.1
  7.6 1.6 %shard_map.69 = (f32[128,1024]{1,0:T(8,128)S(1)}, f32[128,256]{1,0:T(8,128)S(1)}, f32[128,256]{1,0:T(8,128)S(1)}, bf16[128,1024]{1,0:T(8,128)(2,1)S(1)}, f32[2,1,128,128]{3,2,1,0:T(8,128)S(1)}) custom-call(bf16[128,1024]{1,0:T(8,128)(2,1)S(1)} %copy-done, bf16[128,256]{1,0:T(8,128)(2,1)S(1)} %copy-done.2, bf16[128,256]{1,0:T(8,128)(2,1)S(1)} %copy-done.3, ...), custom_call_target="tpu_custom_call" | custom-call | flops 201326592 | bytes 1572864 | tf_op jit(solution)/shard_map/pallas_call | solution.py:195
  9.2 0.6 %collective-permute-done.3 = bf16[2,1,128,128]{3,2,1,0:T(8,128)(2,1)S(1)} collective-permute-done((bf16[2,1,128,128]{3,2,1,0:T(8,128)(2,1)S(1)}, bf16[2,1,128,128]{3,2,1,0:T(8,128)(2,1)S(1)}, u32[]{:S(2)}, u32[]{:S(2)}) %collective-permute-start.3) | collective-permute-done | bytes 65568 | tf_op jit(solution)/shard_map/ppermute | solution.py:205
  9.8 1.7 %collective-permute-done.2 = bf16[2,1,128,128]{3,2,1,0:T(8,128)(2,1)S(1)} collective-permute-done((bf16[2,1,128,128]{3,2,1,0:T(8,128)(2,1)S(1)}, bf16[2,1,128,128]{3,2,1,0:T(8,128)(2,1)S(1)}, u32[]{:S(2)}, u32[]{:S(2)}) %collective-permute-start.2) | collective-permute-done | bytes 65568 | tf_op jit(solution)/shard_map/ppermute | solution.py:205
  11.4 0.3 %collective-permute-done.1 = bf16[2,1,128,128]{3,2,1,0:T(8,128)(2,1)S(1)} collective-permute-done((bf16[2,1,128,128]{3,2,1,0:T(8,128)(2,1)S(1)}, bf16[2,1,128,128]{3,2,1,0:T(8,128)(2,1)S(1)}, u32[]{:S(2)}, u32[]{:S(2)}) %collective-permute-start.1) | collective-permute-done | bytes 65568 | tf_op jit(solution)/shard_map/ppermute | solution.py:205
  11.8 1.3 %collective-permute-start.6 = (bf16[1,128,128]{2,1,0:T(8,128)(2,1)S(1)}, bf16[1,128,128]{2,1,0:T(8,128)(2,1)S(1)}, u32[]{:S(2)}, u32[]{:S(2)}) collective-permute-start(bf16[1,128,128]{2,1,0:T(8,128)(2,1)S(1)} %get-tuple-element.21), channel_id=1, source_target_pairs={{0,9},{1,8},{2,11},{3,10},{4,13},{5,12},{6,15},{7,14},{8,17},{9,16... | collective-permute-start | bytes 98312 | tf_op jit(solution)/shard_map/ppermute | solution.py:218
  13.1 2.6 %collective-permute-start.5 = (bf16[1,128,128]{2,1,0:T(8,128)(2,1)S(1)}, bf16[1,128,128]{2,1,0:T(8,128)(2,1)S(1)}, u32[]{:S(2)}, u32[]{:S(2)}) collective-permute-start(bf16[1,128,128]{2,1,0:T(8,128)(2,1)S(1)} %get-tuple-element.20), channel_id=1, source_target_pairs={{0,16},{1,17},{2,18},{3,19},{4,20},{5,21},{6,22},{7,23},{8,24},{9,... | collective-permute-start | bytes 98312 | tf_op jit(solution)/shard_map/ppermute | solution.py:218
  15.7 1.1 %collective-permute-start.4 = (bf16[1,128,128]{2,1,0:T(8,128)(2,1)S(1)}, bf16[1,128,128]{2,1,0:T(8,128)(2,1)S(1)}, u32[]{:S(2)}, u32[]{:S(2)}) collective-permute-start(bf16[1,128,128]{2,1,0:T(8,128)(2,1)S(1)} %get-tuple-element.19), channel_id=1, source_target_pairs={{0,25},{1,24},{2,27},{3,26},{4,29},{5,28},{6,31},{7,30},{8,1},{9,0... | collective-permute-start | bytes 98312 | tf_op jit(solution)/shard_map/ppermute | solution.py:218
  17.0 0.0 collective-permute-done.6
  17.0 1.1 %collective-permute-done.5 = bf16[1,128,128]{2,1,0:T(8,128)(2,1)S(1)} collective-permute-done((bf16[1,128,128]{2,1,0:T(8,128)(2,1)S(1)}, bf16[1,128,128]{2,1,0:T(8,128)(2,1)S(1)}, u32[]{:S(2)}, u32[]{:S(2)}) %collective-permute-start.5) | collective-permute-done | bytes 32800 | tf_op jit(solution)/shard_map/ppermute | solution.py:218
  18.0 1.0 %collective-permute-done.4 = bf16[1,128,128]{2,1,0:T(8,128)(2,1)S(1)} collective-permute-done((bf16[1,128,128]{2,1,0:T(8,128)(2,1)S(1)}, bf16[1,128,128]{2,1,0:T(8,128)(2,1)S(1)}, u32[]{:S(2)}, u32[]{:S(2)}) %collective-permute-start.4) | collective-permute-done | bytes 32800 | tf_op jit(solution)/shard_map/ppermute | solution.py:218
  19.1 0.1 fusion.26
  19.2 0.2 %collective-permute-start.7 = (bf16[2,1,128,128]{3,2,1,0:T(8,128)(2,1)S(1)}, bf16[2,1,128,128]{3,2,1,0:T(8,128)(2,1)S(1)}, u32[]{:S(2)}, u32[]{:S(2)}) collective-permute-start(bf16[2,1,128,128]{3,2,1,0:T(8,128)(2,1)S(1)} %pad_maximum_fusion), channel_id=1, source_target_pairs={{0,1},{1,0},{2,3},{3,2},{4,5},{5,4},{6,7},{7,6},{8,9},{9,8},{10,11... | collective-permute-start | bytes 196616 | tf_op jit(solution)/shard_map/ppermute | solution.py:227
  19.4 0.9 %shard_map.70 = (bf16[128,1024]{1,0:T(8,128)(2,1)}, bf16[128,256]{1,0:T(8,128)(2,1)}, bf16[128,256]{1,0:T(8,128)(2,1)}) custom-call(bf16[128,256]{1,0:T(8,128)(2,1)S(1)} %copy-done.2, bf16[128,256]{1,0:T(8,128)(2,1)S(1)} %copy-done.3, bf16[128,1024]{1,0:T(8,128)(2,1)S(1)} %get-tuple-element.14.scaled_ref, f32[128,1024]{1,0:T(8,128)S(1)} %get-tuple-element.15.ql_ref, ...), custom_call_target="tpu_custom_call" | custom-call | flops 67108864 | bytes 524288 | tf_op jit(solution)/shard_map/pallas_call | solution.py:274
  20.3 0.2 collective-permute-done.7.state_ref
  20.5 0.9 %shard_map.71 = (bf16[128,1024]{1,0:T(8,128)(2,1)}, bf16[128,256]{1,0:T(8,128)(2,1)}, bf16[128,256]{1,0:T(8,128)(2,1)}) custom-call(bf16[128,256]{1,0:T(8,128)(2,1)S(1)} %copy-done.2, bf16[128,256]{1,0:T(8,128)(2,1)S(1)} %copy-done.3, bf16[128,1024]{1,0:T(8,128)(2,1)S(1)} %get-tuple-element.14.scaled_ref, ...), custom_call_target="tpu_custom_call", output_to_operand_aliasing={{0}: (7, {}), {1}: (8, {}), {2}: (9, {})} | custom-call | flops 67108864 | bytes 524288 | tf_op jit(solution)/shard_map/pallas_call | solution.py:274
  (11 shorter events, 0.2 us)
Async XLA Ops:
  0.6 1.9 %copy-start.2 = (bf16[128,256]{1,0:T(8,128)(2,1)S(1)}, bf16[128,256]{1,0:T(8,128)(2,1)}, u32[]{:S(2)}) copy-start(bf16[128,256]{1,0:T(8,128)(2,1)} %k_ref.7) | copy-start | bytes 196612
  0.6 1.9 %copy-start.3 = (bf16[128,256]{1,0:T(8,128)(2,1)S(1)}, bf16[128,256]{1,0:T(8,128)(2,1)}, u32[]{:S(2)}) copy-start(bf16[128,256]{1,0:T(8,128)(2,1)} %v_ref.7) | copy-start | bytes 196612
  0.7 1.9 %copy-start = (bf16[128,1024]{1,0:T(8,128)(2,1)S(1)}, bf16[128,1024]{1,0:T(8,128)(2,1)}, u32[]{:S(2)}) copy-start(bf16[128,1024]{1,0:T(8,128)(2,1)} %q_ref.3) | copy-start | bytes 786436
  0.7 1.9 %copy-start.1 = (bf16[128,1024]{1,0:T(8,128)(2,1)S(1)}, bf16[128,1024]{1,0:T(8,128)(2,1)}, u32[]{:S(2)}) copy-start(bf16[128,1024]{1,0:T(8,128)(2,1)} %o_ref.3) | copy-start | bytes 786436
  2.0 1.4 %collective-permute-start = (bf16[2,1,128,128]{3,2,1,0:T(8,128)(2,1)S(1)}, bf16[2,1,128,128]{3,2,1,0:T(8,128)(2,1)S(1)}, u32[]{:S(2)}, u32[]{:S(2)}) collective-permute-start(bf16[2,1,128,128]{3,2,1,0:T(8,128)(2,1)S(1)} %shard_map.68), channel_id=1, source_target_pairs={{0,1},{1,0},{2,3},{3,2},{4,5},{5,4},{6,7},{7,6},{8,9},{9,8},{10,11... | collective-permute-start | bytes 196616 | tf_op jit(solution)/shard_map/ppermute | solution.py:193
  3.5 6.3 %collective-permute-start.3 = (bf16[2,1,128,128]{3,2,1,0:T(8,128)(2,1)S(1)}, bf16[2,1,128,128]{3,2,1,0:T(8,128)(2,1)S(1)}, u32[]{:S(2)}, u32[]{:S(2)}) collective-permute-start(bf16[2,1,128,128]{3,2,1,0:T(8,128)(2,1)S(1)} %add_convert_fusion.1), channel_id=1, source_target_pairs={{0,5},{1,4},{2,7},{3,6},{4,1},{5,0},{6,3},{7,2},{8,13},{9,12},{10,... | collective-permute-start | bytes 196616 | tf_op jit(solution)/shard_map/ppermute | solution.py:205
  6.2 5.2 %collective-permute-start.2 = (bf16[2,1,128,128]{3,2,1,0:T(8,128)(2,1)S(1)}, bf16[2,1,128,128]{3,2,1,0:T(8,128)(2,1)S(1)}, u32[]{:S(2)}, u32[]{:S(2)}) collective-permute-start(bf16[2,1,128,128]{3,2,1,0:T(8,128)(2,1)S(1)} %add_convert_fusion.1), channel_id=1, source_target_pairs={{0,6},{1,7},{2,4},{3,5},{4,2},{5,3},{6,0},{7,1},{8,14},{9,15},{10,... | collective-permute-start | bytes 196616 | tf_op jit(solution)/shard_map/ppermute | solution.py:205
  7.6 4.1 %collective-permute-start.1 = (bf16[2,1,128,128]{3,2,1,0:T(8,128)(2,1)S(1)}, bf16[2,1,128,128]{3,2,1,0:T(8,128)(2,1)S(1)}, u32[]{:S(2)}, u32[]{:S(2)}) collective-permute-start(bf16[2,1,128,128]{3,2,1,0:T(8,128)(2,1)S(1)} %add_convert_fusion.1), channel_id=1, source_target_pairs={{0,3},{1,2},{2,1},{3,0},{4,7},{5,6},{6,5},{7,4},{8,11},{9,10},{10,... | collective-permute-start | bytes 196616 | tf_op jit(solution)/shard_map/ppermute | solution.py:205
  11.8 5.2 %collective-permute-start.6 = (bf16[1,128,128]{2,1,0:T(8,128)(2,1)S(1)}, bf16[1,128,128]{2,1,0:T(8,128)(2,1)S(1)}, u32[]{:S(2)}, u32[]{:S(2)}) collective-permute-start(bf16[1,128,128]{2,1,0:T(8,128)(2,1)S(1)} %get-tuple-element.21), channel_id=1, source_target_pairs={{0,9},{1,8},{2,11},{3,10},{4,13},{5,12},{6,15},{7,14},{8,17},{9,16... | collective-permute-start | bytes 98312 | tf_op jit(solution)/shard_map/ppermute | solution.py:218
  13.1 4.9 %collective-permute-start.5 = (bf16[1,128,128]{2,1,0:T(8,128)(2,1)S(1)}, bf16[1,128,128]{2,1,0:T(8,128)(2,1)S(1)}, u32[]{:S(2)}, u32[]{:S(2)}) collective-permute-start(bf16[1,128,128]{2,1,0:T(8,128)(2,1)S(1)} %get-tuple-element.20), channel_id=1, source_target_pairs={{0,16},{1,17},{2,18},{3,19},{4,20},{5,21},{6,22},{7,23},{8,24},{9,... | collective-permute-start | bytes 98312 | tf_op jit(solution)/shard_map/ppermute | solution.py:218
  15.7 3.4 %collective-permute-start.4 = (bf16[1,128,128]{2,1,0:T(8,128)(2,1)S(1)}, bf16[1,128,128]{2,1,0:T(8,128)(2,1)S(1)}, u32[]{:S(2)}, u32[]{:S(2)}) collective-permute-start(bf16[1,128,128]{2,1,0:T(8,128)(2,1)S(1)} %get-tuple-element.19), channel_id=1, source_target_pairs={{0,25},{1,24},{2,27},{3,26},{4,29},{5,28},{6,31},{7,30},{8,1},{9,0... | collective-permute-start | bytes 98312 | tf_op jit(solution)/shard_map/ppermute | solution.py:218
  19.2 1.3 %collective-permute-start.7 = (bf16[2,1,128,128]{3,2,1,0:T(8,128)(2,1)S(1)}, bf16[2,1,128,128]{3,2,1,0:T(8,128)(2,1)S(1)}, u32[]{:S(2)}, u32[]{:S(2)}) collective-permute-start(bf16[2,1,128,128]{3,2,1,0:T(8,128)(2,1)S(1)} %pad_maximum_fusion), channel_id=1, source_target_pairs={{0,1},{1,0},{2,3},{3,2},{4,5},{5,4},{6,7},{7,6},{8,9},{9,8},{10,11... | collective-permute-start | bytes 196616 | tf_op jit(solution)/shard_map/ppermute | solution.py:227
